TPU v7x, 32 devices: a whole 2x2x4 slice. The times are simulated.
32 devices in a mesh: groups: 2 (over y), tensor: 4 (over z), store: 4 (over x, core).
Axes of the slice: x: 2, y: 2, z: 4, core: 2. Of those that a mesh axis runs over, the one named last changes fastest.
Arguments:
- hidden_activations: bfloat16 [2048, 28672], P('groups', 'tensor'), parts along dimension 0, may hold values from -6 to 6
- down_matrix: bfloat16 [28672, 8192], P('tensor', 'store'), may hold values from -0.03125 to 0.03125
- adapter_input_factor: bfloat16 [32, 28672, 128], P(('groups', 'store'), 'tensor'), parts along dimension 0, may hold values from -0.03125 to 0.03125
- adapter_output_factor: bfloat16 [32, 128, 8192], P(('groups', 'store'), 'tensor'), parts along dimension 0, may hold values from -0.5 to 0.5
- token_requests: int32 [2048], P('groups'), parts along dimension 0, may hold values from 0 to 3, never falling along the last dimension, each value on 1 to 512 neighbouring positions
- request_adapters: int32 [8], P('groups'), parts along dimension 0, may hold values from 0 to 15
- adapter_ranks: int32 [32], P('groups'), parts along dimension 0, may hold values from 16 to 128, as said below
- adapter_store_slot: int32 [32], P('groups'), parts along dimension 0, may hold values from 0 to 15, each once
Outputs:
- mixed: bfloat16 [2048, 8192], P(('groups', 'tensor'), 'store'), parts along dimension 0
There are 2 independent parts, one for each index of `groups`. A program takes and returns all parts, laid end to end along the dimension named above; an argument that names none is the same for every part. Nothing has to cross between parts.
Inputs may be any that keep to these rules, and one draw needn't show every extreme that they name: `adapter_ranks`: each rank is 128, 64, 32 or 16; some adapter has rank 128.
All inputs are finite; a program needn't handle non-finite values.
Results may differ from a plain program's by a relative error of at most 0.013.
Values may be sent and summed in bfloat16 or wider, within the bound.
No kernel may reach another device: no remote copies, remote signals or barrier semaphores. Data moves between devices by JAX's collectives and lax.ppermute only.
A program may use at most 192 MiB of HBM per device.

v0:
```python
import functools

import jax
import jax.numpy as jnp
from jax import lax
from jax.experimental import pallas as pl
from jax.experimental.pallas import tpu as pltpu
from jax.sharding import PartitionSpec as P

LINE = 4
LANES = 128
AHEAD = 3
PAIRS = 2
MIB = 1024 * 1024


def line_order(n):
    order = []
    for z in range(n):
        sends = [(t, z >= n // 2, n - 1 - t + z) for t in range(z, n - 1)]
        sends += [(t, z < n // 2, t - (n - 1 - z)) for t in range(n - 1 - z, n - 1)]
        order.append([block for _, _, block in sorted(sends)] + [z])
    return order


def first_divisor(size, choices):
    for choice in choices:
        if size % choice == 0:
            return choice
    return size


def after(token, *done):
    return lax.optimization_barrier((token, done))[0]


def params(mebibytes):
    return pltpu.CompilerParams(vmem_limit_bytes=mebibytes * MIB)


def small_cost():
    return pl.CostEstimate(flops=10**6, bytes_accessed=10**5, transcendentals=0)


def block_at(order, slot, place):
    picked = jnp.int32(order[0][slot])
    for z in range(1, len(order)):
        picked = jnp.where(place == z, order[z][slot], picked)
    return picked


def spans(requests_ref, count):
    requests = requests_ref[...]
    return [jnp.int32(0)] + [jnp.sum((requests <= r).astype(jnp.int32)) for r in range(count)]


class Meta:
    def __init__(self, ref, requests):
        self.ref, self.requests = ref, requests
        self.adapters = (ref.shape[0] - 2 - requests) // 2
        self.place, self.shard = ref[0], ref[1]

    def adapter(self, r):
        return self.ref[2 + r]

    def rank(self, r):
        return self.ref[2 + self.requests + self.adapter(r)]

    def local_slot(self, r, held):
        return self.ref[2 + self.requests + self.adapters + self.adapter(r)] - self.shard * held


def base_kernel(order, groups, half, held, request_count, piece, handed_on, *refs):
    slots = [slot for group in groups for slot in group]
    places = [(g, i) for g, group in enumerate(groups) for i in range(len(group))]
    count = len(slots)
    meta, refs = Meta(refs[0], request_count), refs[1:]
    if held:
        requests_ref, factor, refs = refs[0], refs[1], refs[2:]
    hidden, matrix, refs = refs[0], refs[1], refs[2:]
    under, refs = (refs[0], refs[1:]) if handed_on else (None, refs)
    outs, refs = refs[: len(groups)], refs[len(groups) :]
    (rows, right, sums, sems), refs = refs[:4], refs[4:]
    steps, _, tile = rows.shape
    columns = outs[0].shape[1]
    block = rows.shape[1] // count
    first_rows = [pl.multiple_of(block_at(order, slot, meta.place) * block, block) for slot in slots]

    def depth_of(k):
        return pl.ds(pl.multiple_of(k * tile, tile), tile)

    def copies(k):
        moves = [
            (hidden.at[pl.ds(first_rows[i], block), depth_of(k)], rows.at[k, pl.ds(i * block, block), :])
            for i in range(count)
        ]
        moves.append((matrix.at[depth_of(k), pl.ds(half * columns, columns)], right.at[k]))
        return [pltpu.make_async_copy(a, b, sems.at[k, i]) for i, (a, b) in enumerate(moves)]

    if held:
        factors, inputs, factor_sems = refs
        width = factor.shape[2]

        def factor_copies(k, pair):
            return [
                pltpu.make_async_copy(
                    factor.at[2 * pair + i, depth_of(k), :],
                    factors.at[pair, k, :, pl.ds(i * width, width)],
                    factor_sems.at[k, 2 * pair + i],
                )
                for i in range(2)
            ]

    def start(k):
        for copy in copies(k):
            copy.start()

    def start_factors(k, pairs):
        for pair, used in enumerate(pairs):

            @pl.when(used)
            def _(pair=pair):
                for copy in factor_copies(k, pair):
                    copy.start()

    for k in range(min(AHEAD, steps)):
        start(k)
    used, blocks_using = [], []
    if held:
        bounds = spans(requests_ref, request_count)
        local = [meta.local_slot(r, held) for r in range(request_count)]
        for pair in range(held // 2):
            used_by = []
            for first in first_rows:
                wanted = jnp.bool_(False)
                for r, slot in enumerate(local):
                    here = jnp.maximum(bounds[r], first) < jnp.minimum(bounds[r + 1], first + block)
                    wanted = wanted | (here & (slot // 2 == pair) & (slot >= 0))
                used_by.append(wanted)
            blocks_using.append(used_by)
            used.append(functools.reduce(jnp.logical_or, used_by))
        for k in range(min(AHEAD, steps)):
            start_factors(k, used)
        inputs[...] = jnp.zeros_like(inputs)
    sums[...] = jnp.zeros_like(sums)

    def step(k, _):
        @pl.when(k + AHEAD < steps)
        def _():
            start(k + AHEAD)
            start_factors(k + AHEAD, used)

        for copy in copies(k):
            copy.wait()
        sums[...] += jnp.dot(rows[k], right[k], preferred_element_type=jnp.float32)
        for pair, wanted in enumerate(used):

            @pl.when(wanted)
            def _(pair=pair):
                for copy in factor_copies(k, pair):
                    copy.wait()

            for i, wanted_here in enumerate(blocks_using[pair]):

                @pl.when(wanted_here)
                def _(pair=pair, own=pl.ds(i * block, block)):
                    inputs[pair, own, :] += jnp.dot(
                        rows[k, own, :], factors[pair, k], preferred_element_type=jnp.float32
                    )

        return 0

    lax.fori_loop(0, steps, step, 0)
    if handed_on:
        outs[0][len(groups[0]) * piece :, :] = under[...]
    for i, (group, position) in enumerate(places):
        own = pl.ds(i * block, block)
        out, top = outs[group], position * piece
        out[top : top + block, :] = sums[own, :].astype(jnp.bfloat16)
        if held:
            row = lax.broadcasted_iota(jnp.int32, (block, width), 0) + first_rows[i]
            column = lax.broadcasted_iota(jnp.int32, (block, width), 1)
            total = jnp.zeros((block, width), jnp.float32)
            for r, slot in enumerate(local):
                last = jnp.where((slot >= 0) & (slot < held), bounds[r + 1], 0)
                keep = (row >= bounds[r]) & (row < last) & (column < meta.rank(r))
                slot = jnp.clip(slot, 0, held - 1)
                lanes = pl.ds(pl.multiple_of(slot % 2 * width, width), width)
                total = jnp.where(keep, inputs[slot // 2, own, lanes], total)
            total = total.astype(jnp.bfloat16)
            size = block * width // columns
            for j in range(columns // width):
                lanes = slice(j * width, (j + 1) * width)
                out[top + block : top + block + size, lanes] = total[j * size : (j + 1) * size, :]


def base_terms(meta, requests, request_count, hidden, matrix, factor, groups, half, n, grant, under=None):
    tokens, depth = hidden.shape
    block, columns = tokens // n, matrix.shape[1] // 2
    tile = first_divisor(depth, (1024, 512, 256, 128))
    steps = depth // tile
    count = sum(len(group) for group in groups)
    smem = pl.BlockSpec(memory_space=pltpu.SMEM)
    vmem = pl.BlockSpec(memory_space=pltpu.VMEM)
    hbm = pl.BlockSpec(memory_space=pltpu.HBM)
    held, out_rows = 0, block
    operands, in_specs = [meta], [smem]
    scratch = [
        pltpu.VMEM((steps, count * block, tile), jnp.bfloat16),
        pltpu.VMEM((steps, tile, columns), jnp.bfloat16),
        pltpu.VMEM((count * block, columns), jnp.float32),
        pltpu.SemaphoreType.DMA((steps, count + 1)),
    ]
    if factor is not None:
        held, _, width = factor.shape
        out_rows += block * width // columns
        operands, in_specs = [meta, requests, factor], [smem, vmem, hbm]
        scratch += [
            pltpu.VMEM((held // 2, steps, tile, 2 * width), jnp.bfloat16),
            pltpu.VMEM((held // 2, count * block, 2 * width), jnp.float32),
            pltpu.SemaphoreType.DMA((steps, held)),
        ]
    heights = [len(group) * out_rows for group in groups]
    operands, in_specs = operands + [hidden, matrix], in_specs + [hbm, hbm]
    if under is not None:
        heights[0] += under.shape[0]
        operands, in_specs = operands + [under], in_specs + [vmem]
    handed_on = under is not None
    return pl.pallas_call(
        lambda *refs: base_kernel(line_order(n), groups, half, held, request_count, out_rows, handed_on, *refs),
        out_shape=[jax.ShapeDtypeStruct((height, columns), jnp.bfloat16) for height in heights],
        in_specs=in_specs,
        out_specs=[vmem] * len(groups),
        scratch_shapes=scratch,
        compiler_params=params(grant),
        cost_estimate=small_cost(),
        name="base_terms",
    )(*operands)


def select_rows_kernel(request_count, meta_ref, factor, kept, sent):
    meta = Meta(meta_ref, request_count)
    held, rank_rows, _ = factor.shape
    width = factor.shape[2] // (2 * PAIRS)
    side = meta.shard % 2
    for r in range(request_count):
        slot = meta.local_slot(r, held)
        owned = (slot >= 0) & (slot < held)
        slot = jnp.clip(slot, 0, held - 1)
        for out, core in ((kept, side), (sent, 1 - side)):
            for i in range(PAIRS):
                for c in range(2):
                    first = (2 * i + core) * width + c * (width // 2)
                    rows = factor[slot, :, pl.ds(pl.multiple_of(first, LANES), width // 2)]
                    top = (c * request_count + r) * rank_rows
                    out[i, top : top + rank_rows, :] = jnp.where(owned, rows, jnp.zeros_like(rows))


def select_rows(meta, request_count, factor):
    _, rank_rows, model_width = factor.shape
    smem = pl.BlockSpec(memory_space=pltpu.SMEM)
    vmem = pl.BlockSpec(memory_space=pltpu.VMEM)
    shape = (PAIRS, 2 * request_count * rank_rows, model_width // (4 * PAIRS))
    out = jax.ShapeDtypeStruct(shape, factor.dtype)
    return pl.pallas_call(
        lambda *refs: select_rows_kernel(request_count, *refs),
        out_shape=[out, out],
        in_specs=[smem, vmem],
        out_specs=[vmem, vmem],
        compiler_params=params(16),
        cost_estimate=small_cost(),
        name="select_rows",
    )(meta, factor)


def expanded_inputs(meta, requests_ref, lora_ref):
    block, width = lora_ref.shape
    row = lax.broadcasted_iota(jnp.int32, (block, width), 0) + meta.place * block
    lora = lora_ref[...].astype(jnp.float32)
    bounds = spans(requests_ref, meta.requests)
    parts = []
    for r in range(meta.requests):
        scale = 0.25 * width / meta.rank(r).astype(jnp.float32)
        keep = (row >= bounds[r]) & (row < bounds[r + 1])
        parts.append(jnp.where(keep, lora * scale, 0.0).astype(jnp.bfloat16))
    return jnp.concatenate(parts, axis=1)


def finish_kernel(items, added, requests, rank_rows, n, *refs):
    meta_ref, requests_ref, lora_ref, refs = refs[0], refs[1], refs[2], refs[3:]
    arrays, out, rows = refs[:-2], refs[-2], refs[-1]
    meta = Meta(meta_ref, requests)
    rank = n * rank_rows
    half = out.shape[1] // 2
    for index, top, targets in items:
        for place, k in targets:

            @pl.when(meta.place == place)
            def _(piece=arrays[index], top=top, k=k):
                for r in range(requests):
                    first = r * rank + k * rank_rows
                    for c in range(2):
                        start = top + (c * requests + r) * rank_rows
                        rows[first : first + rank_rows, c * half : (c + 1) * half] = piece[start : start + rank_rows, :]

    expanded = expanded_inputs(meta, requests_ref, lora_ref)
    block = lora_ref.shape[0]
    for c in range(2):
        columns = slice(c * half, (c + 1) * half)
        total = jnp.dot(expanded, rows[:, columns], preferred_element_type=jnp.float32)
        for index, top, which in added:
            if which == c:
                total += arrays[index][top : top + block, :].astype(jnp.float32)
        out[:, columns] = total.astype(out.dtype)


def finish(meta, requests, lora, arrays, items, added, request_count, rank_rows, n):
    smem = pl.BlockSpec(memory_space=pltpu.SMEM)
    vmem = pl.BlockSpec(memory_space=pltpu.VMEM)
    width = 2 * arrays[0].shape[1]
    return pl.pallas_call(
        lambda *refs: finish_kernel(items, added, request_count, rank_rows, n, *refs),
        out_shape=jax.ShapeDtypeStruct((lora.shape[0], width), jnp.bfloat16),
        in_specs=[smem] + [vmem] * (2 + len(arrays)),
        out_specs=vmem,
        scratch_shapes=[pltpu.VMEM((request_count * n * rank_rows, width), jnp.bfloat16)],
        compiler_params=params(20),
        cost_estimate=small_cost(),
        name="finish",
    )(meta, requests, lora, *arrays)


def join_kernel(count, term_top, came_top, under_top, term, came, *refs):
    out = refs[-1]
    total = term[term_top : term_top + count, :].astype(jnp.float32)
    total += came[came_top : came_top + count, :].astype(jnp.float32)
    out[:count, :] = total.astype(out.dtype)
    if len(refs) > 1:
        under = refs[0]
        out[count:, :] = under[under_top : under_top + out.shape[0] - count, :]


def join(token, count, term, term_top, came, came_top, under=None, under_top=0, under_count=0):
    arrays = [term, came] + ([] if under is None else [under])
    arrays = lax.optimization_barrier((arrays, token))[0]
    vmem = pl.BlockSpec(memory_space=pltpu.VMEM)
    return pl.pallas_call(
        lambda *refs: join_kernel(count, term_top, came_top, under_top, *refs),
        out_shape=jax.ShapeDtypeStruct((count + under_count, term.shape[1]), term.dtype),
        in_specs=[vmem] * len(arrays),
        out_specs=vmem,
        compiler_params=params(12),
        cost_estimate=small_cost(),
        name="join",
    )(*arrays)


def add_last_kernel(total, up, down, out):
    half = up.shape[1]
    out[:, :half] = total[:, :half]
    last = total[:, half:].astype(jnp.float32) + up[...].astype(jnp.float32) + down[...].astype(jnp.float32)
    out[:, half:] = last.astype(out.dtype)


def add_last(total, up, down):
    vmem = pl.BlockSpec(memory_space=pltpu.VMEM)
    return pl.pallas_call(
        add_last_kernel,
        out_shape=jax.ShapeDtypeStruct(total.shape, total.dtype),
        in_specs=[vmem] * 3,
        out_specs=vmem,
        compiler_params=params(12),
        cost_estimate=small_cost(),
        name="add_last",
    )(total, up, down)


def pass_kernel(token_ref, out_ref):
    for i in range(token_ref.shape[0]):
        out_ref[i] = token_ref[i]


def pass_on(token):
    smem = pl.BlockSpec(memory_space=pltpu.SMEM)
    return pl.pallas_call(
        pass_kernel,
        out_shape=jax.ShapeDtypeStruct(token.shape, token.dtype),
        in_specs=[smem],
        out_specs=smem,
        cost_estimate=pl.CostEstimate(flops=4 * 10**9, bytes_accessed=10**3, transcendentals=0),
        name="pass_on",
    )(token)


def swap(x, axis, bit):
    return lax.ppermute(x, axis, [(i, i ^ bit) for i in range(lax.axis_size(axis))])


def bits_of(size):
    return [1 << i for i in range(size.bit_length() - 1)]


def along_edge(x, edge):
    n = lax.axis_size("tensor")
    return lax.ppermute(x, "tensor", [(edge, edge + 1), (n - 1 - edge, n - 2 - edge)])


def on_line(hidden, matrix, input_factor, output_factor, requests, token, request_count, n):
    shard = lax.axis_index("store")
    block = hidden.shape[0] // n
    width = input_factor.shape[2]
    rank_rows = output_factor.shape[1]
    piece = block + block * width // (matrix.shape[1] // 2)
    bundle = 2 * request_count * rank_rows

    def base(token, groups, half, grant, under=None):
        factor = input_factor if half == 0 else None
        return base_terms(token, requests, request_count, hidden, matrix, factor, groups, half, n, grant, under)

    def send(x, edge, token):
        return along_edge(after(x, token), edge)

    kept, sent = select_rows(token, request_count, output_factor)
    token = after(token, kept, sent)
    swapped = swap(sent, "store", 1)
    (s00,) = base(token, [[0]], 0, 58)
    token = after(token, s00, swapped)
    e0_1 = along_edge(s00, 0)
    side = shard // 2 % 2
    kept, swapped, _ = lax.optimization_barrier((kept, swapped, token))
    outgoing = kept[1 - side] + swapped[1 - side]
    rows = kept[side] + swapped[side]
    token = after(token, outgoing, rows)
    swapped = swap(outgoing, "store", 2)
    s01, s11 = base(token, [[0], [1]], 1, 50)

    token = after(token, s01)
    e0_2 = send(s01, 0, token)
    token, e0_1 = lax.optimization_barrier((token, e0_1))
    b10 = join(token, piece, s00, 0, e0_1, 0)
    token = after(token, b10)
    e1_2 = along_edge(b10, 1)
    token, swapped = lax.optimization_barrier((token, swapped))
    rows = rows + swapped
    token = after(token, rows)
    near = lax.ppermute(rows, "tensor", [(0, 1), (n - 1, n - 2), (1, 0), (n - 2, n - 1)])
    far = along_edge(rows, 1)
    s10_s11, s20, s30 = base(token, [[1], [2], [3]], 0, 42, s11)

    token = after(token, s10_s11)
    e0_3 = send(s10_s11, 0, token)
    token, e0_2 = lax.optimization_barrier((token, e0_2))
    token = pass_on(token)
    token, e1_2 = lax.optimization_barrier((token, e1_2))
    token, near = lax.optimization_barrier((token, near))
    b11 = join(token, block, s01, 0, e0_2, 0, near, 0, bundle)
    token = after(token, b11)
    e1_3 = along_edge(b11, 1)
    c20 = join(token, piece, s20, 0, e1_2, 0, far, 0, bundle)
    token = after(token, c20)
    e2_3 = along_edge(c20, 2)
    s21, s31 = base(token, [[2], [3]], 1, 50)

    token = after(token, s21)
    e0_4 = send(s20, 0, token)
    token, e0_3 = lax.optimization_barrier((token, e0_3))
    b20 = join(token, piece, s10_s11, 0, e0_3, 0)
    token = after(token, b20)
    e1_4 = along_edge(b20, 1)
    token = after(token, e1_3, e2_3)
    c21 = join(token, block, s21, 0, e1_3, 0, e1_3, block, bundle)
    token = after(token, c21)
    e2_4 = along_edge(c21, 2)
    e0_5 = send(s21, 0, token)
    b21 = join(token, block, s10_s11, piece, e0_3, piece)
    token = after(token, b21)
    e1_5 = along_edge(b21, 1)

    token, e0_4 = lax.optimization_barrier((token, e0_4))
    e1_4 = lax.optimization_barrier((e1_4, token))[0]
    lora = s30[block:].astype(jnp.float32) + e0_4[block:].astype(jnp.float32)
    lora += e1_4[block:].astype(jnp.float32) + e2_3[block:piece].astype(jnp.float32)
    lora = lora.astype(jnp.bfloat16).reshape(piece - block, -1, width).swapaxes(0, 1).reshape(block, width)
    lora = lora + swap(lora, "store", 1)
    lora = lora + swap(lora, "store", 2)
    arrays = [s30, s31, rows, near, far, e1_3, e2_3, e2_4, e0_4, e1_4]
    items = [
        (2, 0, [(z, z) for z in range(n)]),
        (3, 0, [(0, 1), (1, 0), (2, 3), (3, 2)]),
        (4, 0, [(1, 2), (2, 1)]),
        (5, block, [(1, 3), (2, 0)]),
        (6, piece, [(0, 2), (3, 1)]),
        (7, block, [(0, 3), (3, 0)]),
    ]
    added = [(0, 0, 0), (8, 0, 0), (9, 0, 0), (6, 0, 0), (1, 0, 1), (7, 0, 1)]
    out = finish(token, requests, lora, arrays, items, added, request_count, rank_rows, n)
    return add_last(out, e0_5, e1_5)


def anywhere(hidden, matrix, input_factor, output_factor, token_requests, meta):
    request_adapters, ranks, slots = meta
    held = input_factor.shape[0]
    width = input_factor.shape[2]
    rank, slot = ranks[request_adapters], slots[request_adapters]
    owned = slot // held == lax.axis_index("store")
    chosen = token_requests[:, None] == jnp.arange(request_adapters.shape[0])[None, :]
    lora = jnp.zeros((hidden.shape[0], width), jnp.float32)
    for r in range(request_adapters.shape[0]):
        product = jnp.dot(hidden, input_factor[slot[r] % held], preferred_element_type=jnp.float32)
        keep = (chosen[:, r] & owned[r])[:, None] & (jnp.arange(width) < rank[r])[None, :]
        lora = jnp.where(keep, product, lora)
    lora = lax.psum_scatter(lora.astype(jnp.bfloat16), "tensor", scatter_dimension=1, tiled=True)
    lora = lax.psum(lora, "store").astype(jnp.float32)
    rows = jnp.where(owned[:, None, None], output_factor[slot % held], jnp.zeros((), output_factor.dtype))
    rows = lax.psum_scatter(rows, "store", scatter_dimension=2, tiled=True)
    weights = jnp.where(chosen, 0.25 * width / rank.astype(jnp.float32)[None, :], 0.0)
    expanded = (weights[:, :, None] * lora[:, None, :]).reshape(hidden.shape[0], -1).astype(jnp.bfloat16)
    term = jnp.dot(hidden, matrix, preferred_element_type=jnp.float32)
    term += jnp.dot(expanded, rows.reshape(-1, rows.shape[2]), preferred_element_type=jnp.float32)
    return lax.psum_scatter(term.astype(jnp.bfloat16), "tensor", scatter_dimension=0, tiled=True)


def per_device(
    hidden_activations,
    down_matrix,
    adapter_input_factor,
    adapter_output_factor,
    token_requests,
    request_adapters,
    adapter_ranks,
    adapter_store_slot,
):
    n = lax.axis_size("tensor")
    meta = (request_adapters, adapter_ranks, adapter_store_slot)
    arrays = (hidden_activations, down_matrix, adapter_input_factor, adapter_output_factor)
    if n == LINE and lax.axis_size("store") == 2 * PAIRS and adapter_input_factor.shape[0] % 2 == 0:
        place = jnp.stack([lax.axis_index("tensor"), lax.axis_index("store")]).astype(jnp.int32)
        token = jnp.concatenate([place, *meta])
        return on_line(*arrays, token_requests.reshape(-1, LANES), token, request_adapters.shape[0], n)
    return anywhere(*arrays, token_requests, meta)


def solution(mesh):
    in_specs = (
        P("groups", "tensor"),
        P("tensor", "store"),
        P(("groups", "store"), "tensor", None),
        P(("groups", "store"), "tensor", None),
        P("groups"),
        P("groups"),
        P("groups"),
        P("groups"),
    )
    out_specs = P(("groups", "tensor"), "store")
    return jax.shard_map(
        per_device, mesh=mesh, in_specs=in_specs, out_specs=out_specs, check_vma=False
    )
```

profile of v0, /device:TPU:0, one launch (start us, length us, event | category | flops | bytes accessed | tf_op | source)
XLA Modules:
  0.0 131.0 jit_solution(9444371703731528164)
XLA Ops:
  0.8 1.6 %copy-done.1 = bf16[4,32,8192]{2,1,0:T(8,128)(2,1)S(1)} copy-done((bf16[4,32,8192]{2,1,0:T(8,128)(2,1)S(1)}, bf16[4,32,8192]{2,1,0:T(8,128)(2,1)}, u32[]{:S(2)}) %copy-start.1) | copy-done | bytes 2097176
  2.4 0.8 select_rows.1
  3.7 9.3 %base_terms.4.refs_0_ = bf16[288,1024]{1,0:T(8,128)(2,1)} custom-call(s32[38]{0:T(128)} %copy-done.11, s32[8,128]{1,0:T(8,128)} %bitcast.16, bf16[4,7168,128]{2,1,0:T(8,128)(2,1)} %refs_2_.6, bf16[1024,7168]{1,0:T(8,128)(2,1)} %refs_1_.5, bf16[7168,2048]{1,0:T(8,128)(2,1)} %refs_2_.7), custom_call_target="tpu_custom_call" | custom-call | flops 1000000 | bytes 100000 | tf_op jit(solution)/shard_map/base_terms/pallas_call | solution.py:229
  13.0 4.5 %collective-permute-start.1 = (bf16[288,1024]{1,0:T(8,128)(2,1)}, bf16[288,1024]{1,0:T(8,128)(2,1)S(1)}, u32[]{:S(2)}, u32[]{:S(2)}) collective-permute-start(bf16[288,1024]{1,0:T(8,128)(2,1)} %base_terms.4.refs_0_), channel_id=1, source_target_pairs={{0,4},{12,8},{1,5},{13,9},{2,6},{14,10},{3,7},{15,11},{16,20},{28,... | collective-permute-start | bytes 1769480 | tf_op jit(solution)/shard_map/ppermute | solution.py:405
  17.6 1.3 %add_bitcast_fusion = (bf16[256,1024]{1,0:T(8,128)(2,1)S(1)}, bf16[256,1024]{1,0:T(8,128)(2,1)S(1)}) fusion(bf16[2,256,1024]{2,1,0:T(8,128)(2,1)} %collective-permute-done, s32[]{:T(128)S(6)} %select_n.22, bf16[2,256,1024]{2,1,0:T(8,128)(2,1)S(1)} %get-tuple-element.68, s32[]{:T(128)S(6)} %select_n.21), kind=kLoop, calls=%fused_computation | loop fusion | flops 524288 | bytes 3145736 | tf_op jit(solution)/shard_map/add | solution.py:432
  18.9 1.6 %collective-permute-start.2 = (bf16[256,1024]{1,0:T(8,128)(2,1)S(1)}, bf16[256,1024]{1,0:T(8,128)(2,1)S(1)}, u32[]{:S(2)}, u32[]{:S(2)}) collective-permute-start(bf16[256,1024]{1,0:T(8,128)(2,1)S(1)} %get-tuple-element.124), channel_id=1, source_target_pairs={{0,2},{1,3},{2,0},{3,1},{4,6},{5,7},{6,4},{7,5},{8,10},{9,11},{10,... | collective-permute-start | bytes 1572872 | tf_op jit(solution)/shard_map/ppermute | solution.py:396
  20.5 11.8 %base_terms.5 = (bf16[256,1024]{1,0:T(8,128)(2,1)S(1)}, bf16[256,1024]{1,0:T(8,128)(2,1)S(1)}) custom-call(s32[38]{0:T(128)S(1)} %copy-done.12, bf16[1024,7168]{1,0:T(8,128)(2,1)} %refs_1_.5, bf16[7168,2048]{1,0:T(8,128)(2,1)} %refs_2_.7), custom_call_target="tpu_custom_call" | custom-call | flops 1000000 | bytes 100000 | tf_op jit(solution)/shard_map/base_terms/pallas_call | solution.py:229
  32.4 1.3 %collective-permute-start.3 = (bf16[256,1024]{1,0:T(8,128)(2,1)S(1)}, bf16[256,1024]{1,0:T(8,128)(2,1)S(1)}, u32[]{:S(2)}, u32[]{:S(2)}) collective-permute-start(bf16[256,1024]{1,0:T(8,128)(2,1)S(1)} %get-tuple-element.90.refs_0_), channel_id=1, source_target_pairs={{0,4},{12,8},{1,5},{13,9},{2,6},{14,10},{3,7},{15,11},{16,20},{28,... | collective-permute-start | bytes 1572872 | tf_op jit(solution)/shard_map/ppermute | solution.py:405
  33.7 1.0 join.6
  34.7 1.6 %collective-permute-start.4 = (bf16[288,1024]{1,0:T(8,128)(2,1)}, bf16[288,1024]{1,0:T(8,128)(2,1)}, u32[]{:S(2)}, u32[]{:S(2)}) collective-permute-start(bf16[288,1024]{1,0:T(8,128)(2,1)} %join.6), channel_id=1, source_target_pairs={{4,8},{8,4},{5,9},{9,5},{6,10},{10,6},{7,11},{11,7},{20,24},{24,20... | collective-permute-start | bytes 1769480 | tf_op jit(solution)/shard_map/ppermute | solution.py:405
  36.5 2.7 %collective-permute-start.5 = (bf16[256,1024]{1,0:T(8,128)(2,1)S(1)}, bf16[256,1024]{1,0:T(8,128)(2,1)S(1)}, u32[]{:S(2)}, u32[]{:S(2)}) collective-permute-start(bf16[256,1024]{1,0:T(8,128)(2,1)S(1)} %add.51.refs_5_), channel_id=1, source_target_pairs={{0,4},{12,8},{4,0},{8,12},{1,5},{13,9},{5,1},{9,13},{2,6},{14,10},... | collective-permute-start | bytes 1572872 | tf_op jit(solution)/shard_map/ppermute | solution.py:446
  39.2 1.5 %collective-permute-start.6 = (bf16[256,1024]{1,0:T(8,128)(2,1)S(1)}, bf16[256,1024]{1,0:T(8,128)(2,1)}, u32[]{:S(2)}, u32[]{:S(2)}) collective-permute-start(bf16[256,1024]{1,0:T(8,128)(2,1)S(1)} %add.51.refs_5_), channel_id=1, source_target_pairs={{4,8},{8,4},{5,9},{9,5},{6,10},{10,6},{7,11},{11,7},{20,24},{24,20... | collective-permute-start | bytes 1572872 | tf_op jit(solution)/shard_map/ppermute | solution.py:405
  40.7 18.9 %base_terms.6 = (bf16[544,1024]{1,0:T(8,128)(2,1)S(1)}, bf16[288,1024]{1,0:T(8,128)(2,1)S(1)}, bf16[288,1024]{1,0:T(8,128)(2,1)S(1)}) custom-call(s32[38]{0:T(128)S(1)} %copy-done.12, s32[8,128]{1,0:T(8,128)S(1)} %bitcast.17, bf16[4,7168,128]{2,1,0:T(8,128)(2,1)S(1)} %bitcast.15, bf16[1024,7168]{1,0:T(8,128)(2,1)} %refs_1_.5, bf16[7168,2048]{1,0:T(8,128)(2,1)} %refs_2_.7, ...), custom_call_target="tpu_custom_call" | custom-call | flops 1000000 | bytes 100000 | tf_op jit(solution)/shard_map/base_terms/pallas_call | solution.py:229
  59.6 0.8 copy-done.2
  62.1 4.7 %collective-permute-start.7 = (bf16[544,1024]{1,0:T(8,128)(2,1)S(1)}, bf16[544,1024]{1,0:T(8,128)(2,1)S(1)}, u32[]{:S(2)}, u32[]{:S(2)}) collective-permute-start(bf16[544,1024]{1,0:T(8,128)(2,1)S(1)} %get-tuple-element.113.refs_0_), channel_id=1, source_target_pairs={{0,4},{12,8},{1,5},{13,9},{2,6},{14,10},{3,7},{15,11},{16,20},{28,... | collective-permute-start | bytes 3342344 | tf_op jit(solution)/shard_map/ppermute | solution.py:405
  66.8 1.2 pass_on.1.refs_0_
  68.0 1.1 copy-done.7
  69.1 1.0 copy-done.9
  70.3 1.4 %join.8 = bf16[544,1024]{1,0:T(8,128)(2,1)S(1)} custom-call(bf16[288,1024]{1,0:T(8,128)(2,1)S(1)} %copy-done.5, bf16[288,1024]{1,0:T(8,128)(2,1)} %collective-permute-done.4.refs_1_, bf16[256,1024]{1,0:T(8,128)(2,1)} %collective-permute-done.6.refs_2_.refs_7_), custom_call_target="tpu_custom_call" | custom-call | flops 1000000 | bytes 100000 | tf_op jit(solution)/shard_map/join/pallas_call | solution.py:347
  71.7 1.3 collective-permute-start.9
  73.7 11.6 %base_terms.7 = (bf16[256,1024]{1,0:T(8,128)(2,1)S(1)}, bf16[256,1024]{1,0:T(8,128)(2,1)S(1)}) custom-call(s32[38]{0:T(128)S(1)} %copy-done.13, bf16[1024,7168]{1,0:T(8,128)(2,1)} %refs_1_.5, bf16[7168,2048]{1,0:T(8,128)(2,1)} %refs_2_.7), custom_call_target="tpu_custom_call" | custom-call | flops 1000000 | bytes 100000 | tf_op jit(solution)/shard_map/base_terms/pallas_call | solution.py:229
  85.3 5.8 %collective-permute-start.10 = (bf16[288,1024]{1,0:T(8,128)(2,1)S(1)}, bf16[288,1024]{1,0:T(8,128)(2,1)S(1)}, u32[]{:S(2)}, u32[]{:S(2)}) collective-permute-start(bf16[288,1024]{1,0:T(8,128)(2,1)S(1)} %copy-done.5), channel_id=1, source_target_pairs={{0,4},{12,8},{1,5},{13,9},{2,6},{14,10},{3,7},{15,11},{16,20},{28,... | collective-permute-start | bytes 1769480 | tf_op jit(solution)/shard_map/ppermute | solution.py:405
  92.3 8.3 %collective-permute-done.9.refs_9_ = bf16[544,1024]{1,0:T(8,128)(2,1)S(1)} collective-permute-done((bf16[544,1024]{1,0:T(8,128)(2,1)S(1)}, bf16[544,1024]{1,0:T(8,128)(2,1)S(1)}, u32[]{:S(2)}, u32[]{:S(2)}) %collective-permute-start.9) | collective-permute-done | bytes 1114144 | tf_op jit(solution)/shard_map/ppermute | solution.py:405
  100.7 1.4 %collective-permute-start.14 = (bf16[512,1024]{1,0:T(8,128)(2,1)S(1)}, bf16[512,1024]{1,0:T(8,128)(2,1)S(1)}, u32[]{:S(2)}, u32[]{:S(2)}) collective-permute-start(bf16[512,1024]{1,0:T(8,128)(2,1)S(1)} %join.10), channel_id=1, source_target_pairs={{8,12},{4,0},{9,13},{5,1},{10,14},{6,2},{11,15},{7,3},{24,28},{20,... | collective-permute-start | bytes 3145736 | tf_op jit(solution)/shard_map/ppermute | solution.py:405
  103.0 1.4 %collective-permute-done.10.refs_11_ = bf16[288,1024]{1,0:T(8,128)(2,1)S(1)} collective-permute-done((bf16[288,1024]{1,0:T(8,128)(2,1)S(1)}, bf16[288,1024]{1,0:T(8,128)(2,1)S(1)}, u32[]{:S(2)}, u32[]{:S(2)}) %collective-permute-start.10) | collective-permute-done | bytes 589856 | tf_op jit(solution)/shard_map/ppermute | solution.py:405
  104.3 5.0 %collective-permute-start.15 = (bf16[256,1024]{1,0:T(8,128)(2,1)S(1)}, bf16[256,1024]{1,0:T(8,128)(2,1)S(1)}, u32[]{:S(2)}, u32[]{:S(2)}) collective-permute-start(bf16[256,1024]{1,0:T(8,128)(2,1)S(1)} %get-tuple-element.122.refs_0_), channel_id=1, source_target_pairs={{0,4},{12,8},{1,5},{13,9},{2,6},{14,10},{3,7},{15,11},{16,20},{28,... | collective-permute-start | bytes 1572872 | tf_op jit(solution)/shard_map/ppermute | solution.py:405
  109.5 1.2 collective-permute-done.12
  110.7 3.6 %collective-permute-start.13 = (bf16[256,128]{1,0:T(8,128)(2,1)S(1)}, bf16[256,128]{1,0:T(8,128)(2,1)S(1)}, u32[]{:S(2)}, u32[]{:S(2)}) collective-permute-start(bf16[256,128]{1,0:T(8,128)(2,1)S(1)} %bitcast_add_fusion), channel_id=1, source_target_pairs={{0,2},{1,3},{2,0},{3,1},{4,6},{5,7},{6,4},{7,5},{8,10},{9,11},{10,... | collective-permute-start | bytes 196616 | tf_op jit(solution)/shard_map/ppermute | solution.py:396
  114.3 2.6 %collective-permute-done.13 = bf16[256,128]{1,0:T(8,128)(2,1)S(1)} collective-permute-done((bf16[256,128]{1,0:T(8,128)(2,1)S(1)}, bf16[256,128]{1,0:T(8,128)(2,1)S(1)}, u32[]{:S(2)}, u32[]{:S(2)}) %collective-permute-start.13) | collective-permute-done | bytes 65568 | tf_op jit(solution)/shard_map/ppermute | solution.py:396
  116.9 10.6 %collective-permute-done.14.refs_10_ = bf16[512,1024]{1,0:T(8,128)(2,1)S(1)} collective-permute-done((bf16[512,1024]{1,0:T(8,128)(2,1)S(1)}, bf16[512,1024]{1,0:T(8,128)(2,1)S(1)}, u32[]{:S(2)}, u32[]{:S(2)}) %collective-permute-start.14) | collective-permute-done | bytes 1048608 | tf_op jit(solution)/shard_map/ppermute | solution.py:405
  127.5 2.3 %finish.1.total = bf16[256,2048]{1,0:T(8,128)(2,1)S(1)} custom-call(s32[38]{0:T(128)S(1)} %copy-done.13, s32[8,128]{1,0:T(8,128)S(1)} %bitcast.18, bf16[256,128]{1,0:T(8,128)(2,1)S(1)} %add.56.refs_2_, bf16[288,1024]{1,0:T(8,128)(2,1)S(1)} %copy-done.3, bf16[256,1024]{1,0:T(8,128)(2,1)S(1)} %get-tuple-element.121.refs_4_, ...), custom_call_target="tpu_custom_call" | custom-call | flops 1000000 | bytes 100000 | tf_op jit(solution)/shard_map/finish/pallas_call | solution.py:321
  129.8 1.2 add_last.1
  (57 shorter events, 6.2 us)
Async XLA Ops:
  0.8 1.6 %copy-start.1 = (bf16[4,32,8192]{2,1,0:T(8,128)(2,1)S(1)}, bf16[4,32,8192]{2,1,0:T(8,128)(2,1)}, u32[]{:S(2)}) copy-start(bf16[4,32,8192]{2,1,0:T(8,128)(2,1)} %refs_1_.3) | copy-start | bytes 6291460
  2.4 1.4 %copy-start.11 = (s32[38]{0:T(128)}, s32[38]{0:T(128)S(1)}, u32[]{:S(2)}) copy-start(s32[38]{0:T(128)S(1)} %concatenate.3.refs_0_.token_ref) | copy-start | bytes 460
  3.2 14.4 %collective-permute-start = (bf16[2,256,1024]{2,1,0:T(8,128)(2,1)S(1)}, bf16[2,256,1024]{2,1,0:T(8,128)(2,1)}, u32[]{:S(2)}, u32[]{:S(2)}) collective-permute-start(bf16[2,256,1024]{2,1,0:T(8,128)(2,1)S(1)} %get-tuple-element.65), channel_id=1, source_target_pairs={{0,1},{1,0},{2,3},{3,2},{4,5},{5,4},{6,7},{7,6},{8,9},{9,8},{10,11... | collective-permute-start | bytes 3145736 | tf_op jit(solution)/shard_map/ppermute | solution.py:396
  13.0 20.7 %collective-permute-start.1 = (bf16[288,1024]{1,0:T(8,128)(2,1)}, bf16[288,1024]{1,0:T(8,128)(2,1)S(1)}, u32[]{:S(2)}, u32[]{:S(2)}) collective-permute-start(bf16[288,1024]{1,0:T(8,128)(2,1)} %base_terms.4.refs_0_), channel_id=1, source_target_pairs={{0,4},{12,8},{1,5},{13,9},{2,6},{14,10},{3,7},{15,11},{16,20},{28,... | collective-permute-start | bytes 1769480 | tf_op jit(solution)/shard_map/ppermute | solution.py:405
  17.6 2.9 %copy-start.12 = (s32[38]{0:T(128)S(1)}, s32[38]{0:T(128)}, u32[]{:S(2)}) copy-start(s32[38]{0:T(128)} %copy-done.11) | copy-start | bytes 460
  18.9 17.4 %collective-permute-start.2 = (bf16[256,1024]{1,0:T(8,128)(2,1)S(1)}, bf16[256,1024]{1,0:T(8,128)(2,1)S(1)}, u32[]{:S(2)}, u32[]{:S(2)}) collective-permute-start(bf16[256,1024]{1,0:T(8,128)(2,1)S(1)} %get-tuple-element.124), channel_id=1, source_target_pairs={{0,2},{1,3},{2,0},{3,1},{4,6},{5,7},{6,4},{7,5},{8,10},{9,11},{10,... | collective-permute-start | bytes 1572872 | tf_op jit(solution)/shard_map/ppermute | solution.py:396
  20.5 20.2 %slice-start = ((s8[7340032]{0:T(1024)(128)(4,1)}), s8[4194304]{0:T(1024)(128)(4,1)S(1)}, s32[]{:S(2)}) async-start(s8[7340032]{0:T(1024)(128)(4,1)} %bitcast.14), calls=%async_computation | async-start | bytes 8388608
  20.5 13.2 %copy-start = (bf16[288,1024]{1,0:T(8,128)(2,1)S(1)}, bf16[288,1024]{1,0:T(8,128)(2,1)}, u32[]{:S(2)}) copy-start(bf16[288,1024]{1,0:T(8,128)(2,1)} %base_terms.4.refs_0_) | copy-start | bytes 1769476
  20.5 20.2 %slice-start.1 = ((s8[7340032]{0:T(1024)(128)(4,1)}), s8[3145728]{0:T(1024)(128)(4,1)S(1)}, s32[]{:S(2)}) async-start(s8[7340032]{0:T(1024)(128)(4,1)} %bitcast.14), calls=%async_computation.1 | async-start | bytes 6291456
  32.4 4.2 %copy-start.6 = (bf16[256,1024]{1,0:T(8,128)(2,1)}, bf16[256,1024]{1,0:T(8,128)(2,1)S(1)}, u32[]{:S(2)}) copy-start(bf16[256,1024]{1,0:T(8,128)(2,1)S(1)} %get-tuple-element.90.refs_0_) | copy-start | bytes 1572868
  32.4 28.9 %collective-permute-start.3 = (bf16[256,1024]{1,0:T(8,128)(2,1)S(1)}, bf16[256,1024]{1,0:T(8,128)(2,1)S(1)}, u32[]{:S(2)}, u32[]{:S(2)}) collective-permute-start(bf16[256,1024]{1,0:T(8,128)(2,1)S(1)} %get-tuple-element.90.refs_0_), channel_id=1, source_target_pairs={{0,4},{12,8},{1,5},{13,9},{2,6},{14,10},{3,7},{15,11},{16,20},{28,... | collective-permute-start | bytes 1572872 | tf_op jit(solution)/shard_map/ppermute | solution.py:405
  34.7 6.0 %copy-start.10 = (s32[1024]{0:T(1024)S(1)}, s32[1024]{0:T(1024)}, u32[]{:S(2)}) copy-start(s32[1024]{0:T(1024)} %param.12) | copy-start | bytes 12292
  34.7 33.3 %collective-permute-start.4 = (bf16[288,1024]{1,0:T(8,128)(2,1)}, bf16[288,1024]{1,0:T(8,128)(2,1)}, u32[]{:S(2)}, u32[]{:S(2)}) collective-permute-start(bf16[288,1024]{1,0:T(8,128)(2,1)} %join.6), channel_id=1, source_target_pairs={{4,8},{8,4},{5,9},{9,5},{6,10},{10,6},{7,11},{11,7},{20,24},{24,20... | collective-permute-start | bytes 1769480 | tf_op jit(solution)/shard_map/ppermute | solution.py:405
  36.5 31.5 %collective-permute-start.5 = (bf16[256,1024]{1,0:T(8,128)(2,1)S(1)}, bf16[256,1024]{1,0:T(8,128)(2,1)S(1)}, u32[]{:S(2)}, u32[]{:S(2)}) collective-permute-start(bf16[256,1024]{1,0:T(8,128)(2,1)S(1)} %add.51.refs_5_), channel_id=1, source_target_pairs={{0,4},{12,8},{4,0},{8,12},{1,5},{13,9},{5,1},{9,13},{2,6},{14,10},... | collective-permute-start | bytes 1572872 | tf_op jit(solution)/shard_map/ppermute | solution.py:446
  39.2 31.1 %collective-permute-start.6 = (bf16[256,1024]{1,0:T(8,128)(2,1)S(1)}, bf16[256,1024]{1,0:T(8,128)(2,1)}, u32[]{:S(2)}, u32[]{:S(2)}) collective-permute-start(bf16[256,1024]{1,0:T(8,128)(2,1)S(1)} %add.51.refs_5_), channel_id=1, source_target_pairs={{4,8},{8,4},{5,9},{9,5},{6,10},{10,6},{7,11},{11,7},{20,24},{24,20... | collective-permute-start | bytes 1572872 | tf_op jit(solution)/shard_map/ppermute | solution.py:405
  59.6 0.9 copy-start.2
  60.4 0.8 copy-start.4
  62.1 29.4 %collective-permute-start.7 = (bf16[544,1024]{1,0:T(8,128)(2,1)S(1)}, bf16[544,1024]{1,0:T(8,128)(2,1)S(1)}, u32[]{:S(2)}, u32[]{:S(2)}) collective-permute-start(bf16[544,1024]{1,0:T(8,128)(2,1)S(1)} %get-tuple-element.113.refs_0_), channel_id=1, source_target_pairs={{0,4},{12,8},{1,5},{13,9},{2,6},{14,10},{3,7},{15,11},{16,20},{28,... | collective-permute-start | bytes 3342344 | tf_op jit(solution)/shard_map/ppermute | solution.py:405
  68.0 2.3 %copy-start.5 = (bf16[288,1024]{1,0:T(8,128)(2,1)S(1)}, bf16[288,1024]{1,0:T(8,128)(2,1)}, u32[]{:S(2)}) copy-start(bf16[288,1024]{1,0:T(8,128)(2,1)} %copy-done.4) | copy-start | bytes 1769476
  68.0 1.1 copy-start.7
  69.1 1.0 copy-start.9
  70.3 3.4 %copy-start.13 = (s32[38]{0:T(128)S(1)}, s32[38]{0:T(128)}, u32[]{:S(2)}) copy-start(s32[38]{0:T(128)} %pass_on.1.refs_0_) | copy-start | bytes 460
  71.7 28.9 %collective-permute-start.9 = (bf16[544,1024]{1,0:T(8,128)(2,1)S(1)}, bf16[544,1024]{1,0:T(8,128)(2,1)S(1)}, u32[]{:S(2)}, u32[]{:S(2)}) collective-permute-start(bf16[544,1024]{1,0:T(8,128)(2,1)S(1)} %join.8), channel_id=1, source_target_pairs={{8,12},{4,0},{9,13},{5,1},{10,14},{6,2},{11,15},{7,3},{24,28},{20,... | collective-permute-start | bytes 3342344 | tf_op jit(solution)/shard_map/ppermute | solution.py:405
  73.0 19.3 %collective-permute-start.8 = (bf16[512,1024]{1,0:T(8,128)(2,1)S(1)}, bf16[512,1024]{1,0:T(8,128)(2,1)S(1)}, u32[]{:S(2)}, u32[]{:S(2)}) collective-permute-start(bf16[512,1024]{1,0:T(8,128)(2,1)S(1)} %join.7), channel_id=1, source_target_pairs={{4,8},{8,4},{5,9},{9,5},{6,10},{10,6},{7,11},{11,7},{20,24},{24,20... | collective-permute-start | bytes 3145736 | tf_op jit(solution)/shard_map/ppermute | solution.py:405
  85.3 19.0 %collective-permute-start.10 = (bf16[288,1024]{1,0:T(8,128)(2,1)S(1)}, bf16[288,1024]{1,0:T(8,128)(2,1)S(1)}, u32[]{:S(2)}, u32[]{:S(2)}) collective-permute-start(bf16[288,1024]{1,0:T(8,128)(2,1)S(1)} %copy-done.5), channel_id=1, source_target_pairs={{0,4},{12,8},{1,5},{13,9},{2,6},{14,10},{3,7},{15,11},{16,20},{28,... | collective-permute-start | bytes 1769480 | tf_op jit(solution)/shard_map/ppermute | solution.py:405
  91.6 17.7 %collective-permute-start.11 = (bf16[288,1024]{1,0:T(8,128)(2,1)S(1)}, bf16[288,1024]{1,0:T(8,128)(2,1)S(1)}, u32[]{:S(2)}, u32[]{:S(2)}) collective-permute-start(bf16[288,1024]{1,0:T(8,128)(2,1)S(1)} %join.9), channel_id=1, source_target_pairs={{4,8},{8,4},{5,9},{9,5},{6,10},{10,6},{7,11},{11,7},{20,24},{24,20... | collective-permute-start | bytes 1769480 | tf_op jit(solution)/shard_map/ppermute | solution.py:405
  100.7 8.6 %copy-start.3 = (bf16[288,1024]{1,0:T(8,128)(2,1)S(1)}, bf16[288,1024]{1,0:T(8,128)(2,1)}, u32[]{:S(2)}) copy-start(bf16[288,1024]{1,0:T(8,128)(2,1)} %copy-done.2) | copy-start | bytes 1769476
  100.7 26.8 %collective-permute-start.14 = (bf16[512,1024]{1,0:T(8,128)(2,1)S(1)}, bf16[512,1024]{1,0:T(8,128)(2,1)S(1)}, u32[]{:S(2)}, u32[]{:S(2)}) collective-permute-start(bf16[512,1024]{1,0:T(8,128)(2,1)S(1)} %join.10), channel_id=1, source_target_pairs={{8,12},{4,0},{9,13},{5,1},{10,14},{6,2},{11,15},{7,3},{24,28},{20,... | collective-permute-start | bytes 3145736 | tf_op jit(solution)/shard_map/ppermute | solution.py:405
  102.3 27.5 %collective-permute-start.16 = (bf16[256,1024]{1,0:T(8,128)(2,1)S(1)}, bf16[256,1024]{1,0:T(8,128)(2,1)S(1)}, u32[]{:S(2)}, u32[]{:S(2)}) collective-permute-start(bf16[256,1024]{1,0:T(8,128)(2,1)S(1)} %join.11), channel_id=1, source_target_pairs={{4,8},{8,4},{5,9},{9,5},{6,10},{10,6},{7,11},{11,7},{20,24},{24,20... | collective-permute-start | bytes 1572872 | tf_op jit(solution)/shard_map/ppermute | solution.py:405
  104.3 25.5 %collective-permute-start.15 = (bf16[256,1024]{1,0:T(8,128)(2,1)S(1)}, bf16[256,1024]{1,0:T(8,128)(2,1)S(1)}, u32[]{:S(2)}, u32[]{:S(2)}) collective-permute-start(bf16[256,1024]{1,0:T(8,128)(2,1)S(1)} %get-tuple-element.122.refs_0_), channel_id=1, source_target_pairs={{0,4},{12,8},{1,5},{13,9},{2,6},{14,10},{3,7},{15,11},{16,20},{28,... | collective-permute-start | bytes 1572872 | tf_op jit(solution)/shard_map/ppermute | solution.py:405
  109.4 1.3 %collective-permute-start.12 = (bf16[256,128]{1,0:T(8,128)(2,1)S(1)}, bf16[256,128]{1,0:T(8,128)(2,1)S(1)}, u32[]{:S(2)}, u32[]{:S(2)}) collective-permute-start(bf16[256,128]{1,0:T(8,128)(2,1)S(1)} %bitcast.19), channel_id=1, source_target_pairs={{0,1},{1,0},{2,3},{3,2},{4,5},{5,4},{6,7},{7,6},{8,9},{9,8},{10,11... | collective-permute-start | bytes 196616 | tf_op jit(solution)/shard_map/ppermute | solution.py:396
  110.7 6.2 %collective-permute-start.13 = (bf16[256,128]{1,0:T(8,128)(2,1)S(1)}, bf16[256,128]{1,0:T(8,128)(2,1)S(1)}, u32[]{:S(2)}, u32[]{:S(2)}) collective-permute-start(bf16[256,128]{1,0:T(8,128)(2,1)S(1)} %bitcast_add_fusion), channel_id=1, source_target_pairs={{0,2},{1,3},{2,0},{3,1},{4,6},{5,7},{6,4},{7,5},{8,10},{9,11},{10,... | collective-permute-start | bytes 196616 | tf_op jit(solution)/shard_map/ppermute | solution.py:396
  (1 other events, 0.8 us)
where the time goes:
time: 133 us; the launch traced here: 131 us
  Pallas kernels  60 us (45%)
  starting transfers between devices  37.7 us (28%)
  waiting for transfers between devices  24.3 us (18%)
  local copies, waits for them, and re-layouts  7.01 us (5%)
  other arithmetic  1.58 us (1%)
    pallas_call x4, Pallas kernels, base_terms(): pl.pallas_call(lambda *refs: base_kernel(line_order(n), groups, half, hel...  51.7 us
    ppermute x12, starting transfers between devices, along_edge(): lax.ppermute(x, 'tensor', [(edge, edge + 1), (n - 1 - edge, n - 2 - edge)])  29.3 us
    ppermute x12, waiting for transfers between devices, along_edge(): lax.ppermute(x, 'tensor', [(edge, edge + 1), (n - 1 - edge, n - 2 - edge)])  20.4 us
    unnamed x33, local copies, waits for them, and re-layouts  6.23 us
    ppermute x4, starting transfers between devices, swap(): lax.ppermute(x, axis, [(i, i ^ bit) for i in range(lax.axis_size(axis))])  5.72 us
    ppermute x4, waiting for transfers between devices, swap(): lax.ppermute(x, axis, [(i, i ^ bit) for i in range(lax.axis_size(axis))])  3.86 us
    pallas_call x6, Pallas kernels, join(): pl.pallas_call(lambda *refs: join_kernel(count, term_top, came_top, under...  2.89 us
    ppermute x1, starting transfers between devices, on_line(): lax.ppermute(rows, 'tensor', [(0, 1), (n - 1, n - 2), (1, 0), (n - 2, n -...  2.67 us
  transfers between devices with their start and end apart: 17, of which 6 were waited for; matrix products, arithmetic and copies ran while one was open for 1% of the time, Pallas kernels for 44%

commit v1 on v0

--- a/solution.py
+++ b/solution.py
@@ -11,6 +11,7 @@
 LANES = 128
 AHEAD = 3
 PAIRS = 2
+HEAVY = 10**10
 MIB = 1024 * 1024
 
 
@@ -340,7 +341,7 @@
         out[count:, :] = under[under_top : under_top + out.shape[0] - count, :]
 
 
-def join(token, count, term, term_top, came, came_top, under=None, under_top=0, under_count=0):
+def join(token, count, term, term_top, came, came_top, under=None, under_top=0, under_count=0, weight=10**6):
     arrays = [term, came] + ([] if under is None else [under])
     arrays = lax.optimization_barrier((arrays, token))[0]
     vmem = pl.BlockSpec(memory_space=pltpu.VMEM)
@@ -350,46 +351,32 @@
         in_specs=[vmem] * len(arrays),
         out_specs=vmem,
         compiler_params=params(12),
-        cost_estimate=small_cost(),
+        cost_estimate=pl.CostEstimate(flops=weight, bytes_accessed=10**5, transcendentals=0),
         name="join",
     )(*arrays)
 
 
-def add_last_kernel(total, up, down, out):
-    half = up.shape[1]
+def add_last_kernel(total, *refs):
+    arrivals, out = refs[:-1], refs[-1]
+    half = arrivals[0].shape[1]
     out[:, :half] = total[:, :half]
-    last = total[:, half:].astype(jnp.float32) + up[...].astype(jnp.float32) + down[...].astype(jnp.float32)
+    last = total[:, half:].astype(jnp.float32)
+    for arrival in arrivals:
+        last += arrival[...].astype(jnp.float32)
     out[:, half:] = last.astype(out.dtype)
 
 
-def add_last(total, up, down):
+def add_last(total, *arrivals):
     vmem = pl.BlockSpec(memory_space=pltpu.VMEM)
     return pl.pallas_call(
         add_last_kernel,
         out_shape=jax.ShapeDtypeStruct(total.shape, total.dtype),
-        in_specs=[vmem] * 3,
+        in_specs=[vmem] * (1 + len(arrivals)),
         out_specs=vmem,
         compiler_params=params(12),
         cost_estimate=small_cost(),
         name="add_last",
-    )(total, up, down)
-
-
-def pass_kernel(token_ref, out_ref):
-    for i in range(token_ref.shape[0]):
-        out_ref[i] = token_ref[i]
-
-
-def pass_on(token):
-    smem = pl.BlockSpec(memory_space=pltpu.SMEM)
-    return pl.pallas_call(
-        pass_kernel,
-        out_shape=jax.ShapeDtypeStruct(token.shape, token.dtype),
-        in_specs=[smem],
-        out_specs=smem,
-        cost_estimate=pl.CostEstimate(flops=4 * 10**9, bytes_accessed=10**3, transcendentals=0),
-        name="pass_on",
-    )(token)
+    )(total, *arrivals)
 
 
 def swap(x, axis, bit):
@@ -445,17 +432,16 @@
     token = after(token, rows)
     near = lax.ppermute(rows, "tensor", [(0, 1), (n - 1, n - 2), (1, 0), (n - 2, n - 1)])
     far = along_edge(rows, 1)
-    s10_s11, s20, s30 = base(token, [[1], [2], [3]], 0, 42, s11)
+    s10_s11, s20, s30 = base(token, [[1], [2], [3]], 0, 50, s11)
 
     token = after(token, s10_s11)
     e0_3 = send(s10_s11, 0, token)
     token, e0_2 = lax.optimization_barrier((token, e0_2))
-    token = pass_on(token)
-    token, e1_2 = lax.optimization_barrier((token, e1_2))
-    token, near = lax.optimization_barrier((token, near))
-    b11 = join(token, block, s01, 0, e0_2, 0, near, 0, bundle)
-    token = after(token, b11)
+    b11 = join(token, block, s01, 0, e0_2, 0, weight=HEAVY)
+    token, near = lax.optimization_barrier((after(token, b11), near))
     e1_3 = along_edge(b11, 1)
+    far_2 = send(near, 1, token)
+    token, e1_2, far = lax.optimization_barrier((token, e1_2, far))
     c20 = join(token, piece, s20, 0, e1_2, 0, far, 0, bundle)
     token = after(token, c20)
     e2_3 = along_edge(c20, 2)
@@ -467,34 +453,39 @@
     b20 = join(token, piece, s10_s11, 0, e0_3, 0)
     token = after(token, b20)
     e1_4 = along_edge(b20, 1)
-    token = after(token, e1_3, e2_3)
-    c21 = join(token, block, s21, 0, e1_3, 0, e1_3, block, bundle)
+    token, far_2 = lax.optimization_barrier((token, far_2))
+    last_rows = send(far_2, 2, token)
+    token, e1_3 = lax.optimization_barrier((token, e1_3))
+    c21 = join(token, block, s21, 0, e1_3, 0, weight=HEAVY)
     token = after(token, c21)
     e2_4 = along_edge(c21, 2)
+    token, e2_3 = lax.optimization_barrier((token, e2_3))
     e0_5 = send(s21, 0, token)
     b21 = join(token, block, s10_s11, piece, e0_3, piece)
     token = after(token, b21)
     e1_5 = along_edge(b21, 1)
 
     token, e0_4 = lax.optimization_barrier((token, e0_4))
-    e1_4 = lax.optimization_barrier((e1_4, token))[0]
+    token, e1_4 = lax.optimization_barrier((token, e1_4))
+    token, last_rows = lax.optimization_barrier((token, last_rows))
+    e1_4 = after(e1_4, token)
     lora = s30[block:].astype(jnp.float32) + e0_4[block:].astype(jnp.float32)
     lora += e1_4[block:].astype(jnp.float32) + e2_3[block:piece].astype(jnp.float32)
     lora = lora.astype(jnp.bfloat16).reshape(piece - block, -1, width).swapaxes(0, 1).reshape(block, width)
     lora = lora + swap(lora, "store", 1)
     lora = lora + swap(lora, "store", 2)
-    arrays = [s30, s31, rows, near, far, e1_3, e2_3, e2_4, e0_4, e1_4]
+    arrays = [s30, s31, rows, near, far, far_2, e2_3, last_rows, e0_4, e1_4]
     items = [
         (2, 0, [(z, z) for z in range(n)]),
         (3, 0, [(0, 1), (1, 0), (2, 3), (3, 2)]),
         (4, 0, [(1, 2), (2, 1)]),
-        (5, block, [(1, 3), (2, 0)]),
+        (5, 0, [(1, 3), (2, 0)]),
         (6, piece, [(0, 2), (3, 1)]),
-        (7, block, [(0, 3), (3, 0)]),
+        (7, 0, [(0, 3), (3, 0)]),
     ]
-    added = [(0, 0, 0), (8, 0, 0), (9, 0, 0), (6, 0, 0), (1, 0, 1), (7, 0, 1)]
+    added = [(0, 0, 0), (8, 0, 0), (9, 0, 0), (6, 0, 0), (1, 0, 1)]
     out = finish(token, requests, lora, arrays, items, added, request_count, rank_rows, n)
-    return add_last(out, e0_5, e1_5)
+    return add_last(out, e0_5, e1_5, e2_4)
 
 
 def anywhere(hidden, matrix, input_factor, output_factor, token_requests, meta):

time: 133 us -> 118 us (0.89)
  starting transfers between devices: 37.7 us -> 32.7 us
  waiting for transfers between devices: 24.3 us -> 19.6 us
  local copies, waits for them, and re-layouts: 7.01 us -> 2.4 us
    ppermute x12 -> x14, waiting for transfers between devices: 20.4 us -> 14.3 us  [along_edge(): lax.ppermute(x, 'tensor', [(edge, edge + 1), (n - 1 - edge, n - 2 - edge)])]
    unnamed x33 -> x11, local copies, waits for them, and re-layouts: 6.23 us -> 1.62 us
    ppermute x12 -> x14, starting transfers between devices: 29.3 us -> 25.5 us  [along_edge(): lax.ppermute(x, 'tensor', [(edge, edge + 1), (n - 1 - edge, n - 2 - edge)])]
    pallas_call x4, Pallas kernels: 51.7 us -> 55.4 us  [base_terms(): pl.pallas_call(lambda *refs: base_kernel(line_order(n), groups, half, hel...]
    ppermute x4, starting transfers between devices: 5.72 us -> 2.49 us  [swap(): lax.ppermute(x, axis, [(i, i ^ bit) for i in range(lax.axis_size(axis))])]
    pallas_call x6, Pallas kernels: 2.89 us -> 0.81 us  [join(): pl.pallas_call(lambda *refs: join_kernel(count, term_top, came_top, under...]
    ppermute x1, starting transfers between devices: 2.67 us -> 4.64 us  [on_line(): lax.ppermute(rows, 'tensor', [(0, 1), (n - 1, n - 2), (1, 0), (n - 2, n -...]
    ppermute x4, waiting for transfers between devices: 3.86 us -> 5.23 us  [swap(): lax.ppermute(x, axis, [(i, i ^ bit) for i in range(lax.axis_size(axis))])]
  transfers between devices with their start and end apart: 17 -> 19, of which waited for: 6 -> 5; matrix products, arithmetic and copies ran while one was open for 1% -> 1% of each run, Pallas kernels for 44% -> 50%
where the time goes in v1:
time: 118 us; the launch traced here: 117 us
  Pallas kernels  60.1 us (51%)
  starting transfers between devices  32.7 us (28%)
  waiting for transfers between devices  19.6 us (17%)
  local copies, waits for them, and re-layouts  2.4 us (2%)
  other arithmetic  1.58 us (1%)
    pallas_call x4, Pallas kernels, base_terms(): pl.pallas_call(lambda *refs: base_kernel(line_order(n), groups, half, hel...  55.4 us
    ppermute x14, starting transfers between devices, along_edge(): lax.ppermute(x, 'tensor', [(edge, edge + 1), (n - 1 - edge, n - 2 - edge)])  25.5 us
    ppermute x14, waiting for transfers between devices, along_edge(): lax.ppermute(x, 'tensor', [(edge, edge + 1), (n - 1 - edge, n - 2 - edge)])  14.3 us
    ppermute x4, waiting for transfers between devices, swap(): lax.ppermute(x, axis, [(i, i ^ bit) for i in range(lax.axis_size(axis))])  5.23 us
    ppermute x1, starting transfers between devices, on_line(): lax.ppermute(rows, 'tensor', [(0, 1), (n - 1, n - 2), (1, 0), (n - 2, n -...  4.64 us
    ppermute x4, starting transfers between devices, swap(): lax.ppermute(x, axis, [(i, i ^ bit) for i in range(lax.axis_size(axis))])  2.49 us
  transfers between devices with their start and end apart: 19, of which 5 were waited for; matrix products, arithmetic and copies ran while one was open for 1% of the time, Pallas kernels for 50%

profile of v1, /device:TPU:0, one launch (start us, length us, event | category | flops | bytes accessed | tf_op | source)
XLA Modules:
  0.0 116.7 jit_solution(16767316749682433759)
XLA Ops:
  0.0 0.8 concatenate.3.refs_0_
  0.8 1.6 %copy-done.1 = bf16[4,32,8192]{2,1,0:T(8,128)(2,1)S(1)} copy-done((bf16[4,32,8192]{2,1,0:T(8,128)(2,1)S(1)}, bf16[4,32,8192]{2,1,0:T(8,128)(2,1)}, u32[]{:S(2)}) %copy-start.1) | copy-done | bytes 2097176
  2.4 0.8 select_rows.1
  3.2 0.5 collective-permute-start
  3.7 9.3 %base_terms.4.refs_0_ = bf16[288,1024]{1,0:T(8,128)(2,1)} custom-call(s32[38]{0:T(128)} %copy-done.3, s32[8,128]{1,0:T(8,128)} %bitcast.14, bf16[4,7168,128]{2,1,0:T(8,128)(2,1)} %refs_2_.6, bf16[1024,7168]{1,0:T(8,128)(2,1)} %refs_1_.5, bf16[7168,2048]{1,0:T(8,128)(2,1)} %refs_2_.7), custom_call_target="tpu_custom_call" | custom-call | flops 1000000 | bytes 100000 | tf_op jit(solution)/shard_map/base_terms/pallas_call | solution.py:230
  13.0 4.5 %collective-permute-start.1 = (bf16[288,1024]{1,0:T(8,128)(2,1)}, bf16[288,1024]{1,0:T(8,128)(2,1)S(1)}, u32[]{:S(2)}, u32[]{:S(2)}) collective-permute-start(bf16[288,1024]{1,0:T(8,128)(2,1)} %base_terms.4.refs_0_), channel_id=1, source_target_pairs={{0,4},{12,8},{1,5},{13,9},{2,6},{14,10},{3,7},{15,11},{16,20},{28,... | collective-permute-start | bytes 1769480 | tf_op jit(solution)/shard_map/ppermute | solution.py:392
  17.6 1.3 %add_bitcast_fusion = (bf16[256,1024]{1,0:T(8,128)(2,1)S(1)}, bf16[256,1024]{1,0:T(8,128)(2,1)S(1)}) fusion(bf16[2,256,1024]{2,1,0:T(8,128)(2,1)} %collective-permute-done, s32[]{:T(128)S(6)} %select_n.22, bf16[2,256,1024]{2,1,0:T(8,128)(2,1)S(1)} %get-tuple-element.78, s32[]{:T(128)S(6)} %select_n.21), kind=kLoop, calls=%fused_computation | loop fusion | flops 524288 | bytes 3145736 | tf_op jit(solution)/shard_map/add | solution.py:419
  18.9 1.6 %collective-permute-start.2 = (bf16[256,1024]{1,0:T(8,128)(2,1)S(1)}, bf16[256,1024]{1,0:T(8,128)(2,1)S(1)}, u32[]{:S(2)}, u32[]{:S(2)}) collective-permute-start(bf16[256,1024]{1,0:T(8,128)(2,1)S(1)} %get-tuple-element.144), channel_id=1, source_target_pairs={{0,2},{1,3},{2,0},{3,1},{4,6},{5,7},{6,4},{7,5},{8,10},{9,11},{10,... | collective-permute-start | bytes 1572872 | tf_op jit(solution)/shard_map/ppermute | solution.py:383
  20.5 11.6 %base_terms.5 = (bf16[256,1024]{1,0:T(8,128)(2,1)S(1)}, bf16[256,1024]{1,0:T(8,128)(2,1)S(1)}) custom-call(s32[38]{0:T(128)S(1)} %copy-done.4, bf16[1024,7168]{1,0:T(8,128)(2,1)} %refs_1_.5, bf16[7168,2048]{1,0:T(8,128)(2,1)} %refs_2_.7), custom_call_target="tpu_custom_call" | custom-call | flops 1000000 | bytes 100000 | tf_op jit(solution)/shard_map/base_terms/pallas_call | solution.py:230
  32.1 1.3 %collective-permute-start.3 = (bf16[256,1024]{1,0:T(8,128)(2,1)S(1)}, bf16[256,1024]{1,0:T(8,128)(2,1)S(1)}, u32[]{:S(2)}, u32[]{:S(2)}) collective-permute-start(bf16[256,1024]{1,0:T(8,128)(2,1)S(1)} %get-tuple-element.97.refs_0_), channel_id=1, source_target_pairs={{0,4},{12,8},{1,5},{13,9},{2,6},{14,10},{3,7},{15,11},{16,20},{28,... | collective-permute-start | bytes 1572872 | tf_op jit(solution)/shard_map/ppermute | solution.py:392
  33.6 0.7 collective-permute-start.5
  34.5 0.7 collective-permute-start.6
  35.2 4.6 %collective-permute-start.4 = (bf16[256,1024]{1,0:T(8,128)(2,1)S(1)}, bf16[256,1024]{1,0:T(8,128)(2,1)S(1)}, u32[]{:S(2)}, u32[]{:S(2)}) collective-permute-start(bf16[256,1024]{1,0:T(8,128)(2,1)S(1)} %add.51.refs_5_), channel_id=1, source_target_pairs={{0,4},{12,8},{4,0},{8,12},{1,5},{13,9},{5,1},{9,13},{2,6},{14,10},... | collective-permute-start | bytes 1572872 | tf_op jit(solution)/shard_map/ppermute | solution.py:433
  39.9 22.9 %base_terms.6 = (bf16[544,1024]{1,0:T(8,128)(2,1)S(1)}, bf16[288,1024]{1,0:T(8,128)(2,1)S(1)}, bf16[288,1024]{1,0:T(8,128)(2,1)S(1)}) custom-call(s32[38]{0:T(128)S(1)} %copy-done.4, s32[8,128]{1,0:T(8,128)S(1)} %bitcast.15, bf16[4,7168,128]{2,1,0:T(8,128)(2,1)} %refs_2_.6, bf16[1024,7168]{1,0:T(8,128)(2,1)} %refs_1_.5, bf16[7168,2048]{1,0:T(8,128)(2,1)} %refs_2_.7, ...), custom_call_target="tpu_custom_call" | custom-call | flops 1000000 | bytes 100000 | tf_op jit(solution)/shard_map/base_terms/pallas_call | solution.py:230
  62.8 2.0 %collective-permute-start.7 = (bf16[544,1024]{1,0:T(8,128)(2,1)S(1)}, bf16[544,1024]{1,0:T(8,128)(2,1)S(1)}, u32[]{:S(2)}, u32[]{:S(2)}) collective-permute-start(bf16[544,1024]{1,0:T(8,128)(2,1)S(1)} %get-tuple-element.126.refs_0_), channel_id=1, source_target_pairs={{0,4},{12,8},{1,5},{13,9},{2,6},{14,10},{3,7},{15,11},{16,20},{28,... | collective-permute-start | bytes 3342344 | tf_op jit(solution)/shard_map/ppermute | solution.py:392
  65.0 0.7 collective-permute-start.8
  65.7 0.7 collective-permute-start.9
  66.5 1.3 %collective-permute-start.10 = (bf16[544,1024]{1,0:T(8,128)(2,1)S(1)}, bf16[544,1024]{1,0:T(8,128)(2,1)S(1)}, u32[]{:S(2)}, u32[]{:S(2)}) collective-permute-start(bf16[544,1024]{1,0:T(8,128)(2,1)S(1)} %join.8), channel_id=1, source_target_pairs={{8,12},{4,0},{9,13},{5,1},{10,14},{6,2},{11,15},{7,3},{24,28},{20,... | collective-permute-start | bytes 3342344 | tf_op jit(solution)/shard_map/ppermute | solution.py:392
  67.8 11.6 %base_terms.7 = (bf16[256,1024]{1,0:T(8,128)(2,1)S(1)}, bf16[256,1024]{1,0:T(8,128)(2,1)S(1)}) custom-call(s32[38]{0:T(128)S(1)} %copy-done.4, bf16[1024,7168]{1,0:T(8,128)(2,1)} %refs_1_.5, bf16[7168,2048]{1,0:T(8,128)(2,1)} %refs_2_.7), custom_call_target="tpu_custom_call" | custom-call | flops 1000000 | bytes 100000 | tf_op jit(solution)/shard_map/base_terms/pallas_call | solution.py:230
  79.5 5.8 %collective-permute-start.11 = (bf16[288,1024]{1,0:T(8,128)(2,1)S(1)}, bf16[288,1024]{1,0:T(8,128)(2,1)S(1)}, u32[]{:S(2)}, u32[]{:S(2)}) collective-permute-start(bf16[288,1024]{1,0:T(8,128)(2,1)S(1)} %get-tuple-element.129.refs_0_), channel_id=1, source_target_pairs={{0,4},{12,8},{1,5},{13,9},{2,6},{14,10},{3,7},{15,11},{16,20},{28,... | collective-permute-start | bytes 1769480 | tf_op jit(solution)/shard_map/ppermute | solution.py:392
  85.2 2.6 %collective-permute-done.7.refs_1_ = bf16[544,1024]{1,0:T(8,128)(2,1)S(1)} collective-permute-done((bf16[544,1024]{1,0:T(8,128)(2,1)S(1)}, bf16[544,1024]{1,0:T(8,128)(2,1)S(1)}, u32[]{:S(2)}, u32[]{:S(2)}) %collective-permute-start.7) | collective-permute-done | bytes 1114144 | tf_op jit(solution)/shard_map/ppermute | solution.py:392
  88.0 0.7 collective-permute-start.12
  88.7 1.3 %collective-permute-start.13 = (bf16[256,1024]{1,0:T(8,128)(2,1)S(1)}, bf16[256,1024]{1,0:T(8,128)(2,1)S(1)}, u32[]{:S(2)}, u32[]{:S(2)}) collective-permute-start(bf16[256,1024]{1,0:T(8,128)(2,1)S(1)} %collective-permute-done.8.refs_8_), channel_id=1, source_target_pairs={{8,12},{4,0},{9,13},{5,1},{10,14},{6,2},{11,15},{7,3},{24,28},{20,... | collective-permute-start | bytes 1572872 | tf_op jit(solution)/shard_map/ppermute | solution.py:392
  90.2 1.3 %collective-permute-start.18 = (bf16[256,1024]{1,0:T(8,128)(2,1)S(1)}, bf16[256,1024]{1,0:T(8,128)(2,1)S(1)}, u32[]{:S(2)}, u32[]{:S(2)}) collective-permute-start(bf16[256,1024]{1,0:T(8,128)(2,1)S(1)} %join.10), channel_id=1, source_target_pairs={{8,12},{4,0},{9,13},{5,1},{10,14},{6,2},{11,15},{7,3},{24,28},{20,... | collective-permute-start | bytes 1572872 | tf_op jit(solution)/shard_map/ppermute | solution.py:392
  91.5 5.1 %collective-permute-done.10.refs_9_ = bf16[544,1024]{1,0:T(8,128)(2,1)S(1)} collective-permute-done((bf16[544,1024]{1,0:T(8,128)(2,1)S(1)}, bf16[544,1024]{1,0:T(8,128)(2,1)S(1)}, u32[]{:S(2)}, u32[]{:S(2)}) %collective-permute-start.10) | collective-permute-done | bytes 1114144 | tf_op jit(solution)/shard_map/ppermute | solution.py:392
  96.7 0.7 collective-permute-start.17
  97.4 3.8 %collective-permute-start.16 = (bf16[256,1024]{1,0:T(8,128)(2,1)S(1)}, bf16[256,1024]{1,0:T(8,128)(2,1)S(1)}, u32[]{:S(2)}, u32[]{:S(2)}) collective-permute-start(bf16[256,1024]{1,0:T(8,128)(2,1)S(1)} %get-tuple-element.142.refs_0_), channel_id=1, source_target_pairs={{0,4},{12,8},{1,5},{13,9},{2,6},{14,10},{3,7},{15,11},{16,20},{28,... | collective-permute-start | bytes 1572872 | tf_op jit(solution)/shard_map/ppermute | solution.py:392
  101.3 6.6 %collective-permute-done.13.refs_10_ = bf16[256,1024]{1,0:T(8,128)(2,1)S(1)} collective-permute-done((bf16[256,1024]{1,0:T(8,128)(2,1)S(1)}, bf16[256,1024]{1,0:T(8,128)(2,1)S(1)}, u32[]{:S(2)}, u32[]{:S(2)}) %collective-permute-start.13) | collective-permute-done | bytes 524320 | tf_op jit(solution)/shard_map/ppermute | solution.py:392
  108.0 1.2 %collective-permute-done.14 = bf16[256,128]{1,0:T(8,128)(2,1)S(1)} collective-permute-done((bf16[256,128]{1,0:T(8,128)(2,1)S(1)}, bf16[256,128]{1,0:T(8,128)(2,1)S(1)}, u32[]{:S(2)}, u32[]{:S(2)}) %collective-permute-start.14) | collective-permute-done | bytes 65568 | tf_op jit(solution)/shard_map/ppermute | solution.py:383
  109.6 4.0 %collective-permute-done.15 = bf16[256,128]{1,0:T(8,128)(2,1)S(1)} collective-permute-done((bf16[256,128]{1,0:T(8,128)(2,1)S(1)}, bf16[256,128]{1,0:T(8,128)(2,1)S(1)}, u32[]{:S(2)}, u32[]{:S(2)}) %collective-permute-start.15) | collective-permute-done | bytes 65568 | tf_op jit(solution)/shard_map/ppermute | solution.py:383
  113.6 1.8 %finish.1.total = bf16[256,2048]{1,0:T(8,128)(2,1)S(1)} custom-call(s32[38]{0:T(128)S(1)} %copy-done.4, s32[8,128]{1,0:T(8,128)S(1)} %bitcast.16, bf16[256,128]{1,0:T(8,128)(2,1)S(1)} %add.56.refs_2_, bf16[288,1024]{1,0:T(8,128)(2,1)S(1)} %get-tuple-element.135.refs_3_, bf16[256,1024]{1,0:T(8,128)(2,1)S(1)} %get-tuple-element.140.refs_4_, ...), custom_call_target="tpu_custom_call" | custom-call | flops 1000000 | bytes 100000 | tf_op jit(solution)/shard_map/finish/pallas_call | solution.py:322
  115.4 1.3 %add_last.1 = bf16[256,2048]{1,0:T(8,128)(2,1)} custom-call(bf16[256,2048]{1,0:T(8,128)(2,1)S(1)} %finish.1.total, bf16[256,1024]{1,0:T(8,128)(2,1)S(1)} %collective-permute-done.16.refs_0_, bf16[256,1024]{1,0:T(8,128)(2,1)S(1)} %collective-permute-done.17.refs_1_, bf16[256,1024]{1,0:T(8,128)(2,1)S(1)} %collective-permute-done.18.refs_2_), custom_call_target="tpu_custom_call" | custom-call | flops 1000000 | bytes 100000 | tf_op jit(solution)/shard_map/add_last/pallas_call | solution.py:371
  (37 shorter events, 1.6 us)
Async XLA Ops:
  0.8 1.6 %copy-start.1 = (bf16[4,32,8192]{2,1,0:T(8,128)(2,1)S(1)}, bf16[4,32,8192]{2,1,0:T(8,128)(2,1)}, u32[]{:S(2)}) copy-start(bf16[4,32,8192]{2,1,0:T(8,128)(2,1)} %refs_1_.3) | copy-start | bytes 6291460
  2.4 1.4 %copy-start.3 = (s32[38]{0:T(128)}, s32[38]{0:T(128)S(1)}, u32[]{:S(2)}) copy-start(s32[38]{0:T(128)S(1)} %concatenate.3.refs_0_) | copy-start | bytes 460
  3.2 14.4 %collective-permute-start = (bf16[2,256,1024]{2,1,0:T(8,128)(2,1)S(1)}, bf16[2,256,1024]{2,1,0:T(8,128)(2,1)}, u32[]{:S(2)}, u32[]{:S(2)}) collective-permute-start(bf16[2,256,1024]{2,1,0:T(8,128)(2,1)S(1)} %get-tuple-element.75), channel_id=1, source_target_pairs={{0,1},{1,0},{2,3},{3,2},{4,5},{5,4},{6,7},{7,6},{8,9},{9,8},{10,11... | collective-permute-start | bytes 3145736 | tf_op jit(solution)/shard_map/ppermute | solution.py:383
  13.0 20.4 %collective-permute-start.1 = (bf16[288,1024]{1,0:T(8,128)(2,1)}, bf16[288,1024]{1,0:T(8,128)(2,1)S(1)}, u32[]{:S(2)}, u32[]{:S(2)}) collective-permute-start(bf16[288,1024]{1,0:T(8,128)(2,1)} %base_terms.4.refs_0_), channel_id=1, source_target_pairs={{0,4},{12,8},{1,5},{13,9},{2,6},{14,10},{3,7},{15,11},{16,20},{28,... | collective-permute-start | bytes 1769480 | tf_op jit(solution)/shard_map/ppermute | solution.py:392
  17.6 2.9 %copy-start.4 = (s32[38]{0:T(128)S(1)}, s32[38]{0:T(128)}, u32[]{:S(2)}) copy-start(s32[38]{0:T(128)} %copy-done.3) | copy-start | bytes 460
  18.9 15.4 %collective-permute-start.2 = (bf16[256,1024]{1,0:T(8,128)(2,1)S(1)}, bf16[256,1024]{1,0:T(8,128)(2,1)S(1)}, u32[]{:S(2)}, u32[]{:S(2)}) collective-permute-start(bf16[256,1024]{1,0:T(8,128)(2,1)S(1)} %get-tuple-element.144), channel_id=1, source_target_pairs={{0,2},{1,3},{2,0},{3,1},{4,6},{5,7},{6,4},{7,5},{8,10},{9,11},{10,... | collective-permute-start | bytes 1572872 | tf_op jit(solution)/shard_map/ppermute | solution.py:383
  20.5 12.9 %copy-start = (bf16[288,1024]{1,0:T(8,128)(2,1)S(1)}, bf16[288,1024]{1,0:T(8,128)(2,1)}, u32[]{:S(2)}) copy-start(bf16[288,1024]{1,0:T(8,128)(2,1)} %base_terms.4.refs_0_) | copy-start | bytes 1769476
  32.1 30.7 %collective-permute-start.3 = (bf16[256,1024]{1,0:T(8,128)(2,1)S(1)}, bf16[256,1024]{1,0:T(8,128)(2,1)S(1)}, u32[]{:S(2)}, u32[]{:S(2)}) collective-permute-start(bf16[256,1024]{1,0:T(8,128)(2,1)S(1)} %get-tuple-element.97.refs_0_), channel_id=1, source_target_pairs={{0,4},{12,8},{1,5},{13,9},{2,6},{14,10},{3,7},{15,11},{16,20},{28,... | collective-permute-start | bytes 1572872 | tf_op jit(solution)/shard_map/ppermute | solution.py:392
  33.6 6.3 %copy-start.2 = (s32[1024]{0:T(1024)S(1)}, s32[1024]{0:T(1024)}, u32[]{:S(2)}) copy-start(s32[1024]{0:T(1024)} %param.12) | copy-start | bytes 12292
  33.6 32.8 %collective-permute-start.5 = (bf16[288,1024]{1,0:T(8,128)(2,1)S(1)}, bf16[288,1024]{1,0:T(8,128)(2,1)S(1)}, u32[]{:S(2)}, u32[]{:S(2)}) collective-permute-start(bf16[288,1024]{1,0:T(8,128)(2,1)S(1)} %join.6), channel_id=1, source_target_pairs={{4,8},{8,4},{5,9},{9,5},{6,10},{10,6},{7,11},{11,7},{20,24},{24,20... | collective-permute-start | bytes 1769480 | tf_op jit(solution)/shard_map/ppermute | solution.py:392
  34.5 31.9 %collective-permute-start.6 = (bf16[256,1024]{1,0:T(8,128)(2,1)S(1)}, bf16[256,1024]{1,0:T(8,128)(2,1)S(1)}, u32[]{:S(2)}, u32[]{:S(2)}) collective-permute-start(bf16[256,1024]{1,0:T(8,128)(2,1)S(1)} %add.51.refs_5_), channel_id=1, source_target_pairs={{4,8},{8,4},{5,9},{9,5},{6,10},{10,6},{7,11},{11,7},{20,24},{24,20... | collective-permute-start | bytes 1572872 | tf_op jit(solution)/shard_map/ppermute | solution.py:392
  35.2 29.7 %collective-permute-start.4 = (bf16[256,1024]{1,0:T(8,128)(2,1)S(1)}, bf16[256,1024]{1,0:T(8,128)(2,1)S(1)}, u32[]{:S(2)}, u32[]{:S(2)}) collective-permute-start(bf16[256,1024]{1,0:T(8,128)(2,1)S(1)} %add.51.refs_5_), channel_id=1, source_target_pairs={{0,4},{12,8},{4,0},{8,12},{1,5},{13,9},{5,1},{9,13},{2,6},{14,10},... | collective-permute-start | bytes 1572872 | tf_op jit(solution)/shard_map/ppermute | solution.py:433
  62.8 25.1 %collective-permute-start.7 = (bf16[544,1024]{1,0:T(8,128)(2,1)S(1)}, bf16[544,1024]{1,0:T(8,128)(2,1)S(1)}, u32[]{:S(2)}, u32[]{:S(2)}) collective-permute-start(bf16[544,1024]{1,0:T(8,128)(2,1)S(1)} %get-tuple-element.126.refs_0_), channel_id=1, source_target_pairs={{0,4},{12,8},{1,5},{13,9},{2,6},{14,10},{3,7},{15,11},{16,20},{28,... | collective-permute-start | bytes 3342344 | tf_op jit(solution)/shard_map/ppermute | solution.py:392
  65.0 23.7 %collective-permute-start.8 = (bf16[256,1024]{1,0:T(8,128)(2,1)S(1)}, bf16[256,1024]{1,0:T(8,128)(2,1)S(1)}, u32[]{:S(2)}, u32[]{:S(2)}) collective-permute-start(bf16[256,1024]{1,0:T(8,128)(2,1)S(1)} %collective-permute-done.4.refs_6_), channel_id=1, source_target_pairs={{4,8},{8,4},{5,9},{9,5},{6,10},{10,6},{7,11},{11,7},{20,24},{24,20... | collective-permute-start | bytes 1572872 | tf_op jit(solution)/shard_map/ppermute | solution.py:392
  65.7 23.1 %collective-permute-start.9 = (bf16[256,1024]{1,0:T(8,128)(2,1)S(1)}, bf16[256,1024]{1,0:T(8,128)(2,1)S(1)}, u32[]{:S(2)}, u32[]{:S(2)}) collective-permute-start(bf16[256,1024]{1,0:T(8,128)(2,1)S(1)} %join.7), channel_id=1, source_target_pairs={{4,8},{8,4},{5,9},{9,5},{6,10},{10,6},{7,11},{11,7},{20,24},{24,20... | collective-permute-start | bytes 1572872 | tf_op jit(solution)/shard_map/ppermute | solution.py:392
  66.5 30.0 %collective-permute-start.10 = (bf16[544,1024]{1,0:T(8,128)(2,1)S(1)}, bf16[544,1024]{1,0:T(8,128)(2,1)S(1)}, u32[]{:S(2)}, u32[]{:S(2)}) collective-permute-start(bf16[544,1024]{1,0:T(8,128)(2,1)S(1)} %join.8), channel_id=1, source_target_pairs={{8,12},{4,0},{9,13},{5,1},{10,14},{6,2},{11,15},{7,3},{24,28},{20,... | collective-permute-start | bytes 3342344 | tf_op jit(solution)/shard_map/ppermute | solution.py:392
  79.5 18.0 %collective-permute-start.11 = (bf16[288,1024]{1,0:T(8,128)(2,1)S(1)}, bf16[288,1024]{1,0:T(8,128)(2,1)S(1)}, u32[]{:S(2)}, u32[]{:S(2)}) collective-permute-start(bf16[288,1024]{1,0:T(8,128)(2,1)S(1)} %get-tuple-element.129.refs_0_), channel_id=1, source_target_pairs={{0,4},{12,8},{1,5},{13,9},{2,6},{14,10},{3,7},{15,11},{16,20},{28,... | collective-permute-start | bytes 1769480 | tf_op jit(solution)/shard_map/ppermute | solution.py:392
  88.0 13.3 %collective-permute-start.12 = (bf16[288,1024]{1,0:T(8,128)(2,1)S(1)}, bf16[288,1024]{1,0:T(8,128)(2,1)S(1)}, u32[]{:S(2)}, u32[]{:S(2)}) collective-permute-start(bf16[288,1024]{1,0:T(8,128)(2,1)S(1)} %join.9), channel_id=1, source_target_pairs={{4,8},{8,4},{5,9},{9,5},{6,10},{10,6},{7,11},{11,7},{20,24},{24,20... | collective-permute-start | bytes 1769480 | tf_op jit(solution)/shard_map/ppermute | solution.py:392
  88.7 19.1 %collective-permute-start.13 = (bf16[256,1024]{1,0:T(8,128)(2,1)S(1)}, bf16[256,1024]{1,0:T(8,128)(2,1)S(1)}, u32[]{:S(2)}, u32[]{:S(2)}) collective-permute-start(bf16[256,1024]{1,0:T(8,128)(2,1)S(1)} %collective-permute-done.8.refs_8_), channel_id=1, source_target_pairs={{8,12},{4,0},{9,13},{5,1},{10,14},{6,2},{11,15},{7,3},{24,28},{20,... | collective-permute-start | bytes 1572872 | tf_op jit(solution)/shard_map/ppermute | solution.py:392
  90.2 25.2 %collective-permute-start.18 = (bf16[256,1024]{1,0:T(8,128)(2,1)S(1)}, bf16[256,1024]{1,0:T(8,128)(2,1)S(1)}, u32[]{:S(2)}, u32[]{:S(2)}) collective-permute-start(bf16[256,1024]{1,0:T(8,128)(2,1)S(1)} %join.10), channel_id=1, source_target_pairs={{8,12},{4,0},{9,13},{5,1},{10,14},{6,2},{11,15},{7,3},{24,28},{20,... | collective-permute-start | bytes 1572872 | tf_op jit(solution)/shard_map/ppermute | solution.py:392
  96.7 18.7 %collective-permute-start.17 = (bf16[256,1024]{1,0:T(8,128)(2,1)S(1)}, bf16[256,1024]{1,0:T(8,128)(2,1)S(1)}, u32[]{:S(2)}, u32[]{:S(2)}) collective-permute-start(bf16[256,1024]{1,0:T(8,128)(2,1)S(1)} %join.11), channel_id=1, source_target_pairs={{4,8},{8,4},{5,9},{9,5},{6,10},{10,6},{7,11},{11,7},{20,24},{24,20... | collective-permute-start | bytes 1572872 | tf_op jit(solution)/shard_map/ppermute | solution.py:392
  97.4 18.0 %collective-permute-start.16 = (bf16[256,1024]{1,0:T(8,128)(2,1)S(1)}, bf16[256,1024]{1,0:T(8,128)(2,1)S(1)}, u32[]{:S(2)}, u32[]{:S(2)}) collective-permute-start(bf16[256,1024]{1,0:T(8,128)(2,1)S(1)} %get-tuple-element.142.refs_0_), channel_id=1, source_target_pairs={{0,4},{12,8},{1,5},{13,9},{2,6},{14,10},{3,7},{15,11},{16,20},{28,... | collective-permute-start | bytes 1572872 | tf_op jit(solution)/shard_map/ppermute | solution.py:392
  107.9 1.3 %collective-permute-start.14 = (bf16[256,128]{1,0:T(8,128)(2,1)S(1)}, bf16[256,128]{1,0:T(8,128)(2,1)S(1)}, u32[]{:S(2)}, u32[]{:S(2)}) collective-permute-start(bf16[256,128]{1,0:T(8,128)(2,1)S(1)} %bitcast.17), channel_id=1, source_target_pairs={{0,1},{1,0},{2,3},{3,2},{4,5},{5,4},{6,7},{7,6},{8,9},{9,8},{10,11... | collective-permute-start | bytes 196616 | tf_op jit(solution)/shard_map/ppermute | solution.py:383
  109.2 4.3 %collective-permute-start.15 = (bf16[256,128]{1,0:T(8,128)(2,1)S(1)}, bf16[256,128]{1,0:T(8,128)(2,1)S(1)}, u32[]{:S(2)}, u32[]{:S(2)}) collective-permute-start(bf16[256,128]{1,0:T(8,128)(2,1)S(1)} %bitcast_add_fusion), channel_id=1, source_target_pairs={{0,2},{1,3},{2,0},{3,1},{4,6},{5,7},{6,4},{7,5},{8,10},{9,11},{10,... | collective-permute-start | bytes 196616 | tf_op jit(solution)/shard_map/ppermute | solution.py:383

commit v2 on v1

--- a/solution.py
+++ b/solution.py
@@ -71,9 +71,8 @@
         return self.ref[2 + self.requests + self.adapters + self.adapter(r)] - self.shard * held
 
 
-def base_kernel(order, groups, half, held, request_count, piece, handed_on, *refs):
+def base_kernel(order, groups, inputs_for, half, held, request_count, handed_on, *refs):
     slots = [slot for group in groups for slot in group]
-    places = [(g, i) for g, group in enumerate(groups) for i in range(len(group))]
     count = len(slots)
     meta, refs = Meta(refs[0], request_count), refs[1:]
     if held:
@@ -99,7 +98,7 @@
         return [pltpu.make_async_copy(a, b, sems.at[k, i]) for i, (a, b) in enumerate(moves)]
 
     if held:
-        factors, inputs, factor_sems = refs
+        factors, inputs, flags, factor_sems = refs
         width = factor.shape[2]
 
         def factor_copies(k, pair):
@@ -126,23 +125,24 @@
 
     for k in range(min(AHEAD, steps)):
         start(k)
-    used, blocks_using = [], []
+    used = []
     if held:
         bounds = spans(requests_ref, request_count)
         local = [meta.local_slot(r, held) for r in range(request_count)]
+        top = slots.index(inputs_for[0])
+        wide = len(inputs_for)
         for pair in range(held // 2):
             used_by = []
-            for first in first_rows:
+            for first in first_rows[top : top + wide]:
                 wanted = jnp.bool_(False)
                 for r, slot in enumerate(local):
                     here = jnp.maximum(bounds[r], first) < jnp.minimum(bounds[r + 1], first + block)
                     wanted = wanted | (here & (slot // 2 == pair) & (slot >= 0))
+                flags[pair * wide + len(used_by)] = wanted.astype(jnp.int32)
                 used_by.append(wanted)
-            blocks_using.append(used_by)
             used.append(functools.reduce(jnp.logical_or, used_by))
         for k in range(min(AHEAD, steps)):
             start_factors(k, used)
-        inputs[...] = jnp.zeros_like(inputs)
     sums[...] = jnp.zeros_like(sums)
 
     def step(k, _):
@@ -154,48 +154,63 @@
         for copy in copies(k):
             copy.wait()
         sums[...] += jnp.dot(rows[k], right[k], preferred_element_type=jnp.float32)
+        return 0
+
+    lax.fori_loop(0, steps, step, 0)
+
+    if held:
         for pair, wanted in enumerate(used):
 
             @pl.when(wanted)
             def _(pair=pair):
-                for copy in factor_copies(k, pair):
-                    copy.wait()
-
-            for i, wanted_here in enumerate(blocks_using[pair]):
-
-                @pl.when(wanted_here)
-                def _(pair=pair, own=pl.ds(i * block, block)):
-                    inputs[pair, own, :] += jnp.dot(
-                        rows[k, own, :], factors[pair, k], preferred_element_type=jnp.float32
-                    )
-
-        return 0
-
-    lax.fori_loop(0, steps, step, 0)
+                for k in range(steps):
+                    for copy in factor_copies(k, pair):
+                        copy.wait()
+
+        def pair_block(j, _):
+            pair, i = j // wide, j % wide
+
+            @pl.when(flags[j] == 1)
+            def _():
+                own = pl.ds(pl.multiple_of((top + i) * block, block), block)
+                total = jnp.dot(rows[0, own, :], factors[pair, 0], preferred_element_type=jnp.float32)
+                for k in range(1, steps):
+                    total += jnp.dot(rows[k, own, :], factors[pair, k], preferred_element_type=jnp.float32)
+                inputs[pair, pl.ds(pl.multiple_of(i * block, block), block), :] = total
+
+            return 0
+
+        lax.fori_loop(0, held // 2 * wide, pair_block, 0)
+
+    i = 0
+    for out, group in zip(outs, groups):
+        here = 0
+        for slot in group:
+            out[here : here + block, :] = sums[i * block : (i + 1) * block, :].astype(jnp.bfloat16)
+            here += block
+            if held and slot in inputs_for:
+                own = pl.ds((i - top) * block, block)
+                row = lax.broadcasted_iota(jnp.int32, (block, width), 0) + first_rows[i]
+                column = lax.broadcasted_iota(jnp.int32, (block, width), 1)
+                total = jnp.zeros((block, width), jnp.float32)
+                for r, local_slot in enumerate(local):
+                    last = jnp.where((local_slot >= 0) & (local_slot < held), bounds[r + 1], 0)
+                    keep = (row >= bounds[r]) & (row < last) & (column < meta.rank(r))
+                    local_slot = jnp.clip(local_slot, 0, held - 1)
+                    lanes = pl.ds(pl.multiple_of(local_slot % 2 * width, width), width)
+                    total = jnp.where(keep, inputs[local_slot // 2, own, lanes], total)
+                total = total.astype(jnp.bfloat16)
+                size = block * width // columns
+                for j in range(columns // width):
+                    lanes = slice(j * width, (j + 1) * width)
+                    out[here : here + size, lanes] = total[j * size : (j + 1) * size, :]
+                here += size
+            i += 1
     if handed_on:
-        outs[0][len(groups[0]) * piece :, :] = under[...]
-    for i, (group, position) in enumerate(places):
-        own = pl.ds(i * block, block)
-        out, top = outs[group], position * piece
-        out[top : top + block, :] = sums[own, :].astype(jnp.bfloat16)
-        if held:
-            row = lax.broadcasted_iota(jnp.int32, (block, width), 0) + first_rows[i]
-            column = lax.broadcasted_iota(jnp.int32, (block, width), 1)
-            total = jnp.zeros((block, width), jnp.float32)
-            for r, slot in enumerate(local):
-                last = jnp.where((slot >= 0) & (slot < held), bounds[r + 1], 0)
-                keep = (row >= bounds[r]) & (row < last) & (column < meta.rank(r))
-                slot = jnp.clip(slot, 0, held - 1)
-                lanes = pl.ds(pl.multiple_of(slot % 2 * width, width), width)
-                total = jnp.where(keep, inputs[slot // 2, own, lanes], total)
-            total = total.astype(jnp.bfloat16)
-            size = block * width // columns
-            for j in range(columns // width):
-                lanes = slice(j * width, (j + 1) * width)
-                out[top + block : top + block + size, lanes] = total[j * size : (j + 1) * size, :]
-
-
-def base_terms(meta, requests, request_count, hidden, matrix, factor, groups, half, n, grant, under=None):
+        outs[0][outs[0].shape[0] - under.shape[0] :, :] = under[...]
+
+
+def base_terms(meta, requests, request_count, hidden, matrix, factor, groups, inputs_for, half, n, under=None):
     tokens, depth = hidden.shape
     block, columns = tokens // n, matrix.shape[1] // 2
     tile = first_divisor(depth, (1024, 512, 256, 128))
@@ -204,7 +219,7 @@
     smem = pl.BlockSpec(memory_space=pltpu.SMEM)
     vmem = pl.BlockSpec(memory_space=pltpu.VMEM)
     hbm = pl.BlockSpec(memory_space=pltpu.HBM)
-    held, out_rows = 0, block
+    held, extra = 0, 0
     operands, in_specs = [meta], [smem]
     scratch = [
         pltpu.VMEM((steps, count * block, tile), jnp.bfloat16),
@@ -212,28 +227,29 @@
         pltpu.VMEM((count * block, columns), jnp.float32),
         pltpu.SemaphoreType.DMA((steps, count + 1)),
     ]
-    if factor is not None:
+    if inputs_for:
         held, _, width = factor.shape
-        out_rows += block * width // columns
+        extra = block * width // columns
         operands, in_specs = [meta, requests, factor], [smem, vmem, hbm]
         scratch += [
             pltpu.VMEM((held // 2, steps, tile, 2 * width), jnp.bfloat16),
-            pltpu.VMEM((held // 2, count * block, 2 * width), jnp.float32),
+            pltpu.VMEM((held // 2, len(inputs_for) * block, 2 * width), jnp.float32),
+            pltpu.SMEM((held // 2 * len(inputs_for),), jnp.int32),
             pltpu.SemaphoreType.DMA((steps, held)),
         ]
-    heights = [len(group) * out_rows for group in groups]
+    heights = [sum(block + (extra if slot in inputs_for else 0) for slot in group) for group in groups]
     operands, in_specs = operands + [hidden, matrix], in_specs + [hbm, hbm]
     if under is not None:
         heights[0] += under.shape[0]
         operands, in_specs = operands + [under], in_specs + [vmem]
     handed_on = under is not None
     return pl.pallas_call(
-        lambda *refs: base_kernel(line_order(n), groups, half, held, request_count, out_rows, handed_on, *refs),
+        lambda *refs: base_kernel(line_order(n), groups, inputs_for, half, held, request_count, handed_on, *refs),
         out_shape=[jax.ShapeDtypeStruct((height, columns), jnp.bfloat16) for height in heights],
         in_specs=in_specs,
         out_specs=[vmem] * len(groups),
         scratch_shapes=scratch,
-        compiler_params=params(grant),
+        compiler_params=params(50 if half or count > 1 else 58),
         cost_estimate=small_cost(),
         name="base_terms",
     )(*operands)
@@ -400,26 +416,28 @@
     piece = block + block * width // (matrix.shape[1] // 2)
     bundle = 2 * request_count * rank_rows
 
-    def base(token, groups, half, grant, under=None):
-        factor = input_factor if half == 0 else None
-        return base_terms(token, requests, request_count, hidden, matrix, factor, groups, half, n, grant, under)
+    def base(token, groups, inputs_for, half, under=None):
+        return base_terms(
+            token, requests, request_count, hidden, matrix, input_factor, groups, inputs_for, half, n, under
+        )
 
     def send(x, edge, token):
         return along_edge(after(x, token), edge)
 
+    (s00,) = base(token, [[0]], [0], 0)
+    token = after(token, s00)
+    e0_1 = along_edge(s00, 0)
     kept, sent = select_rows(token, request_count, output_factor)
     token = after(token, kept, sent)
     swapped = swap(sent, "store", 1)
-    (s00,) = base(token, [[0]], 0, 58)
-    token = after(token, s00, swapped)
-    e0_1 = along_edge(s00, 0)
+    token = after(token, swapped)
     side = shard // 2 % 2
     kept, swapped, _ = lax.optimization_barrier((kept, swapped, token))
     outgoing = kept[1 - side] + swapped[1 - side]
     rows = kept[side] + swapped[side]
     token = after(token, outgoing, rows)
     swapped = swap(outgoing, "store", 2)
-    s01, s11 = base(token, [[0], [1]], 1, 50)
+    s01, s11 = base(token, [[0], [1]], [], 1)
 
     token = after(token, s01)
     e0_2 = send(s01, 0, token)
@@ -432,7 +450,7 @@
     token = after(token, rows)
     near = lax.ppermute(rows, "tensor", [(0, 1), (n - 1, n - 2), (1, 0), (n - 2, n - 1)])
     far = along_edge(rows, 1)
-    s10_s11, s20, s30 = base(token, [[1], [2], [3]], 0, 50, s11)
+    s10_s11, s20, s30 = base(token, [[1], [2], [3]], [1, 2], 0, s11)
 
     token = after(token, s10_s11)
     e0_3 = send(s10_s11, 0, token)
@@ -445,7 +463,7 @@
     c20 = join(token, piece, s20, 0, e1_2, 0, far, 0, bundle)
     token = after(token, c20)
     e2_3 = along_edge(c20, 2)
-    s21, s31 = base(token, [[2], [3]], 1, 50)
+    s21, s31 = base(token, [[2], [3]], [3], 1)
 
     token = after(token, s21)
     e0_4 = send(s20, 0, token)
@@ -469,7 +487,7 @@
     token, e1_4 = lax.optimization_barrier((token, e1_4))
     token, last_rows = lax.optimization_barrier((token, last_rows))
     e1_4 = after(e1_4, token)
-    lora = s30[block:].astype(jnp.float32) + e0_4[block:].astype(jnp.float32)
+    lora = s31[block:].astype(jnp.float32) + e0_4[block:].astype(jnp.float32)
     lora += e1_4[block:].astype(jnp.float32) + e2_3[block:piece].astype(jnp.float32)
     lora = lora.astype(jnp.bfloat16).reshape(piece - block, -1, width).swapaxes(0, 1).reshape(block, width)
     lora = lora + swap(lora, "store", 1)

time: 118 us -> 117 us (level); the launches traced: 117 us -> 117 us
  starting transfers between devices: 32.7 us -> 34.8 us
  Pallas kernels: 60.1 us -> 58.4 us
    ppermute x14, starting transfers between devices: 25.5 us -> 28.7 us  [along_edge(): lax.ppermute(x, 'tensor', [(edge, edge + 1), (n - 1 - edge, n - 2 - edge)])]
    pallas_call x4, Pallas kernels: 55.4 us -> 53.7 us  [base_terms(): pl.pallas_call(lambda *refs: base_kernel(line_order(n), groups, inputs_fo...]
    unnamed x11 -> x9, local copies, waits for them, and re-layouts: 1.62 us -> 0.17 us
  transfers between devices with their start and end apart: 19 -> 19, of which waited for: 5 -> 6; matrix products, arithmetic and copies ran while one was open for 1% -> 1% of each run, Pallas kernels for 50% -> 38%
where the time goes in v2:
time: 117 us
  Pallas kernels  58.4 us (50%)
  starting transfers between devices  34.8 us (30%)
  waiting for transfers between devices  20.3 us (17%)
  other arithmetic  1.58 us (1%)
  local copies, waits for them, and re-layouts  1.53 us (1%)
    pallas_call x4, Pallas kernels, base_terms(): pl.pallas_call(lambda *refs: base_kernel(line_order(n), groups, inputs_fo...  53.7 us
    ppermute x14, starting transfers between devices, along_edge(): lax.ppermute(x, 'tensor', [(edge, edge + 1), (n - 1 - edge, n - 2 - edge)])  28.7 us
    ppermute x14, waiting for transfers between devices, along_edge(): lax.ppermute(x, 'tensor', [(edge, edge + 1), (n - 1 - edge, n - 2 - edge)])  14.8 us
    ppermute x4, waiting for transfers between devices, swap(): lax.ppermute(x, axis, [(i, i ^ bit) for i in range(lax.axis_size(axis))])  5.5 us
    ppermute x1, starting transfers between devices, on_line(): lax.ppermute(rows, 'tensor', [(0, 1), (n - 1, n - 2), (1, 0), (n - 2, n -...  4.56 us
  transfers between devices with their start and end apart: 19, of which 6 were waited for; matrix products, arithmetic and copies ran while one was open for 1% of the time, Pallas kernels for 38%

profile of v2, /device:TPU:0, one launch (start us, length us, event | category | flops | bytes accessed | tf_op | source)
XLA Modules:
  0.0 117.0 jit_solution(172038925993016537)
XLA Ops:
  0.0 1.3 %concatenate.3.refs_0_ = s32[38]{0:T(128)} concatenate(s32[1]{0:T(128)} %bitcast, s32[1]{0:T(128)} %bitcast.1, s32[4]{0:T(128)} %param.13, s32[16]{0:T(128)} %param.14, s32[16]{0:T(128)} %param.15), dimensions={0} | concatenate | bytes 304 | tf_op jit(solution)/shard_map/concatenate | solution.py:547
  1.3 11.5 %base_terms.4.refs_0_ = bf16[288,1024]{1,0:T(8,128)(2,1)} custom-call(s32[38]{0:T(128)} %concatenate.3.refs_0_, s32[8,128]{1,0:T(8,128)} %bitcast.14, bf16[4,7168,128]{2,1,0:T(8,128)(2,1)} %refs_2_.7, bf16[1024,7168]{1,0:T(8,128)(2,1)} %refs_3_.5, bf16[7168,2048]{1,0:T(8,128)(2,1)} %refs_4_.5), custom_call_target="tpu_custom_call" | custom-call | flops 1000000 | bytes 100000 | tf_op jit(solution)/shard_map/base_terms/pallas_call | solution.py:246
  12.9 0.8 select_rows.1
  14.0 5.0 %collective-permute-start.1 = (bf16[288,1024]{1,0:T(8,128)(2,1)S(1)}, bf16[288,1024]{1,0:T(8,128)(2,1)S(1)}, u32[]{:S(2)}, u32[]{:S(2)}) collective-permute-start(bf16[288,1024]{1,0:T(8,128)(2,1)S(1)} %copy-done), channel_id=1, source_target_pairs={{0,4},{12,8},{1,5},{13,9},{2,6},{14,10},{3,7},{15,11},{16,20},{28,... | collective-permute-start | bytes 1769480 | tf_op jit(solution)/shard_map/ppermute | solution.py:408
  19.0 1.3 %add_bitcast_fusion = (bf16[256,1024]{1,0:T(8,128)(2,1)S(1)}, bf16[256,1024]{1,0:T(8,128)(2,1)S(1)}) fusion(bf16[2,256,1024]{2,1,0:T(8,128)(2,1)} %collective-permute-done, s32[]{:T(128)S(6)} %select_n.22, bf16[2,256,1024]{2,1,0:T(8,128)(2,1)S(1)} %get-tuple-element.80, s32[]{:T(128)S(6)} %select_n.21), kind=kLoop, calls=%fused_computation | loop fusion | flops 524288 | bytes 3145736 | tf_op jit(solution)/shard_map/add | solution.py:437
  20.3 1.3 %collective-permute-start.2 = (bf16[256,1024]{1,0:T(8,128)(2,1)S(1)}, bf16[256,1024]{1,0:T(8,128)(2,1)S(1)}, u32[]{:S(2)}, u32[]{:S(2)}) collective-permute-start(bf16[256,1024]{1,0:T(8,128)(2,1)S(1)} %get-tuple-element.146), channel_id=1, source_target_pairs={{0,2},{1,3},{2,0},{3,1},{4,6},{5,7},{6,4},{7,5},{8,10},{9,11},{10,... | collective-permute-start | bytes 1572872 | tf_op jit(solution)/shard_map/ppermute | solution.py:399
  21.6 11.6 %base_terms.5 = (bf16[256,1024]{1,0:T(8,128)(2,1)S(1)}, bf16[256,1024]{1,0:T(8,128)(2,1)S(1)}) custom-call(s32[38]{0:T(128)S(1)} %copy-done.3, bf16[1024,7168]{1,0:T(8,128)(2,1)} %refs_3_.5, bf16[7168,2048]{1,0:T(8,128)(2,1)} %refs_4_.5), custom_call_target="tpu_custom_call" | custom-call | flops 1000000 | bytes 100000 | tf_op jit(solution)/shard_map/base_terms/pallas_call | solution.py:246
  33.2 2.4 %collective-permute-start.3 = (bf16[256,1024]{1,0:T(8,128)(2,1)S(1)}, bf16[256,1024]{1,0:T(8,128)(2,1)S(1)}, u32[]{:S(2)}, u32[]{:S(2)}) collective-permute-start(bf16[256,1024]{1,0:T(8,128)(2,1)S(1)} %get-tuple-element.99.refs_0_), channel_id=1, source_target_pairs={{0,4},{12,8},{1,5},{13,9},{2,6},{14,10},{3,7},{15,11},{16,20},{28,... | collective-permute-start | bytes 1572872 | tf_op jit(solution)/shard_map/ppermute | solution.py:408
  35.8 0.7 collective-permute-start.5
  36.5 0.2 add.51.refs_5_
  36.7 0.7 collective-permute-start.6
  37.4 4.6 %collective-permute-start.4 = (bf16[256,1024]{1,0:T(8,128)(2,1)S(1)}, bf16[256,1024]{1,0:T(8,128)(2,1)S(1)}, u32[]{:S(2)}, u32[]{:S(2)}) collective-permute-start(bf16[256,1024]{1,0:T(8,128)(2,1)S(1)} %add.51.refs_5_), channel_id=1, source_target_pairs={{0,4},{12,8},{4,0},{8,12},{1,5},{13,9},{5,1},{9,13},{2,6},{14,10},... | collective-permute-start | bytes 1572872 | tf_op jit(solution)/shard_map/ppermute | solution.py:451
  42.0 18.5 %base_terms.6 = (bf16[544,1024]{1,0:T(8,128)(2,1)S(1)}, bf16[288,1024]{1,0:T(8,128)(2,1)S(1)}, bf16[256,1024]{1,0:T(8,128)(2,1)S(1)}) custom-call(s32[38]{0:T(128)S(1)} %copy-done.3, s32[8,128]{1,0:T(8,128)S(1)} %bitcast.15, bf16[4,7168,128]{2,1,0:T(8,128)(2,1)} %refs_2_.7, bf16[1024,7168]{1,0:T(8,128)(2,1)} %refs_3_.5, bf16[7168,2048]{1,0:T(8,128)(2,1)} %refs_4_.5, ...), custom_call_target="tpu_custom_call" | custom-call | flops 1000000 | bytes 100000 | tf_op jit(solution)/shard_map/base_terms/pallas_call | solution.py:246
  60.5 1.4 %collective-permute-start.7 = (bf16[544,1024]{1,0:T(8,128)(2,1)S(1)}, bf16[544,1024]{1,0:T(8,128)(2,1)S(1)}, u32[]{:S(2)}, u32[]{:S(2)}) collective-permute-start(bf16[544,1024]{1,0:T(8,128)(2,1)S(1)} %get-tuple-element.128.refs_0_), channel_id=1, source_target_pairs={{0,4},{12,8},{1,5},{13,9},{2,6},{14,10},{3,7},{15,11},{16,20},{28,... | collective-permute-start | bytes 3342344 | tf_op jit(solution)/shard_map/ppermute | solution.py:408
  62.0 0.7 collective-permute-start.8
  62.7 0.7 collective-permute-start.9
  63.6 1.3 %collective-permute-start.10 = (bf16[544,1024]{1,0:T(8,128)(2,1)S(1)}, bf16[544,1024]{1,0:T(8,128)(2,1)S(1)}, u32[]{:S(2)}, u32[]{:S(2)}) collective-permute-start(bf16[544,1024]{1,0:T(8,128)(2,1)S(1)} %join.8), channel_id=1, source_target_pairs={{8,12},{4,0},{9,13},{5,1},{10,14},{6,2},{11,15},{7,3},{24,28},{20,... | collective-permute-start | bytes 3342344 | tf_op jit(solution)/shard_map/ppermute | solution.py:408
  64.9 12.1 %base_terms.7 = (bf16[256,1024]{1,0:T(8,128)(2,1)S(1)}, bf16[288,1024]{1,0:T(8,128)(2,1)S(1)}) custom-call(s32[38]{0:T(128)S(1)} %copy-done.3, s32[8,128]{1,0:T(8,128)S(1)} %bitcast.16, bf16[4,7168,128]{2,1,0:T(8,128)(2,1)} %refs_2_.7, bf16[1024,7168]{1,0:T(8,128)(2,1)} %refs_3_.5, bf16[7168,2048]{1,0:T(8,128)(2,1)} %refs_4_.5), custom_call_target="tpu_custom_call" | custom-call | flops 1000000 | bytes 100000 | tf_op jit(solution)/shard_map/base_terms/pallas_call | solution.py:246
  77.0 7.6 %collective-permute-start.11 = (bf16[288,1024]{1,0:T(8,128)(2,1)S(1)}, bf16[288,1024]{1,0:T(8,128)(2,1)S(1)}, u32[]{:S(2)}, u32[]{:S(2)}) collective-permute-start(bf16[288,1024]{1,0:T(8,128)(2,1)S(1)} %get-tuple-element.131.refs_0_), channel_id=1, source_target_pairs={{0,4},{12,8},{1,5},{13,9},{2,6},{14,10},{3,7},{15,11},{16,20},{28,... | collective-permute-start | bytes 1769480 | tf_op jit(solution)/shard_map/ppermute | solution.py:408
  84.5 2.2 %collective-permute-done.7.refs_1_ = bf16[544,1024]{1,0:T(8,128)(2,1)S(1)} collective-permute-done((bf16[544,1024]{1,0:T(8,128)(2,1)S(1)}, bf16[544,1024]{1,0:T(8,128)(2,1)S(1)}, u32[]{:S(2)}, u32[]{:S(2)}) %collective-permute-start.7) | collective-permute-done | bytes 1114144 | tf_op jit(solution)/shard_map/ppermute | solution.py:408
  86.8 0.7 collective-permute-start.12
  87.5 1.3 %collective-permute-start.13 = (bf16[256,1024]{1,0:T(8,128)(2,1)S(1)}, bf16[256,1024]{1,0:T(8,128)(2,1)S(1)}, u32[]{:S(2)}, u32[]{:S(2)}) collective-permute-start(bf16[256,1024]{1,0:T(8,128)(2,1)S(1)} %collective-permute-done.8.refs_8_), channel_id=1, source_target_pairs={{8,12},{4,0},{9,13},{5,1},{10,14},{6,2},{11,15},{7,3},{24,28},{20,... | collective-permute-start | bytes 1572872 | tf_op jit(solution)/shard_map/ppermute | solution.py:408
  89.0 1.3 %collective-permute-start.18 = (bf16[256,1024]{1,0:T(8,128)(2,1)S(1)}, bf16[256,1024]{1,0:T(8,128)(2,1)S(1)}, u32[]{:S(2)}, u32[]{:S(2)}) collective-permute-start(bf16[256,1024]{1,0:T(8,128)(2,1)S(1)} %join.10), channel_id=1, source_target_pairs={{8,12},{4,0},{9,13},{5,1},{10,14},{6,2},{11,15},{7,3},{24,28},{20,... | collective-permute-start | bytes 1572872 | tf_op jit(solution)/shard_map/ppermute | solution.py:408
  90.3 3.6 %collective-permute-done.10.refs_9_ = bf16[544,1024]{1,0:T(8,128)(2,1)S(1)} collective-permute-done((bf16[544,1024]{1,0:T(8,128)(2,1)S(1)}, bf16[544,1024]{1,0:T(8,128)(2,1)S(1)}, u32[]{:S(2)}, u32[]{:S(2)}) %collective-permute-start.10) | collective-permute-done | bytes 1114144 | tf_op jit(solution)/shard_map/ppermute | solution.py:408
  94.0 0.7 collective-permute-start.17
  94.7 3.9 %collective-permute-done.11.refs_11_ = bf16[288,1024]{1,0:T(8,128)(2,1)S(1)} collective-permute-done((bf16[288,1024]{1,0:T(8,128)(2,1)S(1)}, bf16[288,1024]{1,0:T(8,128)(2,1)S(1)}, u32[]{:S(2)}, u32[]{:S(2)}) %collective-permute-start.11) | collective-permute-done | bytes 589856 | tf_op jit(solution)/shard_map/ppermute | solution.py:408
  98.6 4.4 %collective-permute-start.16 = (bf16[256,1024]{1,0:T(8,128)(2,1)S(1)}, bf16[256,1024]{1,0:T(8,128)(2,1)S(1)}, u32[]{:S(2)}, u32[]{:S(2)}) collective-permute-start(bf16[256,1024]{1,0:T(8,128)(2,1)S(1)} %get-tuple-element.144.refs_0_), channel_id=1, source_target_pairs={{0,4},{12,8},{1,5},{13,9},{2,6},{14,10},{3,7},{15,11},{16,20},{28,... | collective-permute-start | bytes 1572872 | tf_op jit(solution)/shard_map/ppermute | solution.py:408
  103.0 5.1 %collective-permute-done.13.refs_10_ = bf16[256,1024]{1,0:T(8,128)(2,1)S(1)} collective-permute-done((bf16[256,1024]{1,0:T(8,128)(2,1)S(1)}, bf16[256,1024]{1,0:T(8,128)(2,1)S(1)}, u32[]{:S(2)}, u32[]{:S(2)}) %collective-permute-start.13) | collective-permute-done | bytes 524320 | tf_op jit(solution)/shard_map/ppermute | solution.py:408
  108.3 1.2 %collective-permute-done.14 = bf16[256,128]{1,0:T(8,128)(2,1)S(1)} collective-permute-done((bf16[256,128]{1,0:T(8,128)(2,1)S(1)}, bf16[256,128]{1,0:T(8,128)(2,1)S(1)}, u32[]{:S(2)}, u32[]{:S(2)}) %collective-permute-start.14) | collective-permute-done | bytes 65568 | tf_op jit(solution)/shard_map/ppermute | solution.py:399
  109.6 4.3 %collective-permute-done.15 = bf16[256,128]{1,0:T(8,128)(2,1)S(1)} collective-permute-done((bf16[256,128]{1,0:T(8,128)(2,1)S(1)}, bf16[256,128]{1,0:T(8,128)(2,1)S(1)}, u32[]{:S(2)}, u32[]{:S(2)}) %collective-permute-start.15) | collective-permute-done | bytes 65568 | tf_op jit(solution)/shard_map/ppermute | solution.py:399
  113.9 1.8 %finish.1.total = bf16[256,2048]{1,0:T(8,128)(2,1)S(1)} custom-call(s32[38]{0:T(128)S(1)} %copy-done.3, s32[8,128]{1,0:T(8,128)S(1)} %bitcast.17, bf16[256,128]{1,0:T(8,128)(2,1)S(1)} %add.56.refs_2_, bf16[256,1024]{1,0:T(8,128)(2,1)S(1)} %get-tuple-element.142.refs_3_, bf16[288,1024]{1,0:T(8,128)(2,1)S(1)} %get-tuple-element.137.refs_4_, ...), custom_call_target="tpu_custom_call" | custom-call | flops 1000000 | bytes 100000 | tf_op jit(solution)/shard_map/finish/pallas_call | solution.py:338
  115.7 1.3 %add_last.1 = bf16[256,2048]{1,0:T(8,128)(2,1)} custom-call(bf16[256,2048]{1,0:T(8,128)(2,1)S(1)} %finish.1.total, bf16[256,1024]{1,0:T(8,128)(2,1)S(1)} %collective-permute-done.16.refs_0_, bf16[256,1024]{1,0:T(8,128)(2,1)S(1)} %collective-permute-done.17.refs_1_, bf16[256,1024]{1,0:T(8,128)(2,1)S(1)} %collective-permute-done.18.refs_2_), custom_call_target="tpu_custom_call" | custom-call | flops 1000000 | bytes 100000 | tf_op jit(solution)/shard_map/add_last/pallas_call | solution.py:387
  (35 shorter events, 1.3 us)
Async XLA Ops:
  1.3 11.6 %copy-start.1 = (bf16[4,32,8192]{2,1,0:T(8,128)(2,1)S(1)}, bf16[4,32,8192]{2,1,0:T(8,128)(2,1)}, u32[]{:S(2)}) copy-start(bf16[4,32,8192]{2,1,0:T(8,128)(2,1)} %refs_1_.2) | copy-start | bytes 6291460
  1.3 11.6 %copy-start.3 = (s32[38]{0:T(128)S(1)}, s32[38]{0:T(128)}, u32[]{:S(2)}) copy-start(s32[38]{0:T(128)} %concatenate.3.refs_0_) | copy-start | bytes 460
  12.9 1.1 copy-start
  13.8 5.2 %collective-permute-start = (bf16[2,256,1024]{2,1,0:T(8,128)(2,1)S(1)}, bf16[2,256,1024]{2,1,0:T(8,128)(2,1)}, u32[]{:S(2)}, u32[]{:S(2)}) collective-permute-start(bf16[2,256,1024]{2,1,0:T(8,128)(2,1)S(1)} %get-tuple-element.77), channel_id=1, source_target_pairs={{0,1},{1,0},{2,3},{3,2},{4,5},{5,4},{6,7},{7,6},{8,9},{9,8},{10,11... | collective-permute-start | bytes 3145736 | tf_op jit(solution)/shard_map/ppermute | solution.py:399
  14.0 21.6 %collective-permute-start.1 = (bf16[288,1024]{1,0:T(8,128)(2,1)S(1)}, bf16[288,1024]{1,0:T(8,128)(2,1)S(1)}, u32[]{:S(2)}, u32[]{:S(2)}) collective-permute-start(bf16[288,1024]{1,0:T(8,128)(2,1)S(1)} %copy-done), channel_id=1, source_target_pairs={{0,4},{12,8},{1,5},{13,9},{2,6},{14,10},{3,7},{15,11},{16,20},{28,... | collective-permute-start | bytes 1769480 | tf_op jit(solution)/shard_map/ppermute | solution.py:408
  20.3 16.2 %collective-permute-start.2 = (bf16[256,1024]{1,0:T(8,128)(2,1)S(1)}, bf16[256,1024]{1,0:T(8,128)(2,1)S(1)}, u32[]{:S(2)}, u32[]{:S(2)}) collective-permute-start(bf16[256,1024]{1,0:T(8,128)(2,1)S(1)} %get-tuple-element.146), channel_id=1, source_target_pairs={{0,2},{1,3},{2,0},{3,1},{4,6},{5,7},{6,4},{7,5},{8,10},{9,11},{10,... | collective-permute-start | bytes 1572872 | tf_op jit(solution)/shard_map/ppermute | solution.py:399
  33.2 27.2 %collective-permute-start.3 = (bf16[256,1024]{1,0:T(8,128)(2,1)S(1)}, bf16[256,1024]{1,0:T(8,128)(2,1)S(1)}, u32[]{:S(2)}, u32[]{:S(2)}) collective-permute-start(bf16[256,1024]{1,0:T(8,128)(2,1)S(1)} %get-tuple-element.99.refs_0_), channel_id=1, source_target_pairs={{0,4},{12,8},{1,5},{13,9},{2,6},{14,10},{3,7},{15,11},{16,20},{28,... | collective-permute-start | bytes 1572872 | tf_op jit(solution)/shard_map/ppermute | solution.py:408
  35.8 6.2 %copy-start.2 = (s32[1024]{0:T(1024)S(1)}, s32[1024]{0:T(1024)}, u32[]{:S(2)}) copy-start(s32[1024]{0:T(1024)} %param.12) | copy-start | bytes 12292
  35.8 27.6 %collective-permute-start.5 = (bf16[288,1024]{1,0:T(8,128)(2,1)S(1)}, bf16[288,1024]{1,0:T(8,128)(2,1)S(1)}, u32[]{:S(2)}, u32[]{:S(2)}) collective-permute-start(bf16[288,1024]{1,0:T(8,128)(2,1)S(1)} %join.6), channel_id=1, source_target_pairs={{4,8},{8,4},{5,9},{9,5},{6,10},{10,6},{7,11},{11,7},{20,24},{24,20... | collective-permute-start | bytes 1769480 | tf_op jit(solution)/shard_map/ppermute | solution.py:408
  36.7 26.7 %collective-permute-start.6 = (bf16[256,1024]{1,0:T(8,128)(2,1)S(1)}, bf16[256,1024]{1,0:T(8,128)(2,1)S(1)}, u32[]{:S(2)}, u32[]{:S(2)}) collective-permute-start(bf16[256,1024]{1,0:T(8,128)(2,1)S(1)} %add.51.refs_5_), channel_id=1, source_target_pairs={{4,8},{8,4},{5,9},{9,5},{6,10},{10,6},{7,11},{11,7},{20,24},{24,20... | collective-permute-start | bytes 1572872 | tf_op jit(solution)/shard_map/ppermute | solution.py:408
  37.4 24.6 %collective-permute-start.4 = (bf16[256,1024]{1,0:T(8,128)(2,1)S(1)}, bf16[256,1024]{1,0:T(8,128)(2,1)S(1)}, u32[]{:S(2)}, u32[]{:S(2)}) collective-permute-start(bf16[256,1024]{1,0:T(8,128)(2,1)S(1)} %add.51.refs_5_), channel_id=1, source_target_pairs={{0,4},{12,8},{4,0},{8,12},{1,5},{13,9},{5,1},{9,13},{2,6},{14,10},... | collective-permute-start | bytes 1572872 | tf_op jit(solution)/shard_map/ppermute | solution.py:451
  60.5 26.2 %collective-permute-start.7 = (bf16[544,1024]{1,0:T(8,128)(2,1)S(1)}, bf16[544,1024]{1,0:T(8,128)(2,1)S(1)}, u32[]{:S(2)}, u32[]{:S(2)}) collective-permute-start(bf16[544,1024]{1,0:T(8,128)(2,1)S(1)} %get-tuple-element.128.refs_0_), channel_id=1, source_target_pairs={{0,4},{12,8},{1,5},{13,9},{2,6},{14,10},{3,7},{15,11},{16,20},{28,... | collective-permute-start | bytes 3342344 | tf_op jit(solution)/shard_map/ppermute | solution.py:408
  62.0 25.5 %collective-permute-start.8 = (bf16[256,1024]{1,0:T(8,128)(2,1)S(1)}, bf16[256,1024]{1,0:T(8,128)(2,1)S(1)}, u32[]{:S(2)}, u32[]{:S(2)}) collective-permute-start(bf16[256,1024]{1,0:T(8,128)(2,1)S(1)} %collective-permute-done.4.refs_6_), channel_id=1, source_target_pairs={{4,8},{8,4},{5,9},{9,5},{6,10},{10,6},{7,11},{11,7},{20,24},{24,20... | collective-permute-start | bytes 1572872 | tf_op jit(solution)/shard_map/ppermute | solution.py:408
  62.7 24.8 %collective-permute-start.9 = (bf16[256,1024]{1,0:T(8,128)(2,1)S(1)}, bf16[256,1024]{1,0:T(8,128)(2,1)S(1)}, u32[]{:S(2)}, u32[]{:S(2)}) collective-permute-start(bf16[256,1024]{1,0:T(8,128)(2,1)S(1)} %join.7), channel_id=1, source_target_pairs={{4,8},{8,4},{5,9},{9,5},{6,10},{10,6},{7,11},{11,7},{20,24},{24,20... | collective-permute-start | bytes 1572872 | tf_op jit(solution)/shard_map/ppermute | solution.py:408
  63.6 30.3 %collective-permute-start.10 = (bf16[544,1024]{1,0:T(8,128)(2,1)S(1)}, bf16[544,1024]{1,0:T(8,128)(2,1)S(1)}, u32[]{:S(2)}, u32[]{:S(2)}) collective-permute-start(bf16[544,1024]{1,0:T(8,128)(2,1)S(1)} %join.8), channel_id=1, source_target_pairs={{8,12},{4,0},{9,13},{5,1},{10,14},{6,2},{11,15},{7,3},{24,28},{20,... | collective-permute-start | bytes 3342344 | tf_op jit(solution)/shard_map/ppermute | solution.py:408
  77.0 21.6 %collective-permute-start.11 = (bf16[288,1024]{1,0:T(8,128)(2,1)S(1)}, bf16[288,1024]{1,0:T(8,128)(2,1)S(1)}, u32[]{:S(2)}, u32[]{:S(2)}) collective-permute-start(bf16[288,1024]{1,0:T(8,128)(2,1)S(1)} %get-tuple-element.131.refs_0_), channel_id=1, source_target_pairs={{0,4},{12,8},{1,5},{13,9},{2,6},{14,10},{3,7},{15,11},{16,20},{28,... | collective-permute-start | bytes 1769480 | tf_op jit(solution)/shard_map/ppermute | solution.py:408
  86.8 16.2 %collective-permute-start.12 = (bf16[288,1024]{1,0:T(8,128)(2,1)S(1)}, bf16[288,1024]{1,0:T(8,128)(2,1)S(1)}, u32[]{:S(2)}, u32[]{:S(2)}) collective-permute-start(bf16[288,1024]{1,0:T(8,128)(2,1)S(1)} %join.9), channel_id=1, source_target_pairs={{4,8},{8,4},{5,9},{9,5},{6,10},{10,6},{7,11},{11,7},{20,24},{24,20... | collective-permute-start | bytes 1769480 | tf_op jit(solution)/shard_map/ppermute | solution.py:408
  87.5 20.6 %collective-permute-start.13 = (bf16[256,1024]{1,0:T(8,128)(2,1)S(1)}, bf16[256,1024]{1,0:T(8,128)(2,1)S(1)}, u32[]{:S(2)}, u32[]{:S(2)}) collective-permute-start(bf16[256,1024]{1,0:T(8,128)(2,1)S(1)} %collective-permute-done.8.refs_8_), channel_id=1, source_target_pairs={{8,12},{4,0},{9,13},{5,1},{10,14},{6,2},{11,15},{7,3},{24,28},{20,... | collective-permute-start | bytes 1572872 | tf_op jit(solution)/shard_map/ppermute | solution.py:408
  89.0 26.7 %collective-permute-start.18 = (bf16[256,1024]{1,0:T(8,128)(2,1)S(1)}, bf16[256,1024]{1,0:T(8,128)(2,1)S(1)}, u32[]{:S(2)}, u32[]{:S(2)}) collective-permute-start(bf16[256,1024]{1,0:T(8,128)(2,1)S(1)} %join.10), channel_id=1, source_target_pairs={{8,12},{4,0},{9,13},{5,1},{10,14},{6,2},{11,15},{7,3},{24,28},{20,... | collective-permute-start | bytes 1572872 | tf_op jit(solution)/shard_map/ppermute | solution.py:408
  94.0 21.7 %collective-permute-start.17 = (bf16[256,1024]{1,0:T(8,128)(2,1)S(1)}, bf16[256,1024]{1,0:T(8,128)(2,1)S(1)}, u32[]{:S(2)}, u32[]{:S(2)}) collective-permute-start(bf16[256,1024]{1,0:T(8,128)(2,1)S(1)} %join.11), channel_id=1, source_target_pairs={{4,8},{8,4},{5,9},{9,5},{6,10},{10,6},{7,11},{11,7},{20,24},{24,20... | collective-permute-start | bytes 1572872 | tf_op jit(solution)/shard_map/ppermute | solution.py:408
  98.6 17.1 %collective-permute-start.16 = (bf16[256,1024]{1,0:T(8,128)(2,1)S(1)}, bf16[256,1024]{1,0:T(8,128)(2,1)S(1)}, u32[]{:S(2)}, u32[]{:S(2)}) collective-permute-start(bf16[256,1024]{1,0:T(8,128)(2,1)S(1)} %get-tuple-element.144.refs_0_), channel_id=1, source_target_pairs={{0,4},{12,8},{1,5},{13,9},{2,6},{14,10},{3,7},{15,11},{16,20},{28,... | collective-permute-start | bytes 1572872 | tf_op jit(solution)/shard_map/ppermute | solution.py:408
  108.2 1.3 %collective-permute-start.14 = (bf16[256,128]{1,0:T(8,128)(2,1)S(1)}, bf16[256,128]{1,0:T(8,128)(2,1)S(1)}, u32[]{:S(2)}, u32[]{:S(2)}) collective-permute-start(bf16[256,128]{1,0:T(8,128)(2,1)S(1)} %bitcast.18), channel_id=1, source_target_pairs={{0,1},{1,0},{2,3},{3,2},{4,5},{5,4},{6,7},{7,6},{8,9},{9,8},{10,11... | collective-permute-start | bytes 196616 | tf_op jit(solution)/shard_map/ppermute | solution.py:399
  109.5 4.3 %collective-permute-start.15 = (bf16[256,128]{1,0:T(8,128)(2,1)S(1)}, bf16[256,128]{1,0:T(8,128)(2,1)S(1)}, u32[]{:S(2)}, u32[]{:S(2)}) collective-permute-start(bf16[256,128]{1,0:T(8,128)(2,1)S(1)} %bitcast_add_fusion), channel_id=1, source_target_pairs={{0,2},{1,3},{2,0},{3,1},{4,6},{5,7},{6,4},{7,5},{8,10},{9,11},{10,... | collective-permute-start | bytes 196616 | tf_op jit(solution)/shard_map/ppermute | solution.py:399

commit v3 on v2

--- a/solution.py
+++ b/solution.py
@@ -309,15 +309,15 @@
     meta = Meta(meta_ref, requests)
     rank = n * rank_rows
     half = out.shape[1] // 2
-    for index, top, targets in items:
+    for index, targets in items:
         for place, k in targets:
 
             @pl.when(meta.place == place)
-            def _(piece=arrays[index], top=top, k=k):
+            def _(piece=arrays[index], k=k):
                 for r in range(requests):
                     first = r * rank + k * rank_rows
                     for c in range(2):
-                        start = top + (c * requests + r) * rank_rows
+                        start = (c * requests + r) * rank_rows
                         rows[first : first + rank_rows, c * half : (c + 1) * half] = piece[start : start + rank_rows, :]
 
     expanded = expanded_inputs(meta, requests_ref, lora_ref)
@@ -325,9 +325,9 @@
     for c in range(2):
         columns = slice(c * half, (c + 1) * half)
         total = jnp.dot(expanded, rows[:, columns], preferred_element_type=jnp.float32)
-        for index, top, which in added:
+        for index, which in added:
             if which == c:
-                total += arrays[index][top : top + block, :].astype(jnp.float32)
+                total += arrays[index][:block, :].astype(jnp.float32)
         out[:, columns] = total.astype(out.dtype)
 
 
@@ -342,29 +342,24 @@
         out_specs=vmem,
         scratch_shapes=[pltpu.VMEM((request_count * n * rank_rows, width), jnp.bfloat16)],
         compiler_params=params(20),
-        cost_estimate=small_cost(),
+        cost_estimate=pl.CostEstimate(flops=10**6, bytes_accessed=10**5, transcendentals=0),
         name="finish",
     )(meta, requests, lora, *arrays)
 
 
-def join_kernel(count, term_top, came_top, under_top, term, came, *refs):
-    out = refs[-1]
+def join_kernel(count, term_top, came_top, term, came, out):
     total = term[term_top : term_top + count, :].astype(jnp.float32)
     total += came[came_top : came_top + count, :].astype(jnp.float32)
-    out[:count, :] = total.astype(out.dtype)
-    if len(refs) > 1:
-        under = refs[0]
-        out[count:, :] = under[under_top : under_top + out.shape[0] - count, :]
-
-
-def join(token, count, term, term_top, came, came_top, under=None, under_top=0, under_count=0, weight=10**6):
-    arrays = [term, came] + ([] if under is None else [under])
-    arrays = lax.optimization_barrier((arrays, token))[0]
+    out[...] = total.astype(out.dtype)
+
+
+def join(token, count, term, term_top, came, came_top, weight=10**6):
+    arrays = lax.optimization_barrier(((term, came), token))[0]
     vmem = pl.BlockSpec(memory_space=pltpu.VMEM)
     return pl.pallas_call(
-        lambda *refs: join_kernel(count, term_top, came_top, under_top, *refs),
-        out_shape=jax.ShapeDtypeStruct((count + under_count, term.shape[1]), term.dtype),
-        in_specs=[vmem] * len(arrays),
+        lambda *refs: join_kernel(count, term_top, came_top, *refs),
+        out_shape=jax.ShapeDtypeStruct((count, term.shape[1]), term.dtype),
+        in_specs=[vmem] * 2,
         out_specs=vmem,
         compiler_params=params(12),
         cost_estimate=pl.CostEstimate(flops=weight, bytes_accessed=10**5, transcendentals=0),
@@ -414,7 +409,6 @@
     width = input_factor.shape[2]
     rank_rows = output_factor.shape[1]
     piece = block + block * width // (matrix.shape[1] // 2)
-    bundle = 2 * request_count * rank_rows
 
     def base(token, groups, inputs_for, half, under=None):
         return base_terms(
@@ -454,13 +448,15 @@
 
     token = after(token, s10_s11)
     e0_3 = send(s10_s11, 0, token)
+    token, far = lax.optimization_barrier((token, far))
+    far_1 = send(far, 2, token)
     token, e0_2 = lax.optimization_barrier((token, e0_2))
-    b11 = join(token, block, s01, 0, e0_2, 0, weight=HEAVY)
+    b11 = join(token, block, s01, 0, e0_2, 0, HEAVY)
     token, near = lax.optimization_barrier((after(token, b11), near))
     e1_3 = along_edge(b11, 1)
     far_2 = send(near, 1, token)
-    token, e1_2, far = lax.optimization_barrier((token, e1_2, far))
-    c20 = join(token, piece, s20, 0, e1_2, 0, far, 0, bundle)
+    token, e1_2 = lax.optimization_barrier((token, e1_2))
+    c20 = join(token, piece, s20, 0, e1_2, 0)
     token = after(token, c20)
     e2_3 = along_edge(c20, 2)
     s21, s31 = base(token, [[2], [3]], [3], 1)
@@ -471,10 +467,11 @@
     b20 = join(token, piece, s10_s11, 0, e0_3, 0)
     token = after(token, b20)
     e1_4 = along_edge(b20, 1)
+    token, far_1 = lax.optimization_barrier((token, far_1))
     token, far_2 = lax.optimization_barrier((token, far_2))
-    last_rows = send(far_2, 2, token)
+    far_3 = send(far_2, 2, token)
     token, e1_3 = lax.optimization_barrier((token, e1_3))
-    c21 = join(token, block, s21, 0, e1_3, 0, weight=HEAVY)
+    c21 = join(token, block, s21, 0, e1_3, 0, HEAVY)
     token = after(token, c21)
     e2_4 = along_edge(c21, 2)
     token, e2_3 = lax.optimization_barrier((token, e2_3))
@@ -485,25 +482,24 @@
 
     token, e0_4 = lax.optimization_barrier((token, e0_4))
     token, e1_4 = lax.optimization_barrier((token, e1_4))
-    token, last_rows = lax.optimization_barrier((token, last_rows))
+    token, far_3 = lax.optimization_barrier((token, far_3))
     e1_4 = after(e1_4, token)
     lora = s31[block:].astype(jnp.float32) + e0_4[block:].astype(jnp.float32)
     lora += e1_4[block:].astype(jnp.float32) + e2_3[block:piece].astype(jnp.float32)
     lora = lora.astype(jnp.bfloat16).reshape(piece - block, -1, width).swapaxes(0, 1).reshape(block, width)
-    lora = lora + swap(lora, "store", 1)
-    lora = lora + swap(lora, "store", 2)
-    arrays = [s30, s31, rows, near, far, far_2, e2_3, last_rows, e0_4, e1_4]
+    lora = sum((swap(lora, "store", other) for other in range(1, 2 * PAIRS)), lora)
+    arrays = [s30, s31, rows, near, far, far_1, far_2, far_3, e0_4, e1_4, e2_3, e0_5]
     items = [
-        (2, 0, [(z, z) for z in range(n)]),
-        (3, 0, [(0, 1), (1, 0), (2, 3), (3, 2)]),
-        (4, 0, [(1, 2), (2, 1)]),
-        (5, 0, [(1, 3), (2, 0)]),
-        (6, piece, [(0, 2), (3, 1)]),
-        (7, 0, [(0, 3), (3, 0)]),
+        (2, [(z, z) for z in range(n)]),
+        (3, [(0, 1), (1, 0), (2, 3), (3, 2)]),
+        (4, [(1, 2), (2, 1)]),
+        (5, [(0, 2), (3, 1)]),
+        (6, [(1, 3), (2, 0)]),
+        (7, [(0, 3), (3, 0)]),
     ]
-    added = [(0, 0, 0), (8, 0, 0), (9, 0, 0), (6, 0, 0), (1, 0, 1)]
+    added = [(0, 0), (8, 0), (9, 0), (10, 0), (1, 1), (11, 1)]
     out = finish(token, requests, lora, arrays, items, added, request_count, rank_rows, n)
-    return add_last(out, e0_5, e1_5, e2_4)
+    return add_last(out, e1_5, e2_4)
 
 
 def anywhere(hidden, matrix, input_factor, output_factor, token_requests, meta):

time: 117 us -> 121 us (1.034)
  waiting for transfers between devices: 20.3 us -> 25.6 us
    ppermute x14 -> x15, starting transfers between devices: 28.7 us -> 33.8 us  [along_edge(): lax.ppermute(x, 'tensor', [(edge, edge + 1), (n - 1 - edge, n - 2 - edge)])]
    ppermute x1, starting transfers between devices: 4.56 us -> 0.64 us  [on_line(): lax.ppermute(rows, 'tensor', [(0, 1), (n - 1, n - 2), (1, 0), (n - 2, n -...]
    ppermute x14 -> x15, waiting for transfers between devices: 14.8 us -> 18.2 us  [along_edge(): lax.ppermute(x, 'tensor', [(edge, edge + 1), (n - 1 - edge, n - 2 - edge)])]
    ppermute x4 -> x5, waiting for transfers between devices: 5.5 us -> 7.46 us  [swap(): lax.ppermute(x, axis, [(i, i ^ bit) for i in range(lax.axis_size(axis))])]
  transfers between devices with their start and end apart: 19 -> 21, of which waited for: 6 -> 8; matrix products, arithmetic and copies ran while one was open for 1% -> 1% of each run, Pallas kernels for 38% -> 36%
where the time goes in v3:
time: 121 us
  Pallas kernels  57.2 us (47%)
  starting transfers between devices  35 us (29%)
  waiting for transfers between devices  25.6 us (21%)
  other arithmetic  1.57 us (1%)
  local copies, waits for them, and re-layouts  1.34 us (1%)
    pallas_call x4, Pallas kernels, base_terms(): pl.pallas_call(lambda *refs: base_kernel(line_order(n), groups, inputs_fo...  52.6 us
    ppermute x15, starting transfers between devices, along_edge(): lax.ppermute(x, 'tensor', [(edge, edge + 1), (n - 1 - edge, n - 2 - edge)])  33.8 us
    ppermute x15, waiting for transfers between devices, along_edge(): lax.ppermute(x, 'tensor', [(edge, edge + 1), (n - 1 - edge, n - 2 - edge)])  18.2 us
    ppermute x5, waiting for transfers between devices, swap(): lax.ppermute(x, axis, [(i, i ^ bit) for i in range(lax.axis_size(axis))])  7.46 us
  transfers between devices with their start and end apart: 21, of which 8 were waited for; matrix products, arithmetic and copies ran while one was open for 1% of the time, Pallas kernels for 36%

profile of v3, /device:TPU:0, one launch (start us, length us, event | category | flops | bytes accessed | tf_op | source)
XLA Modules:
  0.0 121.2 jit_solution(3157862916880372512)
XLA Ops:
  0.0 1.3 %concatenate.3.refs_0_ = s32[38]{0:T(128)} concatenate(s32[1]{0:T(128)} %bitcast, s32[1]{0:T(128)} %bitcast.1, s32[4]{0:T(128)} %param.13, s32[16]{0:T(128)} %param.14, s32[16]{0:T(128)} %param.15), dimensions={0} | concatenate | bytes 304 | tf_op jit(solution)/shard_map/concatenate | solution.py:543
  1.3 11.5 %base_terms.4.refs_0_ = bf16[288,1024]{1,0:T(8,128)(2,1)} custom-call(s32[38]{0:T(128)} %concatenate.3.refs_0_, s32[8,128]{1,0:T(8,128)} %bitcast.14, bf16[4,7168,128]{2,1,0:T(8,128)(2,1)} %refs_2_.7, bf16[1024,7168]{1,0:T(8,128)(2,1)} %refs_3_.5, bf16[7168,2048]{1,0:T(8,128)(2,1)} %refs_4_.5), custom_call_target="tpu_custom_call" | custom-call | flops 1000000 | bytes 100000 | tf_op jit(solution)/shard_map/base_terms/pallas_call | solution.py:246
  12.9 0.8 select_rows.1
  13.8 5.0 %collective-permute-start.1 = (bf16[288,1024]{1,0:T(8,128)(2,1)}, bf16[288,1024]{1,0:T(8,128)(2,1)S(1)}, u32[]{:S(2)}, u32[]{:S(2)}) collective-permute-start(bf16[288,1024]{1,0:T(8,128)(2,1)} %base_terms.4.refs_0_), channel_id=1, source_target_pairs={{0,4},{12,8},{1,5},{13,9},{2,6},{14,10},{3,7},{15,11},{16,20},{28,... | collective-permute-start | bytes 1769480 | tf_op jit(solution)/shard_map/ppermute | solution.py:403
  18.8 1.3 %add_bitcast_fusion = (bf16[256,1024]{1,0:T(8,128)(2,1)S(1)}, bf16[256,1024]{1,0:T(8,128)(2,1)S(1)}) fusion(bf16[2,256,1024]{2,1,0:T(8,128)(2,1)} %collective-permute-done, s32[]{:T(128)S(6)} %select_n.22, bf16[2,256,1024]{2,1,0:T(8,128)(2,1)S(1)} %get-tuple-element.83, s32[]{:T(128)S(6)} %select_n.21), kind=kLoop, calls=%fused_computation | loop fusion | flops 524288 | bytes 3145736 | tf_op jit(solution)/shard_map/add | solution.py:431
  20.2 11.6 %base_terms.5 = (bf16[256,1024]{1,0:T(8,128)(2,1)S(1)}, bf16[256,1024]{1,0:T(8,128)(2,1)S(1)}) custom-call(s32[38]{0:T(128)S(1)} %copy-done.3, bf16[1024,7168]{1,0:T(8,128)(2,1)} %refs_3_.5, bf16[7168,2048]{1,0:T(8,128)(2,1)} %refs_4_.5), custom_call_target="tpu_custom_call" | custom-call | flops 1000000 | bytes 100000 | tf_op jit(solution)/shard_map/base_terms/pallas_call | solution.py:246
  32.4 1.8 %collective-permute-done.2 = bf16[256,1024]{1,0:T(8,128)(2,1)S(1)} collective-permute-done((bf16[256,1024]{1,0:T(8,128)(2,1)S(1)}, bf16[256,1024]{1,0:T(8,128)(2,1)S(1)}, u32[]{:S(2)}, u32[]{:S(2)}) %collective-permute-start.2) | collective-permute-done | bytes 524320 | tf_op jit(solution)/shard_map/ppermute | solution.py:394
  34.4 0.7 collective-permute-start.3
  35.1 7.3 %collective-permute-start.4 = (bf16[256,1024]{1,0:T(8,128)(2,1)S(1)}, bf16[256,1024]{1,0:T(8,128)(2,1)S(1)}, u32[]{:S(2)}, u32[]{:S(2)}) collective-permute-start(bf16[256,1024]{1,0:T(8,128)(2,1)S(1)} %get-tuple-element.103.refs_0_), channel_id=1, source_target_pairs={{0,4},{12,8},{1,5},{13,9},{2,6},{14,10},{3,7},{15,11},{16,20},{28,... | collective-permute-start | bytes 1572872 | tf_op jit(solution)/shard_map/ppermute | solution.py:403
  42.4 0.7 collective-permute-start.6
  43.1 0.6 collective-permute-start.5
  43.8 17.4 %base_terms.6 = (bf16[544,1024]{1,0:T(8,128)(2,1)S(1)}, bf16[288,1024]{1,0:T(8,128)(2,1)S(1)}, bf16[256,1024]{1,0:T(8,128)(2,1)S(1)}) custom-call(s32[38]{0:T(128)S(1)} %copy-done.3, s32[8,128]{1,0:T(8,128)S(1)} %bitcast.15, bf16[4,7168,128]{2,1,0:T(8,128)(2,1)} %refs_2_.7, bf16[1024,7168]{1,0:T(8,128)(2,1)} %refs_3_.5, bf16[7168,2048]{1,0:T(8,128)(2,1)} %refs_4_.5, ...), custom_call_target="tpu_custom_call" | custom-call | flops 1000000 | bytes 100000 | tf_op jit(solution)/shard_map/base_terms/pallas_call | solution.py:246
  61.2 3.4 %collective-permute-start.7 = (bf16[544,1024]{1,0:T(8,128)(2,1)S(1)}, bf16[544,1024]{1,0:T(8,128)(2,1)S(1)}, u32[]{:S(2)}, u32[]{:S(2)}) collective-permute-start(bf16[544,1024]{1,0:T(8,128)(2,1)S(1)} %get-tuple-element.133.refs_0_), channel_id=1, source_target_pairs={{0,4},{12,8},{1,5},{13,9},{2,6},{14,10},{3,7},{15,11},{16,20},{28,... | collective-permute-start | bytes 3342344 | tf_op jit(solution)/shard_map/ppermute | solution.py:403
  64.8 1.3 %collective-permute-start.8 = (bf16[256,1024]{1,0:T(8,128)(2,1)S(1)}, bf16[256,1024]{1,0:T(8,128)(2,1)S(1)}, u32[]{:S(2)}, u32[]{:S(2)}) collective-permute-start(bf16[256,1024]{1,0:T(8,128)(2,1)S(1)} %collective-permute-done.3.refs_7_), channel_id=1, source_target_pairs={{8,12},{4,0},{9,13},{5,1},{10,14},{6,2},{11,15},{7,3},{24,28},{20,... | collective-permute-start | bytes 1572872 | tf_op jit(solution)/shard_map/ppermute | solution.py:403
  66.1 0.7 collective-permute-start.9
  66.8 0.7 collective-permute-start.10
  67.6 1.3 %collective-permute-start.11 = (bf16[288,1024]{1,0:T(8,128)(2,1)S(1)}, bf16[288,1024]{1,0:T(8,128)(2,1)S(1)}, u32[]{:S(2)}, u32[]{:S(2)}) collective-permute-start(bf16[288,1024]{1,0:T(8,128)(2,1)S(1)} %join.8), channel_id=1, source_target_pairs={{8,12},{4,0},{9,13},{5,1},{10,14},{6,2},{11,15},{7,3},{24,28},{20,... | collective-permute-start | bytes 1769480 | tf_op jit(solution)/shard_map/ppermute | solution.py:403
  68.9 12.1 %base_terms.7 = (bf16[256,1024]{1,0:T(8,128)(2,1)S(1)}, bf16[288,1024]{1,0:T(8,128)(2,1)S(1)}) custom-call(s32[38]{0:T(128)S(1)} %copy-done.3, s32[8,128]{1,0:T(8,128)S(1)} %bitcast.16, bf16[4,7168,128]{2,1,0:T(8,128)(2,1)} %refs_2_.7, bf16[1024,7168]{1,0:T(8,128)(2,1)} %refs_3_.5, bf16[7168,2048]{1,0:T(8,128)(2,1)} %refs_4_.5), custom_call_target="tpu_custom_call" | custom-call | flops 1000000 | bytes 100000 | tf_op jit(solution)/shard_map/base_terms/pallas_call | solution.py:246
  81.0 7.3 %collective-permute-done.7.refs_1_ = bf16[544,1024]{1,0:T(8,128)(2,1)S(1)} collective-permute-done((bf16[544,1024]{1,0:T(8,128)(2,1)S(1)}, bf16[544,1024]{1,0:T(8,128)(2,1)S(1)}, u32[]{:S(2)}, u32[]{:S(2)}) %collective-permute-start.7) | collective-permute-done | bytes 1114144 | tf_op jit(solution)/shard_map/ppermute | solution.py:403
  88.3 4.4 %collective-permute-start.12 = (bf16[288,1024]{1,0:T(8,128)(2,1)S(1)}, bf16[288,1024]{1,0:T(8,128)(2,1)S(1)}, u32[]{:S(2)}, u32[]{:S(2)}) collective-permute-start(bf16[288,1024]{1,0:T(8,128)(2,1)S(1)} %get-tuple-element.136.refs_0_), channel_id=1, source_target_pairs={{0,4},{12,8},{1,5},{13,9},{2,6},{14,10},{3,7},{15,11},{16,20},{28,... | collective-permute-start | bytes 1769480 | tf_op jit(solution)/shard_map/ppermute | solution.py:403
  92.9 0.7 collective-permute-start.13
  93.6 1.3 %collective-permute-start.14 = (bf16[256,1024]{1,0:T(8,128)(2,1)S(1)}, bf16[256,1024]{1,0:T(8,128)(2,1)S(1)}, u32[]{:S(2)}, u32[]{:S(2)}) collective-permute-start(bf16[256,1024]{1,0:T(8,128)(2,1)S(1)} %collective-permute-done.9.refs_9_), channel_id=1, source_target_pairs={{8,12},{4,0},{9,13},{5,1},{10,14},{6,2},{11,15},{7,3},{24,28},{20,... | collective-permute-start | bytes 1572872 | tf_op jit(solution)/shard_map/ppermute | solution.py:403
  95.2 0.7 collective-permute-start.19
  95.9 1.3 %collective-permute-start.20 = (bf16[256,1024]{1,0:T(8,128)(2,1)S(1)}, bf16[256,1024]{1,0:T(8,128)(2,1)S(1)}, u32[]{:S(2)}, u32[]{:S(2)}) collective-permute-start(bf16[256,1024]{1,0:T(8,128)(2,1)S(1)} %join.10), channel_id=1, source_target_pairs={{8,12},{4,0},{9,13},{5,1},{10,14},{6,2},{11,15},{7,3},{24,28},{20,... | collective-permute-start | bytes 1572872 | tf_op jit(solution)/shard_map/ppermute | solution.py:403
  97.2 7.2 %collective-permute-done.12.refs_11_ = bf16[288,1024]{1,0:T(8,128)(2,1)S(1)} collective-permute-done((bf16[288,1024]{1,0:T(8,128)(2,1)S(1)}, bf16[288,1024]{1,0:T(8,128)(2,1)S(1)}, u32[]{:S(2)}, u32[]{:S(2)}) %collective-permute-start.12) | collective-permute-done | bytes 589856 | tf_op jit(solution)/shard_map/ppermute | solution.py:403
  104.4 4.4 %collective-permute-start.18 = (bf16[256,1024]{1,0:T(8,128)(2,1)S(1)}, bf16[256,1024]{1,0:T(8,128)(2,1)S(1)}, u32[]{:S(2)}, u32[]{:S(2)}) collective-permute-start(bf16[256,1024]{1,0:T(8,128)(2,1)S(1)} %get-tuple-element.150.refs_0_), channel_id=1, source_target_pairs={{0,4},{12,8},{1,5},{13,9},{2,6},{14,10},{3,7},{15,11},{16,20},{28,... | collective-permute-start | bytes 1572872 | tf_op jit(solution)/shard_map/ppermute | solution.py:403
  108.8 1.6 %collective-permute-done.14.refs_10_ = bf16[256,1024]{1,0:T(8,128)(2,1)S(1)} collective-permute-done((bf16[256,1024]{1,0:T(8,128)(2,1)S(1)}, bf16[256,1024]{1,0:T(8,128)(2,1)S(1)}, u32[]{:S(2)}, u32[]{:S(2)}) %collective-permute-start.14) | collective-permute-done | bytes 524320 | tf_op jit(solution)/shard_map/ppermute | solution.py:403
  110.8 4.4 %collective-permute-done.16 = bf16[256,128]{1,0:T(8,128)(2,1)S(1)} collective-permute-done((bf16[256,128]{1,0:T(8,128)(2,1)S(1)}, bf16[256,128]{1,0:T(8,128)(2,1)S(1)}, u32[]{:S(2)}, u32[]{:S(2)}) %collective-permute-start.16) | collective-permute-done | bytes 65568 | tf_op jit(solution)/shard_map/ppermute | solution.py:394
  115.2 1.2 %collective-permute-done.15 = bf16[256,128]{1,0:T(8,128)(2,1)S(1)} collective-permute-done((bf16[256,128]{1,0:T(8,128)(2,1)S(1)}, bf16[256,128]{1,0:T(8,128)(2,1)S(1)}, u32[]{:S(2)}, u32[]{:S(2)}) %collective-permute-start.15) | collective-permute-done | bytes 65568 | tf_op jit(solution)/shard_map/ppermute | solution.py:394
  116.5 1.6 %collective-permute-done.18.refs_14_ = bf16[256,1024]{1,0:T(8,128)(2,1)S(1)} collective-permute-done((bf16[256,1024]{1,0:T(8,128)(2,1)S(1)}, bf16[256,1024]{1,0:T(8,128)(2,1)S(1)}, u32[]{:S(2)}, u32[]{:S(2)}) %collective-permute-start.18) | collective-permute-done | bytes 524320 | tf_op jit(solution)/shard_map/ppermute | solution.py:403
  118.2 1.8 %finish.1.total = bf16[256,2048]{1,0:T(8,128)(2,1)S(1)} custom-call(s32[38]{0:T(128)S(1)} %copy-done.3, s32[8,128]{1,0:T(8,128)S(1)} %bitcast.17, bf16[256,128]{1,0:T(8,128)(2,1)S(1)} %add_add_fusion.refs_2_, bf16[256,1024]{1,0:T(8,128)(2,1)S(1)} %get-tuple-element.147.refs_3_, bf16[288,1024]{1,0:T(8,128)(2,1)S(1)} %get-tuple-element.142.refs_4_, ...), custom_call_target="tpu_custom_call" | custom-call | flops 1000000 | bytes 100000 | tf_op jit(solution)/shard_map/finish/pallas_call | solution.py:338
  120.0 1.2 add_last.1
  (38 shorter events, 2.1 us)
Async XLA Ops:
  1.3 11.6 %copy-start.1 = (bf16[4,32,8192]{2,1,0:T(8,128)(2,1)S(1)}, bf16[4,32,8192]{2,1,0:T(8,128)(2,1)}, u32[]{:S(2)}) copy-start(bf16[4,32,8192]{2,1,0:T(8,128)(2,1)} %refs_1_.2) | copy-start | bytes 6291460
  1.3 11.6 %copy-start.3 = (s32[38]{0:T(128)S(1)}, s32[38]{0:T(128)}, u32[]{:S(2)}) copy-start(s32[38]{0:T(128)} %concatenate.3.refs_0_) | copy-start | bytes 460
  13.7 5.1 %collective-permute-start = (bf16[2,256,1024]{2,1,0:T(8,128)(2,1)S(1)}, bf16[2,256,1024]{2,1,0:T(8,128)(2,1)}, u32[]{:S(2)}, u32[]{:S(2)}) collective-permute-start(bf16[2,256,1024]{2,1,0:T(8,128)(2,1)S(1)} %get-tuple-element.80), channel_id=1, source_target_pairs={{0,1},{1,0},{2,3},{3,2},{4,5},{5,4},{6,7},{7,6},{8,9},{9,8},{10,11... | collective-permute-start | bytes 3145736 | tf_op jit(solution)/shard_map/ppermute | solution.py:394
  13.8 18.5 %collective-permute-start.1 = (bf16[288,1024]{1,0:T(8,128)(2,1)}, bf16[288,1024]{1,0:T(8,128)(2,1)S(1)}, u32[]{:S(2)}, u32[]{:S(2)}) collective-permute-start(bf16[288,1024]{1,0:T(8,128)(2,1)} %base_terms.4.refs_0_), channel_id=1, source_target_pairs={{0,4},{12,8},{1,5},{13,9},{2,6},{14,10},{3,7},{15,11},{16,20},{28,... | collective-permute-start | bytes 1769480 | tf_op jit(solution)/shard_map/ppermute | solution.py:403
  20.1 14.1 %collective-permute-start.2 = (bf16[256,1024]{1,0:T(8,128)(2,1)S(1)}, bf16[256,1024]{1,0:T(8,128)(2,1)S(1)}, u32[]{:S(2)}, u32[]{:S(2)}) collective-permute-start(bf16[256,1024]{1,0:T(8,128)(2,1)S(1)} %get-tuple-element.152), channel_id=1, source_target_pairs={{0,2},{1,3},{2,0},{3,1},{4,6},{5,7},{6,4},{7,5},{8,10},{9,11},{10,... | collective-permute-start | bytes 1572872 | tf_op jit(solution)/shard_map/ppermute | solution.py:394
  20.2 12.1 %copy-start = (bf16[288,1024]{1,0:T(8,128)(2,1)S(1)}, bf16[288,1024]{1,0:T(8,128)(2,1)}, u32[]{:S(2)}) copy-start(bf16[288,1024]{1,0:T(8,128)(2,1)} %base_terms.4.refs_0_) | copy-start | bytes 1769476
  20.2 23.6 %copy-start.2 = (s32[1024]{0:T(1024)S(1)}, s32[1024]{0:T(1024)}, u32[]{:S(2)}) copy-start(s32[1024]{0:T(1024)} %param.12) | copy-start | bytes 12292
  34.4 30.2 %collective-permute-start.3 = (bf16[256,1024]{1,0:T(8,128)(2,1)S(1)}, bf16[256,1024]{1,0:T(8,128)(2,1)S(1)}, u32[]{:S(2)}, u32[]{:S(2)}) collective-permute-start(bf16[256,1024]{1,0:T(8,128)(2,1)S(1)} %add.54.refs_5_), channel_id=1, source_target_pairs={{4,8},{8,4},{5,9},{9,5},{6,10},{10,6},{7,11},{11,7},{20,24},{24,20... | collective-permute-start | bytes 1572872 | tf_op jit(solution)/shard_map/ppermute | solution.py:403
  35.1 29.5 %collective-permute-start.4 = (bf16[256,1024]{1,0:T(8,128)(2,1)S(1)}, bf16[256,1024]{1,0:T(8,128)(2,1)S(1)}, u32[]{:S(2)}, u32[]{:S(2)}) collective-permute-start(bf16[256,1024]{1,0:T(8,128)(2,1)S(1)} %get-tuple-element.103.refs_0_), channel_id=1, source_target_pairs={{0,4},{12,8},{1,5},{13,9},{2,6},{14,10},{3,7},{15,11},{16,20},{28,... | collective-permute-start | bytes 1572872 | tf_op jit(solution)/shard_map/ppermute | solution.py:403
  42.4 25.0 %collective-permute-start.6 = (bf16[288,1024]{1,0:T(8,128)(2,1)S(1)}, bf16[288,1024]{1,0:T(8,128)(2,1)S(1)}, u32[]{:S(2)}, u32[]{:S(2)}) collective-permute-start(bf16[288,1024]{1,0:T(8,128)(2,1)S(1)} %join.6), channel_id=1, source_target_pairs={{4,8},{8,4},{5,9},{9,5},{6,10},{10,6},{7,11},{11,7},{20,24},{24,20... | collective-permute-start | bytes 1769480 | tf_op jit(solution)/shard_map/ppermute | solution.py:403
  43.1 21.6 %collective-permute-start.5 = (bf16[256,1024]{1,0:T(8,128)(2,1)S(1)}, bf16[256,1024]{1,0:T(8,128)(2,1)S(1)}, u32[]{:S(2)}, u32[]{:S(2)}) collective-permute-start(bf16[256,1024]{1,0:T(8,128)(2,1)S(1)} %add.54.refs_5_), channel_id=1, source_target_pairs={{0,4},{12,8},{4,0},{8,12},{1,5},{13,9},{5,1},{9,13},{2,6},{14,10},... | collective-permute-start | bytes 1572872 | tf_op jit(solution)/shard_map/ppermute | solution.py:445
  61.2 27.2 %collective-permute-start.7 = (bf16[544,1024]{1,0:T(8,128)(2,1)S(1)}, bf16[544,1024]{1,0:T(8,128)(2,1)S(1)}, u32[]{:S(2)}, u32[]{:S(2)}) collective-permute-start(bf16[544,1024]{1,0:T(8,128)(2,1)S(1)} %get-tuple-element.133.refs_0_), channel_id=1, source_target_pairs={{0,4},{12,8},{1,5},{13,9},{2,6},{14,10},{3,7},{15,11},{16,20},{28,... | collective-permute-start | bytes 3342344 | tf_op jit(solution)/shard_map/ppermute | solution.py:403
  64.8 28.1 %collective-permute-start.8 = (bf16[256,1024]{1,0:T(8,128)(2,1)S(1)}, bf16[256,1024]{1,0:T(8,128)(2,1)S(1)}, u32[]{:S(2)}, u32[]{:S(2)}) collective-permute-start(bf16[256,1024]{1,0:T(8,128)(2,1)S(1)} %collective-permute-done.3.refs_7_), channel_id=1, source_target_pairs={{8,12},{4,0},{9,13},{5,1},{10,14},{6,2},{11,15},{7,3},{24,28},{20,... | collective-permute-start | bytes 1572872 | tf_op jit(solution)/shard_map/ppermute | solution.py:403
  66.1 27.6 %collective-permute-start.9 = (bf16[256,1024]{1,0:T(8,128)(2,1)S(1)}, bf16[256,1024]{1,0:T(8,128)(2,1)S(1)}, u32[]{:S(2)}, u32[]{:S(2)}) collective-permute-start(bf16[256,1024]{1,0:T(8,128)(2,1)S(1)} %collective-permute-done.5.refs_6_), channel_id=1, source_target_pairs={{4,8},{8,4},{5,9},{9,5},{6,10},{10,6},{7,11},{11,7},{20,24},{24,20... | collective-permute-start | bytes 1572872 | tf_op jit(solution)/shard_map/ppermute | solution.py:403
  66.8 26.9 %collective-permute-start.10 = (bf16[256,1024]{1,0:T(8,128)(2,1)S(1)}, bf16[256,1024]{1,0:T(8,128)(2,1)S(1)}, u32[]{:S(2)}, u32[]{:S(2)}) collective-permute-start(bf16[256,1024]{1,0:T(8,128)(2,1)S(1)} %join.7), channel_id=1, source_target_pairs={{4,8},{8,4},{5,9},{9,5},{6,10},{10,6},{7,11},{11,7},{20,24},{24,20... | collective-permute-start | bytes 1572872 | tf_op jit(solution)/shard_map/ppermute | solution.py:403
  67.6 27.4 %collective-permute-start.11 = (bf16[288,1024]{1,0:T(8,128)(2,1)S(1)}, bf16[288,1024]{1,0:T(8,128)(2,1)S(1)}, u32[]{:S(2)}, u32[]{:S(2)}) collective-permute-start(bf16[288,1024]{1,0:T(8,128)(2,1)S(1)} %join.8), channel_id=1, source_target_pairs={{8,12},{4,0},{9,13},{5,1},{10,14},{6,2},{11,15},{7,3},{24,28},{20,... | collective-permute-start | bytes 1769480 | tf_op jit(solution)/shard_map/ppermute | solution.py:403
  88.3 16.1 %collective-permute-start.12 = (bf16[288,1024]{1,0:T(8,128)(2,1)S(1)}, bf16[288,1024]{1,0:T(8,128)(2,1)S(1)}, u32[]{:S(2)}, u32[]{:S(2)}) collective-permute-start(bf16[288,1024]{1,0:T(8,128)(2,1)S(1)} %get-tuple-element.136.refs_0_), channel_id=1, source_target_pairs={{0,4},{12,8},{1,5},{13,9},{2,6},{14,10},{3,7},{15,11},{16,20},{28,... | collective-permute-start | bytes 1769480 | tf_op jit(solution)/shard_map/ppermute | solution.py:403
  92.9 15.9 %collective-permute-start.13 = (bf16[288,1024]{1,0:T(8,128)(2,1)S(1)}, bf16[288,1024]{1,0:T(8,128)(2,1)S(1)}, u32[]{:S(2)}, u32[]{:S(2)}) collective-permute-start(bf16[288,1024]{1,0:T(8,128)(2,1)S(1)} %join.9), channel_id=1, source_target_pairs={{4,8},{8,4},{5,9},{9,5},{6,10},{10,6},{7,11},{11,7},{20,24},{24,20... | collective-permute-start | bytes 1769480 | tf_op jit(solution)/shard_map/ppermute | solution.py:403
  93.6 16.8 %collective-permute-start.14 = (bf16[256,1024]{1,0:T(8,128)(2,1)S(1)}, bf16[256,1024]{1,0:T(8,128)(2,1)S(1)}, u32[]{:S(2)}, u32[]{:S(2)}) collective-permute-start(bf16[256,1024]{1,0:T(8,128)(2,1)S(1)} %collective-permute-done.9.refs_9_), channel_id=1, source_target_pairs={{8,12},{4,0},{9,13},{5,1},{10,14},{6,2},{11,15},{7,3},{24,28},{20,... | collective-permute-start | bytes 1572872 | tf_op jit(solution)/shard_map/ppermute | solution.py:403
  95.2 24.8 %collective-permute-start.19 = (bf16[256,1024]{1,0:T(8,128)(2,1)S(1)}, bf16[256,1024]{1,0:T(8,128)(2,1)S(1)}, u32[]{:S(2)}, u32[]{:S(2)}) collective-permute-start(bf16[256,1024]{1,0:T(8,128)(2,1)S(1)} %join.11), channel_id=1, source_target_pairs={{4,8},{8,4},{5,9},{9,5},{6,10},{10,6},{7,11},{11,7},{20,24},{24,20... | collective-permute-start | bytes 1572872 | tf_op jit(solution)/shard_map/ppermute | solution.py:403
  95.9 24.1 %collective-permute-start.20 = (bf16[256,1024]{1,0:T(8,128)(2,1)S(1)}, bf16[256,1024]{1,0:T(8,128)(2,1)S(1)}, u32[]{:S(2)}, u32[]{:S(2)}) collective-permute-start(bf16[256,1024]{1,0:T(8,128)(2,1)S(1)} %join.10), channel_id=1, source_target_pairs={{8,12},{4,0},{9,13},{5,1},{10,14},{6,2},{11,15},{7,3},{24,28},{20,... | collective-permute-start | bytes 1572872 | tf_op jit(solution)/shard_map/ppermute | solution.py:403
  104.4 13.7 %collective-permute-start.18 = (bf16[256,1024]{1,0:T(8,128)(2,1)S(1)}, bf16[256,1024]{1,0:T(8,128)(2,1)S(1)}, u32[]{:S(2)}, u32[]{:S(2)}) collective-permute-start(bf16[256,1024]{1,0:T(8,128)(2,1)S(1)} %get-tuple-element.150.refs_0_), channel_id=1, source_target_pairs={{0,4},{12,8},{1,5},{13,9},{2,6},{14,10},{3,7},{15,11},{16,20},{28,... | collective-permute-start | bytes 1572872 | tf_op jit(solution)/shard_map/ppermute | solution.py:403
  110.5 4.8 %collective-permute-start.16 = (bf16[256,128]{1,0:T(8,128)(2,1)S(1)}, bf16[256,128]{1,0:T(8,128)(2,1)S(1)}, u32[]{:S(2)}, u32[]{:S(2)}) collective-permute-start(bf16[256,128]{1,0:T(8,128)(2,1)S(1)} %bitcast.18), channel_id=1, source_target_pairs={{0,2},{1,3},{2,0},{3,1},{4,6},{5,7},{6,4},{7,5},{8,10},{9,11},{10,... | collective-permute-start | bytes 196616 | tf_op jit(solution)/shard_map/ppermute | solution.py:394
  110.8 4.4 %collective-permute-start.17 = (bf16[256,128]{1,0:T(8,128)(2,1)S(1)}, bf16[256,128]{1,0:T(8,128)(2,1)S(1)}, u32[]{:S(2)}, u32[]{:S(2)}) collective-permute-start(bf16[256,128]{1,0:T(8,128)(2,1)S(1)} %bitcast.19), channel_id=1, source_target_pairs={{0,3},{1,2},{2,1},{3,0},{4,7},{5,6},{6,5},{7,4},{8,11},{9,10},{10,... | collective-permute-start | bytes 196616 | tf_op jit(solution)/shard_map/ppermute | solution.py:394
  115.2 1.3 %collective-permute-start.15 = (bf16[256,128]{1,0:T(8,128)(2,1)S(1)}, bf16[256,128]{1,0:T(8,128)(2,1)S(1)}, u32[]{:S(2)}, u32[]{:S(2)}) collective-permute-start(bf16[256,128]{1,0:T(8,128)(2,1)S(1)} %bitcast.20), channel_id=1, source_target_pairs={{0,1},{1,0},{2,3},{3,2},{4,5},{5,4},{6,7},{7,6},{8,9},{9,8},{10,11... | collective-permute-start | bytes 196616 | tf_op jit(solution)/shard_map/ppermute | solution.py:394

commit v4 on v2

--- a/solution.py
+++ b/solution.py
@@ -395,6 +395,24 @@
     )(total, *arrivals)
 
 
+def under_each_other_kernel(upper, lower, out):
+    out[: upper.shape[0], :] = upper[...]
+    out[upper.shape[0] :, :] = lower[...]
+
+
+def under_each_other(upper, lower):
+    vmem = pl.BlockSpec(memory_space=pltpu.VMEM)
+    return pl.pallas_call(
+        under_each_other_kernel,
+        out_shape=jax.ShapeDtypeStruct((upper.shape[0] + lower.shape[0], upper.shape[1]), upper.dtype),
+        in_specs=[vmem] * 2,
+        out_specs=vmem,
+        compiler_params=params(12),
+        cost_estimate=small_cost(),
+        name="under_each_other",
+    )(upper, lower)
+
+
 def swap(x, axis, bit):
     return lax.ppermute(x, axis, [(i, i ^ bit) for i in range(lax.axis_size(axis))])
 
@@ -434,9 +452,8 @@
     side = shard // 2 % 2
     kept, swapped, _ = lax.optimization_barrier((kept, swapped, token))
     outgoing = kept[1 - side] + swapped[1 - side]
-    rows = kept[side] + swapped[side]
-    token = after(token, outgoing, rows)
-    swapped = swap(outgoing, "store", 2)
+    token = after(token, outgoing)
+    across = swap(outgoing, "store", 2)
     s01, s11 = base(token, [[0], [1]], [], 1)
 
     token = after(token, s01)
@@ -445,8 +462,8 @@
     b10 = join(token, piece, s00, 0, e0_1, 0)
     token = after(token, b10)
     e1_2 = along_edge(b10, 1)
-    token, swapped = lax.optimization_barrier((token, swapped))
-    rows = rows + swapped
+    token, across, kept, swapped = lax.optimization_barrier((token, across, kept, swapped))
+    rows = kept[side] + swapped[side] + across
     token = after(token, rows)
     near = lax.ppermute(rows, "tensor", [(0, 1), (n - 1, n - 2), (1, 0), (n - 2, n - 1)])
     far = along_edge(rows, 1)
@@ -457,8 +474,7 @@
     token, e0_2 = lax.optimization_barrier((token, e0_2))
     b11 = join(token, block, s01, 0, e0_2, 0, weight=HEAVY)
     token, near = lax.optimization_barrier((after(token, b11), near))
-    e1_3 = along_edge(b11, 1)
-    far_2 = send(near, 1, token)
+    e1_3 = along_edge(under_each_other(b11, near), 1)
     token, e1_2, far = lax.optimization_barrier((token, e1_2, far))
     c20 = join(token, piece, s20, 0, e1_2, 0, far, 0, bundle)
     token = after(token, c20)
@@ -471,10 +487,9 @@
     b20 = join(token, piece, s10_s11, 0, e0_3, 0)
     token = after(token, b20)
     e1_4 = along_edge(b20, 1)
-    token, far_2 = lax.optimization_barrier((token, far_2))
-    last_rows = send(far_2, 2, token)
     token, e1_3 = lax.optimization_barrier((token, e1_3))
-    c21 = join(token, block, s21, 0, e1_3, 0, weight=HEAVY)
+    last_rows = send(e1_3[block:], 2, token)
+    c21 = join(token, block, s21, 0, e1_3, 0, weight=HEAVY // 5)
     token = after(token, c21)
     e2_4 = along_edge(c21, 2)
     token, e2_3 = lax.optimization_barrier((token, e2_3))
@@ -492,12 +507,12 @@
     lora = lora.astype(jnp.bfloat16).reshape(piece - block, -1, width).swapaxes(0, 1).reshape(block, width)
     lora = lora + swap(lora, "store", 1)
     lora = lora + swap(lora, "store", 2)
-    arrays = [s30, s31, rows, near, far, far_2, e2_3, last_rows, e0_4, e1_4]
+    arrays = [s30, s31, rows, near, far, e1_3, e2_3, last_rows, e0_4, e1_4]
     items = [
         (2, 0, [(z, z) for z in range(n)]),
         (3, 0, [(0, 1), (1, 0), (2, 3), (3, 2)]),
         (4, 0, [(1, 2), (2, 1)]),
-        (5, 0, [(1, 3), (2, 0)]),
+        (5, block, [(1, 3), (2, 0)]),
         (6, piece, [(0, 2), (3, 1)]),
         (7, 0, [(0, 3), (3, 0)]),
     ]

time: 117 us -> 119 us (1.017)
  Pallas kernels: 58.4 us -> 56.1 us
  waiting for transfers between devices: 20.3 us -> 22.3 us
  other arithmetic: 1.58 us -> 3.25 us
    pallas_call x4, Pallas kernels: 53.7 us -> 49.5 us  [base_terms(): pl.pallas_call(lambda *refs: base_kernel(line_order(n), groups, inputs_fo...]
    ppermute x14 -> x13, waiting for transfers between devices: 14.8 us -> 18.3 us  [along_edge(): lax.ppermute(x, 'tensor', [(edge, edge + 1), (n - 1 - edge, n - 2 - edge)])]
    ppermute x4, starting transfers between devices: 1.53 us -> 4.28 us  [swap(): lax.ppermute(x, axis, [(i, i ^ bit) for i in range(lax.axis_size(axis))])]
    ppermute x14 -> x13, starting transfers between devices: 28.7 us -> 26.2 us  [along_edge(): lax.ppermute(x, 'tensor', [(edge, edge + 1), (n - 1 - edge, n - 2 - edge)])]
    add x2, other arithmetic: 1.5 us -> 3.18 us  [the longest x1 1.89 us: on_line(): outgoing = kept[1 - side] + swapped[1 - side]]
    ppermute x4, waiting for transfers between devices: 5.5 us -> 3.96 us  [swap(): lax.ppermute(x, axis, [(i, i ^ bit) for i in range(lax.axis_size(axis))])]
  transfers between devices with their start and end apart: 19 -> 18, of which waited for: 6 -> 7; matrix products, arithmetic and copies ran while one was open for 1% -> 3% of each run, Pallas kernels for 38% -> 37%
where the time goes in v4:
time: 119 us
  Pallas kernels  56.1 us (47%)
  starting transfers between devices  35.1 us (29%)
  waiting for transfers between devices  22.3 us (19%)
  other arithmetic  3.25 us (3%)
  local copies, waits for them, and re-layouts  1.44 us (1%)
    pallas_call x4, Pallas kernels, base_terms(): pl.pallas_call(lambda *refs: base_kernel(line_order(n), groups, inputs_fo...  49.5 us
    ppermute x13, starting transfers between devices, along_edge(): lax.ppermute(x, 'tensor', [(edge, edge + 1), (n - 1 - edge, n - 2 - edge)])  26.2 us
    ppermute x13, waiting for transfers between devices, along_edge(): lax.ppermute(x, 'tensor', [(edge, edge + 1), (n - 1 - edge, n - 2 - edge)])  18.3 us
    ppermute x1, starting transfers between devices, on_line(): lax.ppermute(rows, 'tensor', [(0, 1), (n - 1, n - 2), (1, 0), (n - 2, n -...  4.69 us
    ppermute x4, starting transfers between devices, swap(): lax.ppermute(x, axis, [(i, i ^ bit) for i in range(lax.axis_size(axis))])  4.28 us
    ppermute x4, waiting for transfers between devices, swap(): lax.ppermute(x, axis, [(i, i ^ bit) for i in range(lax.axis_size(axis))])  3.96 us
  transfers between devices with their start and end apart: 18, of which 7 were waited for; matrix products, arithmetic and copies ran while one was open for 3% of the time, Pallas kernels for 37%

profile of v4, /device:TPU:0, one launch (start us, length us, event | category | flops | bytes accessed | tf_op | source)
XLA Modules:
  0.0 118.6 jit_solution(8182224068697127012)
XLA Ops:
  0.0 1.4 %concatenate.3.refs_0_ = s32[38]{0:T(128)} concatenate(s32[1]{0:T(128)} %bitcast, s32[1]{0:T(128)} %bitcast.1, s32[4]{0:T(128)} %param.13, s32[16]{0:T(128)} %param.14, s32[16]{0:T(128)} %param.15), dimensions={0} | concatenate | bytes 304 | tf_op jit(solution)/shard_map/concatenate | solution.py:562
  1.4 9.5 %base_terms.4.refs_0_ = bf16[288,1024]{1,0:T(8,128)(2,1)} custom-call(s32[38]{0:T(128)} %concatenate.3.refs_0_, s32[8,128]{1,0:T(8,128)} %bitcast.14, bf16[4,7168,128]{2,1,0:T(8,128)(2,1)} %refs_2_.7, bf16[1024,7168]{1,0:T(8,128)(2,1)} %refs_3_.5, bf16[7168,2048]{1,0:T(8,128)(2,1)} %refs_4_.5), custom_call_target="tpu_custom_call" | custom-call | flops 1000000 | bytes 100000 | tf_op jit(solution)/shard_map/base_terms/pallas_call | solution.py:246
  10.9 1.7 %select_rows.1 = (bf16[2,256,1024]{2,1,0:T(8,128)(2,1)S(1)}, bf16[2,256,1024]{2,1,0:T(8,128)(2,1)}) custom-call(s32[38]{0:T(128)S(1)} %copy-done.3, bf16[4,32,8192]{2,1,0:T(8,128)(2,1)S(1)} %copy-done.1), custom_call_target="tpu_custom_call" | custom-call | flops 1000000 | bytes 100000 | tf_op jit(solution)/shard_map/select_rows/pallas_call | solution.py:282
  12.6 2.6 %collective-permute-start = (bf16[2,256,1024]{2,1,0:T(8,128)(2,1)}, bf16[2,256,1024]{2,1,0:T(8,128)(2,1)}, u32[]{:S(2)}, u32[]{:S(2)}) collective-permute-start(bf16[2,256,1024]{2,1,0:T(8,128)(2,1)} %get-tuple-element.76), channel_id=1, source_target_pairs={{0,1},{1,0},{2,3},{3,2},{4,5},{5,4},{6,7},{7,6},{8,9},{9,8},{10,11... | collective-permute-start | bytes 3145736 | tf_op jit(solution)/shard_map/ppermute | solution.py:417
  15.2 4.3 %collective-permute-start.1 = (bf16[288,1024]{1,0:T(8,128)(2,1)S(1)}, bf16[288,1024]{1,0:T(8,128)(2,1)S(1)}, u32[]{:S(2)}, u32[]{:S(2)}) collective-permute-start(bf16[288,1024]{1,0:T(8,128)(2,1)S(1)} %copy-done), channel_id=1, source_target_pairs={{0,4},{12,8},{1,5},{13,9},{2,6},{14,10},{3,7},{15,11},{16,20},{28,... | collective-permute-start | bytes 1769480 | tf_op jit(solution)/shard_map/ppermute | solution.py:426
  19.6 1.9 %add_bitcast_fusion = bf16[256,1024]{1,0:T(8,128)(2,1)} fusion(bf16[2,256,1024]{2,1,0:T(8,128)(2,1)} %collective-permute-done, s32[]{:T(128)S(6)} %select_n.21, bf16[2,256,1024]{2,1,0:T(8,128)(2,1)S(1)} %get-tuple-element.90), kind=kLoop, calls=%fused_computation.1 | loop fusion | flops 262144 | bytes 1572868 | tf_op jit(solution)/shard_map/add | solution.py:454
  21.5 11.6 %base_terms.5 = (bf16[256,1024]{1,0:T(8,128)(2,1)S(1)}, bf16[256,1024]{1,0:T(8,128)(2,1)S(1)}) custom-call(s32[38]{0:T(128)S(1)} %copy-done.3, bf16[1024,7168]{1,0:T(8,128)(2,1)} %refs_3_.5, bf16[7168,2048]{1,0:T(8,128)(2,1)} %refs_4_.5), custom_call_target="tpu_custom_call" | custom-call | flops 1000000 | bytes 100000 | tf_op jit(solution)/shard_map/base_terms/pallas_call | solution.py:246
  33.1 3.4 %collective-permute-start.3 = (bf16[256,1024]{1,0:T(8,128)(2,1)S(1)}, bf16[256,1024]{1,0:T(8,128)(2,1)}, u32[]{:S(2)}, u32[]{:S(2)}) collective-permute-start(bf16[256,1024]{1,0:T(8,128)(2,1)S(1)} %get-tuple-element.100.refs_0_), channel_id=1, source_target_pairs={{0,4},{12,8},{1,5},{13,9},{2,6},{14,10},{3,7},{15,11},{16,20},{28,... | collective-permute-start | bytes 1572872 | tf_op jit(solution)/shard_map/ppermute | solution.py:426
  36.7 0.7 collective-permute-start.5
  37.4 1.3 %bitcast_add_fusion.refs_5_ = bf16[256,1024]{1,0:T(8,128)(2,1)S(1)} fusion(bf16[256,1024]{1,0:T(8,128)(2,1)} %collective-permute-done.2, bf16[2,256,1024]{2,1,0:T(8,128)(2,1)} %collective-permute-done, s32[]{:T(128)S(6)} %select_n.22, bf16[2,256,1024]{2,1,0:T(8,128)(2,1)S(1)} %get-tuple-element.90), kind=kLoop, calls=%fused_computation | loop fusion | flops 524288 | bytes 2097156 | tf_op jit(solution)/shard_map/add | solution.py:466
  39.4 4.7 %collective-permute-start.4 = (bf16[256,1024]{1,0:T(8,128)(2,1)S(1)}, bf16[256,1024]{1,0:T(8,128)(2,1)S(1)}, u32[]{:S(2)}, u32[]{:S(2)}) collective-permute-start(bf16[256,1024]{1,0:T(8,128)(2,1)S(1)} %bitcast_add_fusion.refs_5_), channel_id=1, source_target_pairs={{0,4},{12,8},{4,0},{8,12},{1,5},{13,9},{5,1},{9,13},{2,6},{14,10},... | collective-permute-start | bytes 1572872 | tf_op jit(solution)/shard_map/ppermute | solution.py:468
  44.0 16.3 %base_terms.6 = (bf16[544,1024]{1,0:T(8,128)(2,1)S(1)}, bf16[288,1024]{1,0:T(8,128)(2,1)S(1)}, bf16[256,1024]{1,0:T(8,128)(2,1)S(1)}) custom-call(s32[38]{0:T(128)S(1)} %copy-done.3, s32[8,128]{1,0:T(8,128)S(1)} %bitcast.15, bf16[4,7168,128]{2,1,0:T(8,128)(2,1)} %refs_2_.7, bf16[1024,7168]{1,0:T(8,128)(2,1)} %refs_3_.5, bf16[7168,2048]{1,0:T(8,128)(2,1)} %refs_4_.5, ...), custom_call_target="tpu_custom_call" | custom-call | flops 1000000 | bytes 100000 | tf_op jit(solution)/shard_map/base_terms/pallas_call | solution.py:246
  60.3 2.0 %collective-permute-start.7 = (bf16[544,1024]{1,0:T(8,128)(2,1)S(1)}, bf16[544,1024]{1,0:T(8,128)(2,1)S(1)}, u32[]{:S(2)}, u32[]{:S(2)}) collective-permute-start(bf16[544,1024]{1,0:T(8,128)(2,1)S(1)} %get-tuple-element.127.refs_0_), channel_id=1, source_target_pairs={{0,4},{12,8},{1,5},{13,9},{2,6},{14,10},{3,7},{15,11},{16,20},{28,... | collective-permute-start | bytes 3342344 | tf_op jit(solution)/shard_map/ppermute | solution.py:426
  62.3 1.2 join.7.upper
  63.6 0.7 collective-permute-start.8
  64.5 1.3 %collective-permute-start.9 = (bf16[544,1024]{1,0:T(8,128)(2,1)S(1)}, bf16[544,1024]{1,0:T(8,128)(2,1)S(1)}, u32[]{:S(2)}, u32[]{:S(2)}) collective-permute-start(bf16[544,1024]{1,0:T(8,128)(2,1)S(1)} %join.8), channel_id=1, source_target_pairs={{8,12},{4,0},{9,13},{5,1},{10,14},{6,2},{11,15},{7,3},{24,28},{20,... | collective-permute-start | bytes 3342344 | tf_op jit(solution)/shard_map/ppermute | solution.py:426
  65.8 12.1 %base_terms.7 = (bf16[256,1024]{1,0:T(8,128)(2,1)S(1)}, bf16[288,1024]{1,0:T(8,128)(2,1)S(1)}) custom-call(s32[38]{0:T(128)S(1)} %copy-done.3, s32[8,128]{1,0:T(8,128)S(1)} %bitcast.16, bf16[4,7168,128]{2,1,0:T(8,128)(2,1)} %refs_2_.7, bf16[1024,7168]{1,0:T(8,128)(2,1)} %refs_3_.5, bf16[7168,2048]{1,0:T(8,128)(2,1)} %refs_4_.5), custom_call_target="tpu_custom_call" | custom-call | flops 1000000 | bytes 100000 | tf_op jit(solution)/shard_map/base_terms/pallas_call | solution.py:246
  77.9 4.7 %collective-permute-start.10 = (bf16[288,1024]{1,0:T(8,128)(2,1)S(1)}, bf16[288,1024]{1,0:T(8,128)(2,1)S(1)}, u32[]{:S(2)}, u32[]{:S(2)}) collective-permute-start(bf16[288,1024]{1,0:T(8,128)(2,1)S(1)} %get-tuple-element.130.refs_0_), channel_id=1, source_target_pairs={{0,4},{12,8},{1,5},{13,9},{2,6},{14,10},{3,7},{15,11},{16,20},{28,... | collective-permute-start | bytes 1769480 | tf_op jit(solution)/shard_map/ppermute | solution.py:426
  82.6 3.8 %collective-permute-done.7.refs_1_ = bf16[544,1024]{1,0:T(8,128)(2,1)S(1)} collective-permute-done((bf16[544,1024]{1,0:T(8,128)(2,1)S(1)}, bf16[544,1024]{1,0:T(8,128)(2,1)S(1)}, u32[]{:S(2)}, u32[]{:S(2)}) %collective-permute-start.7) | collective-permute-done | bytes 1114144 | tf_op jit(solution)/shard_map/ppermute | solution.py:426
  86.5 0.7 collective-permute-start.11
  87.3 1.3 %collective-permute-start.12 = (bf16[256,1024]{1,0:T(8,128)(2,1)S(1)}, bf16[256,1024]{1,0:T(8,128)(2,1)S(1)}, u32[]{:S(2)}, u32[]{:S(2)}) collective-permute-start(bf16[256,1024]{1,0:T(8,128)(2,1)S(1)} %slice.15), channel_id=1, source_target_pairs={{8,12},{4,0},{9,13},{5,1},{10,14},{6,2},{11,15},{7,3},{24,28},{20,... | collective-permute-start | bytes 1572872 | tf_op jit(solution)/shard_map/ppermute | solution.py:426
  88.7 1.3 %collective-permute-start.17 = (bf16[256,1024]{1,0:T(8,128)(2,1)S(1)}, bf16[256,1024]{1,0:T(8,128)(2,1)S(1)}, u32[]{:S(2)}, u32[]{:S(2)}) collective-permute-start(bf16[256,1024]{1,0:T(8,128)(2,1)S(1)} %join.10), channel_id=1, source_target_pairs={{8,12},{4,0},{9,13},{5,1},{10,14},{6,2},{11,15},{7,3},{24,28},{20,... | collective-permute-start | bytes 1572872 | tf_op jit(solution)/shard_map/ppermute | solution.py:426
  90.0 3.3 %collective-permute-done.9.refs_9_ = bf16[544,1024]{1,0:T(8,128)(2,1)S(1)} collective-permute-done((bf16[544,1024]{1,0:T(8,128)(2,1)S(1)}, bf16[544,1024]{1,0:T(8,128)(2,1)S(1)}, u32[]{:S(2)}, u32[]{:S(2)}) %collective-permute-start.9) | collective-permute-done | bytes 1114144 | tf_op jit(solution)/shard_map/ppermute | solution.py:426
  94.2 4.9 %collective-permute-done.10.refs_11_ = bf16[288,1024]{1,0:T(8,128)(2,1)S(1)} collective-permute-done((bf16[288,1024]{1,0:T(8,128)(2,1)S(1)}, bf16[288,1024]{1,0:T(8,128)(2,1)S(1)}, u32[]{:S(2)}, u32[]{:S(2)}) %collective-permute-start.10) | collective-permute-done | bytes 589856 | tf_op jit(solution)/shard_map/ppermute | solution.py:426
  99.0 4.4 %collective-permute-start.15 = (bf16[256,1024]{1,0:T(8,128)(2,1)S(1)}, bf16[256,1024]{1,0:T(8,128)(2,1)S(1)}, u32[]{:S(2)}, u32[]{:S(2)}) collective-permute-start(bf16[256,1024]{1,0:T(8,128)(2,1)S(1)} %get-tuple-element.142.refs_0_), channel_id=1, source_target_pairs={{0,4},{12,8},{1,5},{13,9},{2,6},{14,10},{3,7},{15,11},{16,20},{28,... | collective-permute-start | bytes 1572872 | tf_op jit(solution)/shard_map/ppermute | solution.py:426
  103.5 4.4 %collective-permute-done.12.refs_10_ = bf16[256,1024]{1,0:T(8,128)(2,1)S(1)} collective-permute-done((bf16[256,1024]{1,0:T(8,128)(2,1)S(1)}, bf16[256,1024]{1,0:T(8,128)(2,1)S(1)}, u32[]{:S(2)}, u32[]{:S(2)}) %collective-permute-start.12) | collective-permute-done | bytes 524320 | tf_op jit(solution)/shard_map/ppermute | solution.py:426
  108.0 1.2 %collective-permute-done.13 = bf16[256,128]{1,0:T(8,128)(2,1)S(1)} collective-permute-done((bf16[256,128]{1,0:T(8,128)(2,1)S(1)}, bf16[256,128]{1,0:T(8,128)(2,1)S(1)}, u32[]{:S(2)}, u32[]{:S(2)}) %collective-permute-start.13) | collective-permute-done | bytes 65568 | tf_op jit(solution)/shard_map/ppermute | solution.py:417
  109.3 1.6 %collective-permute-start.14 = (bf16[256,128]{1,0:T(8,128)(2,1)S(1)}, bf16[256,128]{1,0:T(8,128)(2,1)S(1)}, u32[]{:S(2)}, u32[]{:S(2)}) collective-permute-start(bf16[256,128]{1,0:T(8,128)(2,1)S(1)} %bitcast_add_fusion.1), channel_id=1, source_target_pairs={{0,2},{1,3},{2,0},{3,1},{4,6},{5,7},{6,4},{7,5},{8,10},{9,11},{10,... | collective-permute-start | bytes 196616 | tf_op jit(solution)/shard_map/ppermute | solution.py:417
  110.9 2.7 %collective-permute-done.14 = bf16[256,128]{1,0:T(8,128)(2,1)S(1)} collective-permute-done((bf16[256,128]{1,0:T(8,128)(2,1)S(1)}, bf16[256,128]{1,0:T(8,128)(2,1)S(1)}, u32[]{:S(2)}, u32[]{:S(2)}) %collective-permute-start.14) | collective-permute-done | bytes 65568 | tf_op jit(solution)/shard_map/ppermute | solution.py:417
  113.6 1.8 %finish.1.total = bf16[256,2048]{1,0:T(8,128)(2,1)S(1)} custom-call(s32[38]{0:T(128)S(1)} %copy-done.3, s32[8,128]{1,0:T(8,128)S(1)} %bitcast.17, bf16[256,128]{1,0:T(8,128)(2,1)S(1)} %add.56.refs_2_, bf16[256,1024]{1,0:T(8,128)(2,1)S(1)} %get-tuple-element.140.refs_3_, bf16[288,1024]{1,0:T(8,128)(2,1)S(1)} %get-tuple-element.135.refs_4_, ...), custom_call_target="tpu_custom_call" | custom-call | flops 1000000 | bytes 100000 | tf_op jit(solution)/shard_map/finish/pallas_call | solution.py:338
  115.4 1.9 %collective-permute-done.17.refs_2_ = bf16[256,1024]{1,0:T(8,128)(2,1)S(1)} collective-permute-done((bf16[256,1024]{1,0:T(8,128)(2,1)S(1)}, bf16[256,1024]{1,0:T(8,128)(2,1)S(1)}, u32[]{:S(2)}, u32[]{:S(2)}) %collective-permute-start.17) | collective-permute-done | bytes 524320 | tf_op jit(solution)/shard_map/ppermute | solution.py:426
  117.4 1.3 %add_last.1 = bf16[256,2048]{1,0:T(8,128)(2,1)} custom-call(bf16[256,2048]{1,0:T(8,128)(2,1)S(1)} %finish.1.total, bf16[256,1024]{1,0:T(8,128)(2,1)S(1)} %collective-permute-done.15.refs_0_, bf16[256,1024]{1,0:T(8,128)(2,1)S(1)} %collective-permute-done.16.refs_1_, bf16[256,1024]{1,0:T(8,128)(2,1)S(1)} %collective-permute-done.17.refs_2_), custom_call_target="tpu_custom_call" | custom-call | flops 1000000 | bytes 100000 | tf_op jit(solution)/shard_map/add_last/pallas_call | solution.py:387
  (35 shorter events, 2.4 us)
Async XLA Ops:
  1.4 9.5 %copy-start.1 = (bf16[4,32,8192]{2,1,0:T(8,128)(2,1)S(1)}, bf16[4,32,8192]{2,1,0:T(8,128)(2,1)}, u32[]{:S(2)}) copy-start(bf16[4,32,8192]{2,1,0:T(8,128)(2,1)} %refs_1_.2) | copy-start | bytes 6291460
  1.4 9.5 %copy-start.3 = (s32[38]{0:T(128)S(1)}, s32[38]{0:T(128)}, u32[]{:S(2)}) copy-start(s32[38]{0:T(128)} %concatenate.3.refs_0_) | copy-start | bytes 460
  10.9 4.3 %copy-start = (bf16[288,1024]{1,0:T(8,128)(2,1)S(1)}, bf16[288,1024]{1,0:T(8,128)(2,1)}, u32[]{:S(2)}) copy-start(bf16[288,1024]{1,0:T(8,128)(2,1)} %base_terms.4.refs_0_) | copy-start | bytes 1769476
  12.6 7.0 %collective-permute-start = (bf16[2,256,1024]{2,1,0:T(8,128)(2,1)}, bf16[2,256,1024]{2,1,0:T(8,128)(2,1)}, u32[]{:S(2)}, u32[]{:S(2)}) collective-permute-start(bf16[2,256,1024]{2,1,0:T(8,128)(2,1)} %get-tuple-element.76), channel_id=1, source_target_pairs={{0,1},{1,0},{2,3},{3,2},{4,5},{5,4},{6,7},{7,6},{8,9},{9,8},{10,11... | collective-permute-start | bytes 3145736 | tf_op jit(solution)/shard_map/ppermute | solution.py:417
  15.2 21.3 %collective-permute-start.1 = (bf16[288,1024]{1,0:T(8,128)(2,1)S(1)}, bf16[288,1024]{1,0:T(8,128)(2,1)S(1)}, u32[]{:S(2)}, u32[]{:S(2)}) collective-permute-start(bf16[288,1024]{1,0:T(8,128)(2,1)S(1)} %copy-done), channel_id=1, source_target_pairs={{0,4},{12,8},{1,5},{13,9},{2,6},{14,10},{3,7},{15,11},{16,20},{28,... | collective-permute-start | bytes 1769480 | tf_op jit(solution)/shard_map/ppermute | solution.py:426
  21.5 15.8 %collective-permute-start.2 = (bf16[256,1024]{1,0:T(8,128)(2,1)}, bf16[256,1024]{1,0:T(8,128)(2,1)}, u32[]{:S(2)}, u32[]{:S(2)}) collective-permute-start(bf16[256,1024]{1,0:T(8,128)(2,1)} %add_bitcast_fusion), channel_id=1, source_target_pairs={{0,2},{1,3},{2,0},{3,1},{4,6},{5,7},{6,4},{7,5},{8,10},{9,11},{10,... | collective-permute-start | bytes 1572872 | tf_op jit(solution)/shard_map/ppermute | solution.py:417
  33.1 27.2 %collective-permute-start.3 = (bf16[256,1024]{1,0:T(8,128)(2,1)S(1)}, bf16[256,1024]{1,0:T(8,128)(2,1)}, u32[]{:S(2)}, u32[]{:S(2)}) collective-permute-start(bf16[256,1024]{1,0:T(8,128)(2,1)S(1)} %get-tuple-element.100.refs_0_), channel_id=1, source_target_pairs={{0,4},{12,8},{1,5},{13,9},{2,6},{14,10},{3,7},{15,11},{16,20},{28,... | collective-permute-start | bytes 1572872 | tf_op jit(solution)/shard_map/ppermute | solution.py:426
  36.6 7.4 %copy-start.2 = (s32[1024]{0:T(1024)S(1)}, s32[1024]{0:T(1024)}, u32[]{:S(2)}) copy-start(s32[1024]{0:T(1024)} %param.12) | copy-start | bytes 12292
  36.7 27.7 %collective-permute-start.5 = (bf16[288,1024]{1,0:T(8,128)(2,1)S(1)}, bf16[288,1024]{1,0:T(8,128)(2,1)S(1)}, u32[]{:S(2)}, u32[]{:S(2)}) collective-permute-start(bf16[288,1024]{1,0:T(8,128)(2,1)S(1)} %join.6), channel_id=1, source_target_pairs={{4,8},{8,4},{5,9},{9,5},{6,10},{10,6},{7,11},{11,7},{20,24},{24,20... | collective-permute-start | bytes 1769480 | tf_op jit(solution)/shard_map/ppermute | solution.py:426
  38.7 25.7 %collective-permute-start.6 = (bf16[256,1024]{1,0:T(8,128)(2,1)S(1)}, bf16[256,1024]{1,0:T(8,128)(2,1)S(1)}, u32[]{:S(2)}, u32[]{:S(2)}) collective-permute-start(bf16[256,1024]{1,0:T(8,128)(2,1)S(1)} %bitcast_add_fusion.refs_5_), channel_id=1, source_target_pairs={{4,8},{8,4},{5,9},{9,5},{6,10},{10,6},{7,11},{11,7},{20,24},{24,20... | collective-permute-start | bytes 1572872 | tf_op jit(solution)/shard_map/ppermute | solution.py:426
  39.4 24.2 %collective-permute-start.4 = (bf16[256,1024]{1,0:T(8,128)(2,1)S(1)}, bf16[256,1024]{1,0:T(8,128)(2,1)S(1)}, u32[]{:S(2)}, u32[]{:S(2)}) collective-permute-start(bf16[256,1024]{1,0:T(8,128)(2,1)S(1)} %bitcast_add_fusion.refs_5_), channel_id=1, source_target_pairs={{0,4},{12,8},{4,0},{8,12},{1,5},{13,9},{5,1},{9,13},{2,6},{14,10},... | collective-permute-start | bytes 1572872 | tf_op jit(solution)/shard_map/ppermute | solution.py:468
  60.3 26.1 %collective-permute-start.7 = (bf16[544,1024]{1,0:T(8,128)(2,1)S(1)}, bf16[544,1024]{1,0:T(8,128)(2,1)S(1)}, u32[]{:S(2)}, u32[]{:S(2)}) collective-permute-start(bf16[544,1024]{1,0:T(8,128)(2,1)S(1)} %get-tuple-element.127.refs_0_), channel_id=1, source_target_pairs={{0,4},{12,8},{1,5},{13,9},{2,6},{14,10},{3,7},{15,11},{16,20},{28,... | collective-permute-start | bytes 3342344 | tf_op jit(solution)/shard_map/ppermute | solution.py:426
  63.6 23.6 %collective-permute-start.8 = (bf16[512,1024]{1,0:T(8,128)(2,1)S(1)}, bf16[512,1024]{1,0:T(8,128)(2,1)S(1)}, u32[]{:S(2)}, u32[]{:S(2)}) collective-permute-start(bf16[512,1024]{1,0:T(8,128)(2,1)S(1)} %under_each_other.1), channel_id=1, source_target_pairs={{4,8},{8,4},{5,9},{9,5},{6,10},{10,6},{7,11},{11,7},{20,24},{24,20... | collective-permute-start | bytes 3145736 | tf_op jit(solution)/shard_map/ppermute | solution.py:426
  64.5 28.8 %collective-permute-start.9 = (bf16[544,1024]{1,0:T(8,128)(2,1)S(1)}, bf16[544,1024]{1,0:T(8,128)(2,1)S(1)}, u32[]{:S(2)}, u32[]{:S(2)}) collective-permute-start(bf16[544,1024]{1,0:T(8,128)(2,1)S(1)} %join.8), channel_id=1, source_target_pairs={{8,12},{4,0},{9,13},{5,1},{10,14},{6,2},{11,15},{7,3},{24,28},{20,... | collective-permute-start | bytes 3342344 | tf_op jit(solution)/shard_map/ppermute | solution.py:426
  77.9 21.1 %collective-permute-start.10 = (bf16[288,1024]{1,0:T(8,128)(2,1)S(1)}, bf16[288,1024]{1,0:T(8,128)(2,1)S(1)}, u32[]{:S(2)}, u32[]{:S(2)}) collective-permute-start(bf16[288,1024]{1,0:T(8,128)(2,1)S(1)} %get-tuple-element.130.refs_0_), channel_id=1, source_target_pairs={{0,4},{12,8},{1,5},{13,9},{2,6},{14,10},{3,7},{15,11},{16,20},{28,... | collective-permute-start | bytes 1769480 | tf_op jit(solution)/shard_map/ppermute | solution.py:426
  86.5 16.9 %collective-permute-start.11 = (bf16[288,1024]{1,0:T(8,128)(2,1)S(1)}, bf16[288,1024]{1,0:T(8,128)(2,1)S(1)}, u32[]{:S(2)}, u32[]{:S(2)}) collective-permute-start(bf16[288,1024]{1,0:T(8,128)(2,1)S(1)} %join.9), channel_id=1, source_target_pairs={{4,8},{8,4},{5,9},{9,5},{6,10},{10,6},{7,11},{11,7},{20,24},{24,20... | collective-permute-start | bytes 1769480 | tf_op jit(solution)/shard_map/ppermute | solution.py:426
  87.3 20.6 %collective-permute-start.12 = (bf16[256,1024]{1,0:T(8,128)(2,1)S(1)}, bf16[256,1024]{1,0:T(8,128)(2,1)S(1)}, u32[]{:S(2)}, u32[]{:S(2)}) collective-permute-start(bf16[256,1024]{1,0:T(8,128)(2,1)S(1)} %slice.15), channel_id=1, source_target_pairs={{8,12},{4,0},{9,13},{5,1},{10,14},{6,2},{11,15},{7,3},{24,28},{20,... | collective-permute-start | bytes 1572872 | tf_op jit(solution)/shard_map/ppermute | solution.py:426
  88.7 28.6 %collective-permute-start.17 = (bf16[256,1024]{1,0:T(8,128)(2,1)S(1)}, bf16[256,1024]{1,0:T(8,128)(2,1)S(1)}, u32[]{:S(2)}, u32[]{:S(2)}) collective-permute-start(bf16[256,1024]{1,0:T(8,128)(2,1)S(1)} %join.10), channel_id=1, source_target_pairs={{8,12},{4,0},{9,13},{5,1},{10,14},{6,2},{11,15},{7,3},{24,28},{20,... | collective-permute-start | bytes 1572872 | tf_op jit(solution)/shard_map/ppermute | solution.py:426
  93.5 23.9 %collective-permute-start.16 = (bf16[256,1024]{1,0:T(8,128)(2,1)S(1)}, bf16[256,1024]{1,0:T(8,128)(2,1)S(1)}, u32[]{:S(2)}, u32[]{:S(2)}) collective-permute-start(bf16[256,1024]{1,0:T(8,128)(2,1)S(1)} %join.11), channel_id=1, source_target_pairs={{4,8},{8,4},{5,9},{9,5},{6,10},{10,6},{7,11},{11,7},{20,24},{24,20... | collective-permute-start | bytes 1572872 | tf_op jit(solution)/shard_map/ppermute | solution.py:426
  99.0 18.3 %collective-permute-start.15 = (bf16[256,1024]{1,0:T(8,128)(2,1)S(1)}, bf16[256,1024]{1,0:T(8,128)(2,1)S(1)}, u32[]{:S(2)}, u32[]{:S(2)}) collective-permute-start(bf16[256,1024]{1,0:T(8,128)(2,1)S(1)} %get-tuple-element.142.refs_0_), channel_id=1, source_target_pairs={{0,4},{12,8},{1,5},{13,9},{2,6},{14,10},{3,7},{15,11},{16,20},{28,... | collective-permute-start | bytes 1572872 | tf_op jit(solution)/shard_map/ppermute | solution.py:426
  108.0 1.3 %collective-permute-start.13 = (bf16[256,128]{1,0:T(8,128)(2,1)S(1)}, bf16[256,128]{1,0:T(8,128)(2,1)S(1)}, u32[]{:S(2)}, u32[]{:S(2)}) collective-permute-start(bf16[256,128]{1,0:T(8,128)(2,1)S(1)} %bitcast.18), channel_id=1, source_target_pairs={{0,1},{1,0},{2,3},{3,2},{4,5},{5,4},{6,7},{7,6},{8,9},{9,8},{10,11... | collective-permute-start | bytes 196616 | tf_op jit(solution)/shard_map/ppermute | solution.py:417
  109.3 4.3 %collective-permute-start.14 = (bf16[256,128]{1,0:T(8,128)(2,1)S(1)}, bf16[256,128]{1,0:T(8,128)(2,1)S(1)}, u32[]{:S(2)}, u32[]{:S(2)}) collective-permute-start(bf16[256,128]{1,0:T(8,128)(2,1)S(1)} %bitcast_add_fusion.1), channel_id=1, source_target_pairs={{0,2},{1,3},{2,0},{3,1},{4,6},{5,7},{6,4},{7,5},{8,10},{9,11},{10,... | collective-permute-start | bytes 196616 | tf_op jit(solution)/shard_map/ppermute | solution.py:417

commit v5 on v4

--- a/solution.py
+++ b/solution.py
@@ -452,7 +452,8 @@
     side = shard // 2 % 2
     kept, swapped, _ = lax.optimization_barrier((kept, swapped, token))
     outgoing = kept[1 - side] + swapped[1 - side]
-    token = after(token, outgoing)
+    rows = kept[side] + swapped[side]
+    token = after(token, outgoing, rows)
     across = swap(outgoing, "store", 2)
     s01, s11 = base(token, [[0], [1]], [], 1)
 
@@ -462,8 +463,8 @@
     b10 = join(token, piece, s00, 0, e0_1, 0)
     token = after(token, b10)
     e1_2 = along_edge(b10, 1)
-    token, across, kept, swapped = lax.optimization_barrier((token, across, kept, swapped))
-    rows = kept[side] + swapped[side] + across
+    token, across = lax.optimization_barrier((token, across))
+    rows = rows + across
     token = after(token, rows)
     near = lax.ppermute(rows, "tensor", [(0, 1), (n - 1, n - 2), (1, 0), (n - 2, n - 1)])
     far = along_edge(rows, 1)

time: 119 us -> 117 us (0.983)
  Pallas kernels: 56.1 us -> 58.5 us
  starting transfers between devices: 35.1 us -> 32.9 us
  other arithmetic: 3.25 us -> 1.58 us
    pallas_call x4, Pallas kernels: 49.5 us -> 53.7 us  [base_terms(): pl.pallas_call(lambda *refs: base_kernel(line_order(n), groups, inputs_fo...]
    ppermute x4, starting transfers between devices: 4.28 us -> 0.28 us  [swap(): lax.ppermute(x, axis, [(i, i ^ bit) for i in range(lax.axis_size(axis))])]
    ppermute x13, waiting for transfers between devices: 18.3 us -> 16.6 us  [along_edge(): lax.ppermute(x, 'tensor', [(edge, edge + 1), (n - 1 - edge, n - 2 - edge)])]
    add x2, other arithmetic: 3.18 us -> 1.51 us  [the longest x1 1.31 us: on_line(): rows = kept[side] + swapped[side]]
    ppermute x4, waiting for transfers between devices: 3.96 us -> 5.5 us  [swap(): lax.ppermute(x, axis, [(i, i ^ bit) for i in range(lax.axis_size(axis))])]
  transfers between devices with their start and end apart: 18 -> 18, of which waited for: 7 -> 6; matrix products, arithmetic and copies ran while one was open for 3% -> 1% of each run, Pallas kernels for 37% -> 38%
where the time goes in v5:
time: 117 us
  Pallas kernels  58.5 us (50%)
  starting transfers between devices  32.9 us (28%)
  waiting for transfers between devices  22.1 us (19%)
  other arithmetic  1.58 us (1%)
  local copies, waits for them, and re-layouts  1.5 us (1%)
    pallas_call x4, Pallas kernels, base_terms(): pl.pallas_call(lambda *refs: base_kernel(line_order(n), groups, inputs_fo...  53.7 us
    ppermute x13, starting transfers between devices, along_edge(): lax.ppermute(x, 'tensor', [(edge, edge + 1), (n - 1 - edge, n - 2 - edge)])  27 us
    ppermute x13, waiting for transfers between devices, along_edge(): lax.ppermute(x, 'tensor', [(edge, edge + 1), (n - 1 - edge, n - 2 - edge)])  16.6 us
    ppermute x1, starting transfers between devices, on_line(): lax.ppermute(rows, 'tensor', [(0, 1), (n - 1, n - 2), (1, 0), (n - 2, n -...  5.6 us
    ppermute x4, waiting for transfers between devices, swap(): lax.ppermute(x, axis, [(i, i ^ bit) for i in range(lax.axis_size(axis))])  5.5 us
  transfers between devices with their start and end apart: 18, of which 6 were waited for; matrix products, arithmetic and copies ran while one was open for 1% of the time, Pallas kernels for 38%

profile of v5, /device:TPU:0, one launch (start us, length us, event | category | flops | bytes accessed | tf_op | source)
XLA Modules:
  0.0 117.0 jit_solution(5219030952150022088)
XLA Ops:
  0.0 1.3 %concatenate.3.refs_0_ = s32[38]{0:T(128)} concatenate(s32[1]{0:T(128)} %bitcast, s32[1]{0:T(128)} %bitcast.1, s32[4]{0:T(128)} %param.13, s32[16]{0:T(128)} %param.14, s32[16]{0:T(128)} %param.15), dimensions={0} | concatenate | bytes 304 | tf_op jit(solution)/shard_map/concatenate | solution.py:563
  1.3 11.6 %base_terms.4.refs_0_ = bf16[288,1024]{1,0:T(8,128)(2,1)} custom-call(s32[38]{0:T(128)} %concatenate.3.refs_0_, s32[8,128]{1,0:T(8,128)} %bitcast.14, bf16[4,7168,128]{2,1,0:T(8,128)(2,1)} %refs_2_.7, bf16[1024,7168]{1,0:T(8,128)(2,1)} %refs_3_.5, bf16[7168,2048]{1,0:T(8,128)(2,1)} %refs_4_.5), custom_call_target="tpu_custom_call" | custom-call | flops 1000000 | bytes 100000 | tf_op jit(solution)/shard_map/base_terms/pallas_call | solution.py:246
  12.9 0.8 select_rows.1
  13.8 0.1 copy-done
  13.9 4.9 %collective-permute-start.1 = (bf16[288,1024]{1,0:T(8,128)(2,1)S(1)}, bf16[288,1024]{1,0:T(8,128)(2,1)S(1)}, u32[]{:S(2)}, u32[]{:S(2)}) collective-permute-start(bf16[288,1024]{1,0:T(8,128)(2,1)S(1)} %copy-done), channel_id=1, source_target_pairs={{0,4},{12,8},{1,5},{13,9},{2,6},{14,10},{3,7},{15,11},{16,20},{28,... | collective-permute-start | bytes 1769480 | tf_op jit(solution)/shard_map/ppermute | solution.py:426
  18.9 1.3 %add_bitcast_fusion = (bf16[256,1024]{1,0:T(8,128)(2,1)S(1)}, bf16[256,1024]{1,0:T(8,128)(2,1)S(1)}) fusion(bf16[2,256,1024]{2,1,0:T(8,128)(2,1)} %collective-permute-done, s32[]{:T(128)S(6)} %select_n.22, bf16[2,256,1024]{2,1,0:T(8,128)(2,1)S(1)} %get-tuple-element.77, s32[]{:T(128)S(6)} %select_n.21), kind=kLoop, calls=%fused_computation | loop fusion | flops 524288 | bytes 3145736 | tf_op jit(solution)/shard_map/add | solution.py:455
  20.3 11.6 %base_terms.5 = (bf16[256,1024]{1,0:T(8,128)(2,1)S(1)}, bf16[256,1024]{1,0:T(8,128)(2,1)S(1)}) custom-call(s32[38]{0:T(128)S(1)} %copy-done.3, bf16[1024,7168]{1,0:T(8,128)(2,1)} %refs_3_.5, bf16[7168,2048]{1,0:T(8,128)(2,1)} %refs_4_.5), custom_call_target="tpu_custom_call" | custom-call | flops 1000000 | bytes 100000 | tf_op jit(solution)/shard_map/base_terms/pallas_call | solution.py:246
  31.9 2.6 %collective-permute-start.3 = (bf16[256,1024]{1,0:T(8,128)(2,1)S(1)}, bf16[256,1024]{1,0:T(8,128)(2,1)S(1)}, u32[]{:S(2)}, u32[]{:S(2)}) collective-permute-start(bf16[256,1024]{1,0:T(8,128)(2,1)S(1)} %get-tuple-element.96.refs_0_), channel_id=1, source_target_pairs={{0,4},{12,8},{1,5},{13,9},{2,6},{14,10},{3,7},{15,11},{16,20},{28,... | collective-permute-start | bytes 1572872 | tf_op jit(solution)/shard_map/ppermute | solution.py:426
  34.7 0.7 collective-permute-start.5
  35.4 0.2 add.51.refs_5_
  35.6 0.7 collective-permute-start.6
  36.3 5.6 %collective-permute-start.4 = (bf16[256,1024]{1,0:T(8,128)(2,1)S(1)}, bf16[256,1024]{1,0:T(8,128)(2,1)S(1)}, u32[]{:S(2)}, u32[]{:S(2)}) collective-permute-start(bf16[256,1024]{1,0:T(8,128)(2,1)S(1)} %add.51.refs_5_), channel_id=1, source_target_pairs={{0,4},{12,8},{4,0},{8,12},{1,5},{13,9},{5,1},{9,13},{2,6},{14,10},... | collective-permute-start | bytes 1572872 | tf_op jit(solution)/shard_map/ppermute | solution.py:469
  41.9 18.5 %base_terms.6 = (bf16[544,1024]{1,0:T(8,128)(2,1)S(1)}, bf16[288,1024]{1,0:T(8,128)(2,1)S(1)}, bf16[256,1024]{1,0:T(8,128)(2,1)S(1)}) custom-call(s32[38]{0:T(128)S(1)} %copy-done.3, s32[8,128]{1,0:T(8,128)S(1)} %bitcast.15, bf16[4,7168,128]{2,1,0:T(8,128)(2,1)} %refs_2_.7, bf16[1024,7168]{1,0:T(8,128)(2,1)} %refs_3_.5, bf16[7168,2048]{1,0:T(8,128)(2,1)} %refs_4_.5, ...), custom_call_target="tpu_custom_call" | custom-call | flops 1000000 | bytes 100000 | tf_op jit(solution)/shard_map/base_terms/pallas_call | solution.py:246
  60.4 1.4 %collective-permute-start.7 = (bf16[544,1024]{1,0:T(8,128)(2,1)S(1)}, bf16[544,1024]{1,0:T(8,128)(2,1)S(1)}, u32[]{:S(2)}, u32[]{:S(2)}) collective-permute-start(bf16[544,1024]{1,0:T(8,128)(2,1)S(1)} %get-tuple-element.123.refs_0_), channel_id=1, source_target_pairs={{0,4},{12,8},{1,5},{13,9},{2,6},{14,10},{3,7},{15,11},{16,20},{28,... | collective-permute-start | bytes 3342344 | tf_op jit(solution)/shard_map/ppermute | solution.py:426
  62.0 0.7 collective-permute-start.8
  62.8 0.2 join.8
  62.9 1.3 %collective-permute-start.9 = (bf16[544,1024]{1,0:T(8,128)(2,1)S(1)}, bf16[544,1024]{1,0:T(8,128)(2,1)S(1)}, u32[]{:S(2)}, u32[]{:S(2)}) collective-permute-start(bf16[544,1024]{1,0:T(8,128)(2,1)S(1)} %join.8), channel_id=1, source_target_pairs={{8,12},{4,0},{9,13},{5,1},{10,14},{6,2},{11,15},{7,3},{24,28},{20,... | collective-permute-start | bytes 3342344 | tf_op jit(solution)/shard_map/ppermute | solution.py:426
  64.2 12.1 %base_terms.7 = (bf16[256,1024]{1,0:T(8,128)(2,1)S(1)}, bf16[288,1024]{1,0:T(8,128)(2,1)S(1)}) custom-call(s32[38]{0:T(128)S(1)} %copy-done.3, s32[8,128]{1,0:T(8,128)S(1)} %bitcast.16, bf16[4,7168,128]{2,1,0:T(8,128)(2,1)} %refs_2_.7, bf16[1024,7168]{1,0:T(8,128)(2,1)} %refs_3_.5, bf16[7168,2048]{1,0:T(8,128)(2,1)} %refs_4_.5), custom_call_target="tpu_custom_call" | custom-call | flops 1000000 | bytes 100000 | tf_op jit(solution)/shard_map/base_terms/pallas_call | solution.py:246
  76.3 6.3 %collective-permute-start.10 = (bf16[288,1024]{1,0:T(8,128)(2,1)S(1)}, bf16[288,1024]{1,0:T(8,128)(2,1)S(1)}, u32[]{:S(2)}, u32[]{:S(2)}) collective-permute-start(bf16[288,1024]{1,0:T(8,128)(2,1)S(1)} %get-tuple-element.126.refs_0_), channel_id=1, source_target_pairs={{0,4},{12,8},{1,5},{13,9},{2,6},{14,10},{3,7},{15,11},{16,20},{28,... | collective-permute-start | bytes 1769480 | tf_op jit(solution)/shard_map/ppermute | solution.py:426
  82.6 4.0 %collective-permute-done.7.refs_1_ = bf16[544,1024]{1,0:T(8,128)(2,1)S(1)} collective-permute-done((bf16[544,1024]{1,0:T(8,128)(2,1)S(1)}, bf16[544,1024]{1,0:T(8,128)(2,1)S(1)}, u32[]{:S(2)}, u32[]{:S(2)}) %collective-permute-start.7) | collective-permute-done | bytes 1114144 | tf_op jit(solution)/shard_map/ppermute | solution.py:426
  86.8 0.7 collective-permute-start.11
  87.5 1.3 %collective-permute-start.12 = (bf16[256,1024]{1,0:T(8,128)(2,1)S(1)}, bf16[256,1024]{1,0:T(8,128)(2,1)S(1)}, u32[]{:S(2)}, u32[]{:S(2)}) collective-permute-start(bf16[256,1024]{1,0:T(8,128)(2,1)S(1)} %slice.15), channel_id=1, source_target_pairs={{8,12},{4,0},{9,13},{5,1},{10,14},{6,2},{11,15},{7,3},{24,28},{20,... | collective-permute-start | bytes 1572872 | tf_op jit(solution)/shard_map/ppermute | solution.py:426
  89.0 1.3 %collective-permute-start.17 = (bf16[256,1024]{1,0:T(8,128)(2,1)S(1)}, bf16[256,1024]{1,0:T(8,128)(2,1)S(1)}, u32[]{:S(2)}, u32[]{:S(2)}) collective-permute-start(bf16[256,1024]{1,0:T(8,128)(2,1)S(1)} %join.10), channel_id=1, source_target_pairs={{8,12},{4,0},{9,13},{5,1},{10,14},{6,2},{11,15},{7,3},{24,28},{20,... | collective-permute-start | bytes 1572872 | tf_op jit(solution)/shard_map/ppermute | solution.py:426
  90.3 1.0 collective-permute-done.9.refs_9_
  91.3 0.7 collective-permute-start.16
  92.0 6.5 %collective-permute-done.10.refs_11_ = bf16[288,1024]{1,0:T(8,128)(2,1)S(1)} collective-permute-done((bf16[288,1024]{1,0:T(8,128)(2,1)S(1)}, bf16[288,1024]{1,0:T(8,128)(2,1)S(1)}, u32[]{:S(2)}, u32[]{:S(2)}) %collective-permute-start.10) | collective-permute-done | bytes 589856 | tf_op jit(solution)/shard_map/ppermute | solution.py:426
  98.5 4.4 %collective-permute-start.15 = (bf16[256,1024]{1,0:T(8,128)(2,1)S(1)}, bf16[256,1024]{1,0:T(8,128)(2,1)S(1)}, u32[]{:S(2)}, u32[]{:S(2)}) collective-permute-start(bf16[256,1024]{1,0:T(8,128)(2,1)S(1)} %get-tuple-element.138.refs_0_), channel_id=1, source_target_pairs={{0,4},{12,8},{1,5},{13,9},{2,6},{14,10},{3,7},{15,11},{16,20},{28,... | collective-permute-start | bytes 1572872 | tf_op jit(solution)/shard_map/ppermute | solution.py:426
  103.0 5.1 %collective-permute-done.12.refs_10_ = bf16[256,1024]{1,0:T(8,128)(2,1)S(1)} collective-permute-done((bf16[256,1024]{1,0:T(8,128)(2,1)S(1)}, bf16[256,1024]{1,0:T(8,128)(2,1)S(1)}, u32[]{:S(2)}, u32[]{:S(2)}) %collective-permute-start.12) | collective-permute-done | bytes 524320 | tf_op jit(solution)/shard_map/ppermute | solution.py:426
  108.3 1.2 %collective-permute-done.13 = bf16[256,128]{1,0:T(8,128)(2,1)S(1)} collective-permute-done((bf16[256,128]{1,0:T(8,128)(2,1)S(1)}, bf16[256,128]{1,0:T(8,128)(2,1)S(1)}, u32[]{:S(2)}, u32[]{:S(2)}) %collective-permute-start.13) | collective-permute-done | bytes 65568 | tf_op jit(solution)/shard_map/ppermute | solution.py:417
  109.6 4.3 %collective-permute-done.14 = bf16[256,128]{1,0:T(8,128)(2,1)S(1)} collective-permute-done((bf16[256,128]{1,0:T(8,128)(2,1)S(1)}, bf16[256,128]{1,0:T(8,128)(2,1)S(1)}, u32[]{:S(2)}, u32[]{:S(2)}) %collective-permute-start.14) | collective-permute-done | bytes 65568 | tf_op jit(solution)/shard_map/ppermute | solution.py:417
  113.9 1.8 %finish.1.total = bf16[256,2048]{1,0:T(8,128)(2,1)S(1)} custom-call(s32[38]{0:T(128)S(1)} %copy-done.3, s32[8,128]{1,0:T(8,128)S(1)} %bitcast.17, bf16[256,128]{1,0:T(8,128)(2,1)S(1)} %add.56.refs_2_, bf16[256,1024]{1,0:T(8,128)(2,1)S(1)} %get-tuple-element.136.refs_3_, bf16[288,1024]{1,0:T(8,128)(2,1)S(1)} %get-tuple-element.131.refs_4_, ...), custom_call_target="tpu_custom_call" | custom-call | flops 1000000 | bytes 100000 | tf_op jit(solution)/shard_map/finish/pallas_call | solution.py:338
  115.7 1.3 %add_last.1 = bf16[256,2048]{1,0:T(8,128)(2,1)} custom-call(bf16[256,2048]{1,0:T(8,128)(2,1)S(1)} %finish.1.total, bf16[256,1024]{1,0:T(8,128)(2,1)S(1)} %collective-permute-done.15.refs_0_, bf16[256,1024]{1,0:T(8,128)(2,1)S(1)} %collective-permute-done.16.refs_1_, bf16[256,1024]{1,0:T(8,128)(2,1)S(1)} %collective-permute-done.17.refs_2_), custom_call_target="tpu_custom_call" | custom-call | flops 1000000 | bytes 100000 | tf_op jit(solution)/shard_map/add_last/pallas_call | solution.py:387
  (35 shorter events, 1.2 us)
Async XLA Ops:
  1.3 11.6 %copy-start.1 = (bf16[4,32,8192]{2,1,0:T(8,128)(2,1)S(1)}, bf16[4,32,8192]{2,1,0:T(8,128)(2,1)}, u32[]{:S(2)}) copy-start(bf16[4,32,8192]{2,1,0:T(8,128)(2,1)} %refs_1_.2) | copy-start | bytes 6291460
  1.3 11.6 %copy-start.3 = (s32[38]{0:T(128)S(1)}, s32[38]{0:T(128)}, u32[]{:S(2)}) copy-start(s32[38]{0:T(128)} %concatenate.3.refs_0_) | copy-start | bytes 460
  12.9 1.1 copy-start
  13.7 5.2 %collective-permute-start = (bf16[2,256,1024]{2,1,0:T(8,128)(2,1)S(1)}, bf16[2,256,1024]{2,1,0:T(8,128)(2,1)}, u32[]{:S(2)}, u32[]{:S(2)}) collective-permute-start(bf16[2,256,1024]{2,1,0:T(8,128)(2,1)S(1)} %get-tuple-element.74), channel_id=1, source_target_pairs={{0,1},{1,0},{2,3},{3,2},{4,5},{5,4},{6,7},{7,6},{8,9},{9,8},{10,11... | collective-permute-start | bytes 3145736 | tf_op jit(solution)/shard_map/ppermute | solution.py:417
  13.9 20.6 %collective-permute-start.1 = (bf16[288,1024]{1,0:T(8,128)(2,1)S(1)}, bf16[288,1024]{1,0:T(8,128)(2,1)S(1)}, u32[]{:S(2)}, u32[]{:S(2)}) collective-permute-start(bf16[288,1024]{1,0:T(8,128)(2,1)S(1)} %copy-done), channel_id=1, source_target_pairs={{0,4},{12,8},{1,5},{13,9},{2,6},{14,10},{3,7},{15,11},{16,20},{28,... | collective-permute-start | bytes 1769480 | tf_op jit(solution)/shard_map/ppermute | solution.py:426
  20.2 15.1 %collective-permute-start.2 = (bf16[256,1024]{1,0:T(8,128)(2,1)S(1)}, bf16[256,1024]{1,0:T(8,128)(2,1)S(1)}, u32[]{:S(2)}, u32[]{:S(2)}) collective-permute-start(bf16[256,1024]{1,0:T(8,128)(2,1)S(1)} %get-tuple-element.140), channel_id=1, source_target_pairs={{0,2},{1,3},{2,0},{3,1},{4,6},{5,7},{6,4},{7,5},{8,10},{9,11},{10,... | collective-permute-start | bytes 1572872 | tf_op jit(solution)/shard_map/ppermute | solution.py:417
  31.9 28.5 %collective-permute-start.3 = (bf16[256,1024]{1,0:T(8,128)(2,1)S(1)}, bf16[256,1024]{1,0:T(8,128)(2,1)S(1)}, u32[]{:S(2)}, u32[]{:S(2)}) collective-permute-start(bf16[256,1024]{1,0:T(8,128)(2,1)S(1)} %get-tuple-element.96.refs_0_), channel_id=1, source_target_pairs={{0,4},{12,8},{1,5},{13,9},{2,6},{14,10},{3,7},{15,11},{16,20},{28,... | collective-permute-start | bytes 1572872 | tf_op jit(solution)/shard_map/ppermute | solution.py:426
  34.7 7.2 %copy-start.2 = (s32[1024]{0:T(1024)S(1)}, s32[1024]{0:T(1024)}, u32[]{:S(2)}) copy-start(s32[1024]{0:T(1024)} %param.12) | copy-start | bytes 12292
  34.7 28.1 %collective-permute-start.5 = (bf16[288,1024]{1,0:T(8,128)(2,1)S(1)}, bf16[288,1024]{1,0:T(8,128)(2,1)S(1)}, u32[]{:S(2)}, u32[]{:S(2)}) collective-permute-start(bf16[288,1024]{1,0:T(8,128)(2,1)S(1)} %join.6), channel_id=1, source_target_pairs={{4,8},{8,4},{5,9},{9,5},{6,10},{10,6},{7,11},{11,7},{20,24},{24,20... | collective-permute-start | bytes 1769480 | tf_op jit(solution)/shard_map/ppermute | solution.py:426
  35.6 27.2 %collective-permute-start.6 = (bf16[256,1024]{1,0:T(8,128)(2,1)S(1)}, bf16[256,1024]{1,0:T(8,128)(2,1)S(1)}, u32[]{:S(2)}, u32[]{:S(2)}) collective-permute-start(bf16[256,1024]{1,0:T(8,128)(2,1)S(1)} %add.51.refs_5_), channel_id=1, source_target_pairs={{4,8},{8,4},{5,9},{9,5},{6,10},{10,6},{7,11},{11,7},{20,24},{24,20... | collective-permute-start | bytes 1572872 | tf_op jit(solution)/shard_map/ppermute | solution.py:426
  36.3 25.6 %collective-permute-start.4 = (bf16[256,1024]{1,0:T(8,128)(2,1)S(1)}, bf16[256,1024]{1,0:T(8,128)(2,1)S(1)}, u32[]{:S(2)}, u32[]{:S(2)}) collective-permute-start(bf16[256,1024]{1,0:T(8,128)(2,1)S(1)} %add.51.refs_5_), channel_id=1, source_target_pairs={{0,4},{12,8},{4,0},{8,12},{1,5},{13,9},{5,1},{9,13},{2,6},{14,10},... | collective-permute-start | bytes 1572872 | tf_op jit(solution)/shard_map/ppermute | solution.py:469
  60.4 26.2 %collective-permute-start.7 = (bf16[544,1024]{1,0:T(8,128)(2,1)S(1)}, bf16[544,1024]{1,0:T(8,128)(2,1)S(1)}, u32[]{:S(2)}, u32[]{:S(2)}) collective-permute-start(bf16[544,1024]{1,0:T(8,128)(2,1)S(1)} %get-tuple-element.123.refs_0_), channel_id=1, source_target_pairs={{0,4},{12,8},{1,5},{13,9},{2,6},{14,10},{3,7},{15,11},{16,20},{28,... | collective-permute-start | bytes 3342344 | tf_op jit(solution)/shard_map/ppermute | solution.py:426
  62.0 25.5 %collective-permute-start.8 = (bf16[512,1024]{1,0:T(8,128)(2,1)S(1)}, bf16[512,1024]{1,0:T(8,128)(2,1)S(1)}, u32[]{:S(2)}, u32[]{:S(2)}) collective-permute-start(bf16[512,1024]{1,0:T(8,128)(2,1)S(1)} %under_each_other.1), channel_id=1, source_target_pairs={{4,8},{8,4},{5,9},{9,5},{6,10},{10,6},{7,11},{11,7},{20,24},{24,20... | collective-permute-start | bytes 3145736 | tf_op jit(solution)/shard_map/ppermute | solution.py:426
  62.9 28.3 %collective-permute-start.9 = (bf16[544,1024]{1,0:T(8,128)(2,1)S(1)}, bf16[544,1024]{1,0:T(8,128)(2,1)S(1)}, u32[]{:S(2)}, u32[]{:S(2)}) collective-permute-start(bf16[544,1024]{1,0:T(8,128)(2,1)S(1)} %join.8), channel_id=1, source_target_pairs={{8,12},{4,0},{9,13},{5,1},{10,14},{6,2},{11,15},{7,3},{24,28},{20,... | collective-permute-start | bytes 3342344 | tf_op jit(solution)/shard_map/ppermute | solution.py:426
  76.3 22.2 %collective-permute-start.10 = (bf16[288,1024]{1,0:T(8,128)(2,1)S(1)}, bf16[288,1024]{1,0:T(8,128)(2,1)S(1)}, u32[]{:S(2)}, u32[]{:S(2)}) collective-permute-start(bf16[288,1024]{1,0:T(8,128)(2,1)S(1)} %get-tuple-element.126.refs_0_), channel_id=1, source_target_pairs={{0,4},{12,8},{1,5},{13,9},{2,6},{14,10},{3,7},{15,11},{16,20},{28,... | collective-permute-start | bytes 1769480 | tf_op jit(solution)/shard_map/ppermute | solution.py:426
  86.8 16.2 %collective-permute-start.11 = (bf16[288,1024]{1,0:T(8,128)(2,1)S(1)}, bf16[288,1024]{1,0:T(8,128)(2,1)S(1)}, u32[]{:S(2)}, u32[]{:S(2)}) collective-permute-start(bf16[288,1024]{1,0:T(8,128)(2,1)S(1)} %join.9), channel_id=1, source_target_pairs={{4,8},{8,4},{5,9},{9,5},{6,10},{10,6},{7,11},{11,7},{20,24},{24,20... | collective-permute-start | bytes 1769480 | tf_op jit(solution)/shard_map/ppermute | solution.py:426
  87.5 20.6 %collective-permute-start.12 = (bf16[256,1024]{1,0:T(8,128)(2,1)S(1)}, bf16[256,1024]{1,0:T(8,128)(2,1)S(1)}, u32[]{:S(2)}, u32[]{:S(2)}) collective-permute-start(bf16[256,1024]{1,0:T(8,128)(2,1)S(1)} %slice.15), channel_id=1, source_target_pairs={{8,12},{4,0},{9,13},{5,1},{10,14},{6,2},{11,15},{7,3},{24,28},{20,... | collective-permute-start | bytes 1572872 | tf_op jit(solution)/shard_map/ppermute | solution.py:426
  89.0 26.7 %collective-permute-start.17 = (bf16[256,1024]{1,0:T(8,128)(2,1)S(1)}, bf16[256,1024]{1,0:T(8,128)(2,1)S(1)}, u32[]{:S(2)}, u32[]{:S(2)}) collective-permute-start(bf16[256,1024]{1,0:T(8,128)(2,1)S(1)} %join.10), channel_id=1, source_target_pairs={{8,12},{4,0},{9,13},{5,1},{10,14},{6,2},{11,15},{7,3},{24,28},{20,... | collective-permute-start | bytes 1572872 | tf_op jit(solution)/shard_map/ppermute | solution.py:426
  91.3 24.3 %collective-permute-start.16 = (bf16[256,1024]{1,0:T(8,128)(2,1)S(1)}, bf16[256,1024]{1,0:T(8,128)(2,1)S(1)}, u32[]{:S(2)}, u32[]{:S(2)}) collective-permute-start(bf16[256,1024]{1,0:T(8,128)(2,1)S(1)} %join.11), channel_id=1, source_target_pairs={{4,8},{8,4},{5,9},{9,5},{6,10},{10,6},{7,11},{11,7},{20,24},{24,20... | collective-permute-start | bytes 1572872 | tf_op jit(solution)/shard_map/ppermute | solution.py:426
  98.5 17.2 %collective-permute-start.15 = (bf16[256,1024]{1,0:T(8,128)(2,1)S(1)}, bf16[256,1024]{1,0:T(8,128)(2,1)S(1)}, u32[]{:S(2)}, u32[]{:S(2)}) collective-permute-start(bf16[256,1024]{1,0:T(8,128)(2,1)S(1)} %get-tuple-element.138.refs_0_), channel_id=1, source_target_pairs={{0,4},{12,8},{1,5},{13,9},{2,6},{14,10},{3,7},{15,11},{16,20},{28,... | collective-permute-start | bytes 1572872 | tf_op jit(solution)/shard_map/ppermute | solution.py:426
  108.2 1.3 %collective-permute-start.13 = (bf16[256,128]{1,0:T(8,128)(2,1)S(1)}, bf16[256,128]{1,0:T(8,128)(2,1)S(1)}, u32[]{:S(2)}, u32[]{:S(2)}) collective-permute-start(bf16[256,128]{1,0:T(8,128)(2,1)S(1)} %bitcast.18), channel_id=1, source_target_pairs={{0,1},{1,0},{2,3},{3,2},{4,5},{5,4},{6,7},{7,6},{8,9},{9,8},{10,11... | collective-permute-start | bytes 196616 | tf_op jit(solution)/shard_map/ppermute | solution.py:417
  109.5 4.3 %collective-permute-start.14 = (bf16[256,128]{1,0:T(8,128)(2,1)S(1)}, bf16[256,128]{1,0:T(8,128)(2,1)S(1)}, u32[]{:S(2)}, u32[]{:S(2)}) collective-permute-start(bf16[256,128]{1,0:T(8,128)(2,1)S(1)} %bitcast_add_fusion), channel_id=1, source_target_pairs={{0,2},{1,3},{2,0},{3,1},{4,6},{5,7},{6,4},{7,5},{8,10},{9,11},{10,... | collective-permute-start | bytes 196616 | tf_op jit(solution)/shard_map/ppermute | solution.py:417
